TPU v7x, 128 devices: a whole 4x4x4 slice. The times are simulated.
128 devices in a mesh: gx: 8 (over y_lo, z), gy: 16 (over y_hi, x, core).
Axes of the slice: x: 4, y: 4 (y_hi: 2, y_lo: 2; y = y_hi * 2 + y_lo), z: 4, core: 2. Of those that a mesh axis runs over, the one named last changes fastest.
Arguments:
- state: float32 [4, 256, 512, 128], P(None, 'gx', 'gy'), may hold values from 0 to 1
- velocity: float32 [3, 256, 512, 128], P(None, 'gx', 'gy'), may hold values from -1 to 1
- routes: int32 [16, 32, 8], P('gx', 'gy'), may hold values from -1 to 223, as said below
- w_in: bfloat16 [128, 7], replicated, may hold values from -2 to 2
- w_mid: bfloat16 [128, 128], replicated, may hold values from -0.5 to 0.5
- w_deep: bfloat16 [128, 128], replicated, may hold values from -0.5 to 0.5
- w_out: bfloat16 [4, 128], replicated, may hold values from -1.5 to 1.5
Outputs:
- evolved: float32 [4, 256, 512, 128], P(None, 'gx', 'gy')
Inputs may be any that keep to these rules, and one draw needn't show every extreme that they name: `routes`: -1 for a block outside the interface band; for a band block d * 14 + s, where d is the gy index of the device with the same gx index that evaluates its closure and s its place there. Each device receives exactly 14 band blocks from the devices of its gy group, in distinct places, and at most 2 from any one device.
All inputs are finite; a program needn't handle non-finite values.
Results may differ from a plain program's by a relative error of at most 0.0008.
Values may be sent and summed in bfloat16 or wider, within the bound.
No kernel may reach another device: no remote copies, remote signals or barrier semaphores. Data moves between devices by JAX's collectives and lax.ppermute only.
A program may use at most 128 MiB of HBM per device.

v0:
```python
import jax
import jax.numpy as jnp
from jax import lax
from jax.sharding import PartitionSpec as P

BS = 16
SLOTS = 14


EPS = 1e-06
STEP = 0.25


def padded_2(cells, sides, width):
    for axis, dim in sides:
        count = lax.axis_size(axis)
        head = lax.slice_in_dim(cells, 0, width, axis=dim)
        tail = lax.slice_in_dim(cells, cells.shape[dim] - width, cells.shape[dim], axis=dim)
        cells = jnp.concatenate(
            [
                lax.ppermute(tail, axis, [(i, (i + 1) % count) for i in range(count)]),
                cells,
                lax.ppermute(head, axis, [((i + 1) % count, i) for i in range(count)]),
            ],
            axis=dim,
        )
    return cells


def weno_face(far_left, near_left, centre, near_right, far_right):
    smooth_zero = (
        13.0 / 12.0 * (far_left - 2.0 * near_left + centre) ** 2
        + 0.25 * (far_left - 4.0 * near_left + 3.0 * centre) ** 2
    )
    smooth_one = (
        13.0 / 12.0 * (near_left - 2.0 * centre + near_right) ** 2
        + 0.25 * (near_left - near_right) ** 2
    )
    smooth_two = (
        13.0 / 12.0 * (centre - 2.0 * near_right + far_right) ** 2
        + 0.25 * (3.0 * centre - 4.0 * near_right + far_right) ** 2
    )
    weight_zero = 0.1 / (EPS + smooth_zero) ** 2
    weight_one = 0.6 / (EPS + smooth_one) ** 2
    weight_two = 0.3 / (EPS + smooth_two) ** 2
    guess_zero = (2.0 * far_left - 7.0 * near_left + 11.0 * centre) / 6.0
    guess_one = (-near_left + 5.0 * centre + 2.0 * near_right) / 6.0
    guess_two = (2.0 * centre + 5.0 * near_right - far_right) / 6.0
    return (weight_zero * guess_zero + weight_one * guess_one + weight_two * guess_two) / (
        weight_zero + weight_one + weight_two
    )


def flux_difference(extended, speed_ext, axis, length):
    faces = length + 1

    def window(array, start, count):
        return lax.slice_in_dim(array, start, start + count, axis=axis)

    flux = speed_ext * extended
    magnitude = jnp.abs(speed_ext)
    face_speed = jnp.maximum(window(magnitude, 2, faces), window(magnitude, 3, faces))

    def upper(offset):
        return 0.5 * (window(flux, offset, faces) + face_speed * window(extended, offset, faces))

    def lower(offset):
        return 0.5 * (window(flux, offset, faces) - face_speed * window(extended, offset, faces))

    face_flux = weno_face(upper(0), upper(1), upper(2), upper(3), upper(4)) + weno_face(
        lower(5), lower(4), lower(3), lower(2), lower(1)
    )
    return window(face_flux, 1, length) - window(face_flux, 0, length)


def wrap_depth(field, axis):
    length = field.shape[axis]
    return jnp.concatenate(
        [
            lax.slice_in_dim(field, length - 3, length, axis=axis),
            field,
            lax.slice_in_dim(field, 0, 3, axis=axis),
        ],
        axis=axis,
    )


def to_blocks(field):
    channels, size_x, size_y, size_z = field.shape
    shaped = field.reshape(channels, size_x // BS, BS, size_y // BS, BS, size_z // BS, BS)
    shaped = shaped.transpose(1, 3, 5, 0, 2, 4, 6)
    return shaped.reshape(-1, channels, BS**3)


def from_blocks(blocks, size_x, size_y, size_z):
    channels = blocks.shape[1]
    shaped = blocks.reshape(size_x // BS, size_y // BS, size_z // BS, channels, BS, BS, BS)
    shaped = shaped.transpose(3, 0, 4, 1, 5, 2, 6)
    return shaped.reshape(channels, size_x, size_y, size_z)


def closure_batch(features, weights):
    w_in, w_mid, w_deep, w_out = weights

    def apply_pair(paired):
        hidden = jnp.einsum("hf,bfc->bhc", w_in, paired, preferred_element_type=jnp.float32)
        hidden = jax.nn.silu(hidden).astype(jnp.bfloat16)
        hidden = jnp.einsum("hg,bgc->bhc", w_mid, hidden, preferred_element_type=jnp.float32)
        hidden = jax.nn.silu(hidden).astype(jnp.bfloat16)
        hidden = jnp.einsum("hg,bgc->bhc", w_deep, hidden, preferred_element_type=jnp.float32)
        hidden = jax.nn.silu(hidden).astype(jnp.bfloat16)
        return jnp.einsum("vh,bhc->bvc", w_out, hidden, preferred_element_type=jnp.float32)

    count = features.shape[0]
    grouped = features.reshape(count // 2, 2, features.shape[1], features.shape[2])
    result = lax.map(apply_pair, grouped)
    return result.reshape(count, result.shape[2], result.shape[3])


def transport(state, velocity, vel_rim):
    padded = padded_2(state.astype(jnp.bfloat16), (("gx", 1), ("gy", 2)), 3).astype(state.dtype)
    along_x = padded[:, :, 3:-3, :]
    along_y = padded[:, 3:-3, :, :]
    total = flux_difference(along_x, vel_rim[0:1, :, 3:-3, :], 1, state.shape[1])
    total = total + flux_difference(along_y, vel_rim[1:2, 3:-3, :, :], 2, state.shape[2])
    total = total + flux_difference(
        wrap_depth(state, 3), wrap_depth(velocity[2:3], 3), 3, state.shape[3]
    )
    return -total


def sources(state, velocity, routes, weights):
    features = jnp.concatenate([to_blocks(state), to_blocks(velocity)], axis=1).astype(jnp.bfloat16)
    codes = routes.reshape(-1)
    in_band = codes >= 0
    group_size = lax.axis_size("gy")
    block_count = codes.shape[0]
    per_pair = -(-block_count // group_size)
    target = codes // SLOTS
    place = codes % SLOTS
    index_range = jnp.arange(block_count)
    earlier = (
        (index_range[None, :] < index_range[:, None])
        & (target[None, :] == target[:, None])
        & in_band[None, :]
    )
    rank_within = jnp.sum(earlier.astype(jnp.int32), axis=1)
    column = target * per_pair + rank_within
    lanes = jnp.arange(group_size * per_pair)
    packing = (column[:, None] == lanes[None, :]) & in_band[:, None]
    outgoing = jnp.einsum(
        "km,kfc->mfc", packing.astype(jnp.bfloat16), features, preferred_element_type=jnp.float32
    ).astype(jnp.bfloat16)
    labels = jnp.sum(jnp.where(packing, place[:, None] + 1, 0), axis=0) - 1
    outgoing = outgoing.reshape(group_size, per_pair, features.shape[1], features.shape[2])
    labels = labels.reshape(group_size, per_pair)
    arrived, arrived_labels = (
        lax.all_to_all(outgoing, "gy", split_axis=0, concat_axis=0, tiled=True),
        lax.all_to_all(labels, "gy", split_axis=0, concat_axis=0, tiled=True),
    )
    arrived = arrived.reshape(group_size * per_pair, features.shape[1], features.shape[2])
    compact = arrived_labels.reshape(-1)[:, None] == jnp.arange(SLOTS)[None, :]
    work = jnp.einsum(
        "is,ifc->sfc", compact.astype(jnp.bfloat16), arrived, preferred_element_type=jnp.float32
    ).astype(jnp.bfloat16)
    evaluated = closure_batch(work, weights)
    answered = jnp.einsum(
        "is,svc->ivc", compact.astype(jnp.float32), evaluated, precision=lax.Precision.HIGHEST
    )
    answered = answered.reshape(group_size, per_pair, evaluated.shape[1], evaluated.shape[2])
    returned = lax.all_to_all(
        answered.astype(jnp.bfloat16), "gy", split_axis=0, concat_axis=0, tiled=True
    ).astype(answered.dtype)
    returned = returned.reshape(group_size * per_pair, evaluated.shape[1], evaluated.shape[2])
    result = jnp.einsum(
        "km,mvc->kvc", packing.astype(jnp.float32), returned, precision=lax.Precision.HIGHEST
    )
    return from_blocks(result, state.shape[1], state.shape[2], state.shape[3])


def shards(state, velocity, routes, w_in, w_mid, w_deep, w_out):
    weights = (w_in, w_mid, w_deep, w_out)
    vel_rim = padded_2(velocity.astype(jnp.bfloat16), (("gx", 1), ("gy", 2)), 3).astype(
        velocity.dtype
    )

    def rate(field):
        return transport(field, velocity, vel_rim) + sources(field, velocity, routes, weights)

    first = state + STEP * rate(state)
    return 0.75 * state + 0.25 * (first + STEP * rate(first))


def solution(mesh):
    placed = (
        P(None, "gx", "gy", None),
        P(None, "gx", "gy", None),
        P("gx", "gy", None),
        P(),
        P(),
        P(),
        P(),
    )
    return jax.shard_map(
        shards, mesh=mesh, in_specs=placed, out_specs=P(None, "gx", "gy", None), check_vma=False
    )
```

profile of v0, /device:TPU:0, one launch (start us, length us, event | category | flops | bytes accessed | tf_op | source)
XLA Modules:
  0.0 602.0 jit_solution(8816136071755681804)
XLA Ops:
  3.4 7.2 %all-to-all-start = ((s32[16,1,2]{2,1,0:T(1,128)}), s32[16,1,2]{2,1,0:T(1,128)}, u32[]{:S(2)}, u32[]{:S(2)}) async-start(s32[16,1,2]{2,1,0:T(1,128)} %bitcast.29), calls=%async_computation | async-start | bytes 16384 | tf_op jit(solution)/shard_map/all_to_all | solution.py:159
  13.2 4.2 collective-permute-start.5
  18.2 4.1 collective-permute-start.1
  22.5 5.7 reshape.311
  28.2 9.7 %reshape.292 = bf16[4,2,16,2,16,8,16]{6,5,4,3,2,1,0:T(8,128)(2,1)} reshape(bf16[4,32,32,128]{3,2,1,0:T(8,128)(2,1)} %copy-done.6) | data formatting | bytes 2097152 | tf_op jit(solution)/shard_map/reshape | solution.py:90
  42.5 7.2 %copy.97 = bf16[3,2,16,2,16,8,16]{6,4,2,5,3,1,0:T(8,128)(2,1)} copy(bf16[3,2,16,2,16,8,16]{6,5,4,3,2,1,0:T(8,128)(2,1)} %reshape.311) | data formatting | bytes 1572864 | tf_op jit(solution)/shard_map/convert.6
  49.7 12.3 %reshape.310 = bf16[32,3,4096]{2,0,1:T(8,128)(2,1)} reshape(bf16[2,2,8,3,16,16,16]{6,5,4,2,1,0,3:T(8,128)(2,1)} %bitcast.234) | data formatting | bytes 1572864 | tf_op jit(solution)/shard_map/convert.6
  62.0 9.1 %copy.96 = bf16[4,2,16,2,16,8,16]{6,4,2,5,3,1,0:T(8,128)(2,1)} copy(bf16[4,2,16,2,16,8,16]{6,5,4,3,2,1,0:T(8,128)(2,1)} %reshape.292) | data formatting | bytes 2097152 | tf_op jit(solution)/shard_map/reshape | solution.py:90
  71.2 15.9 %reshape.293 = bf16[32,4,4096]{2,0,1:T(8,128)(2,1)} reshape(bf16[2,2,8,4,16,16,16]{6,5,4,2,1,0,3:T(8,128)(2,1)} %bitcast.232) | data formatting | bytes 2097152 | tf_op jit(solution)/shard_map/reshape | solution.py:92
  94.3 25.7 %divide_add_fusion.1 = f32[4,32,32,129]{3,2,1,0:T(8,128)} fusion(f32[4,32,32,3]{3,2,1,0:T(8,128)S(1)} %copy-done.5, f32[4,32,32,128]{3,2,1,0:T(8,128)S(1)} %copy-done, f32[4,32,32,134]{3,2,1,0:T(8,128)S(1)} %maximum_multiply_fusion, f32[4,32,32,3]{3,2,1,0:T(8,128)S(1)} %copy-done.4, f32[32,32,129]{2,1,0:T(8,128)S(1)} %fusion.96), kind=kLoop, calls=%fused_computation.98 | loop fusion | flops 80842752 | bytes 17518592 | tf_op jit(solution)/shard_map/add | solution.py:70
  120.0 3.9 reshape.296
  127.1 7.9 %all-to-all-start.1 = ((bf16[16,2,7,4096]{3,1,2,0:T(2,128)(2,1)}), bf16[16,2,7,4096]{3,1,2,0:T(2,128)(2,1)}, u32[]{:S(2)}, u32[]{:S(2)}) async-start(bf16[16,2,7,4096]{3,1,2,0:T(2,128)(2,1)} %copy.61), calls=%async_computation.1 | async-start | bytes 3670016 | tf_op jit(solution)/shard_map/all_to_all | solution.py:158
  138.3 5.3 collective-permute-start.3
  144.6 5.4 collective-permute-start.7
  150.0 7.7 %collective-permute-done.3 = bf16[3,38,3,128]{3,2,1,0:T(4,128)(2,1)S(1)} collective-permute-done((bf16[3,38,3,128]{3,2,1,0:T(4,128)(2,1)S(1)}, bf16[3,38,3,128]{3,2,1,0:T(4,128)(2,1)S(1)}, u32[]{:S(2)}, u32[]{:S(2)}) %collective-permute-start.3) | collective-permute-done | bytes 87584 | tf_op jit(solution)/shard_map/ppermute | solution.py:23
  157.7 5.0 collective-permute-done.2
  166.7 16.1 %divide_add_fusion.3 = f32[4,32,33,128]{3,2,1,0:T(8,128)} fusion(f32[4,38,38,128]{3,2,1,0:T(8,128)S(1)} %maximum_convert_fusion, f32[4,32,38,128]{3,2,1,0:T(8,128)S(1)} %slice_multiply_fusion.13, f32[32,33,128]{2,1,0:T(8,128)S(1)} %fusion.101), kind=kLoop, calls=%fused_computation.130 | loop fusion | flops 79478784 | bytes 28655616 | tf_op jit(solution)/shard_map/add | solution.py:70
  184.7 5.0 copy.62
  189.7 5.0 reshape.297
  199.3 57.9 %while.20 = (s32[]{:T(128)}, f32[7,2,4,4096]{3,2,1,0:T(4,128)}, bf16[7,2,7,4096]{3,2,1,0:T(8,128)(2,1)}, bf16[128,7]{0,1:T(8,128)(2,1)S(1)}, bf16[128,128]{1,0:T...) while((s32[]{:T(128)}, f32[7,2,4,4096]{3,2,1,0:T(4,128)}, ...), condition=%wide.region_3.4_spmd, body=%wide.region_2.3_spmd.sunk | while | flops 575668224 | bytes 4524901 | solution.py:116
  199.4 4.6 multiply_convert_fusion.8
  207.6 4.6 multiply_convert_fusion.8
  212.3 3.6 fusion.172
  215.9 4.6 multiply_convert_fusion.8
  224.2 4.6 multiply_convert_fusion.8
  228.8 3.6 fusion.172
  232.5 4.6 multiply_convert_fusion.8
  240.7 4.6 multiply_convert_fusion.8
  249.0 4.6 multiply_convert_fusion.8
  261.6 4.5 all-to-all-start.2
  266.2 14.9 %divide_add_fusion.5 = f32[4,33,32,128]{3,2,1,0:T(8,128)} fusion(f32[4,38,38,128]{3,2,1,0:T(8,128)S(1)} %maximum_convert_fusion, f32[4,38,32,128]{3,2,1,0:T(8,128)} %slice_multiply_fusion.15, f32[33,32,128]{2,1,0:T(8,128)} %fusion.102), kind=kLoop, calls=%fused_computation.162 | loop fusion | flops 79478784 | bytes 28655616 | tf_op jit(solution)/shard_map/add | solution.py:70
  284.2 4.7 copy.66
  288.9 13.8 %convolution_bitcast_fusion.9 = f32[4,2,16,2,16,8,16]{6,5,4,2,0,3,1:T(8,128)S(1)} fusion(bf16[4,16,16,16,32,1,1]{4,3,2,1,0,6,5:T(8,128)(2,1)} %bitcast.236, s32[2,2,8]{2,1,0:T(2,128)S(1)} %fusion.134, pred[2,2,8]{2,1,0:T(4,128)(4,1)S(1)} %copy-done.29), kind=kOutput, calls=%fused_computation.37 | convolution fusion | flops 33556480 | bytes 3145888 | tf_op jit(solution)/shard_map/km,mvc->kvc/dot_general | solution.py:175
  302.7 6.3 %copy.67 = f32[4,2,16,2,16,8,16]{6,5,4,3,2,1,0:T(8,128)} copy(f32[4,2,16,2,16,8,16]{6,5,4,2,0,3,1:T(8,128)S(1)} %convolution_bitcast_fusion.9) | data formatting | bytes 4194304 | tf_op jit(solution)/shard_map/transpose | solution.py:98
  309.0 11.6 %reshape.301 = f32[4,32,32,128]{3,2,1,0:T(8,128)} reshape(f32[4,2,16,2,16,8,16]{6,5,4,3,2,1,0:T(8,128)} %copy.67) | data formatting | bytes 4194304 | tf_op jit(solution)/shard_map/reshape | solution.py:99
  320.6 9.5 %fusion.138 = (bf16[4,32,32,128]{3,2,1,0:T(8,128)(2,1)S(1)}, f32[4,32,32,128]{3,2,1,0:T(8,128)}) fusion(f32[4,32,32,128]{3,2,1,0:T(8,128)S(1)} %copy-done.1, f32[4,32,32,128]{3,2,1,0:T(8,128)} %reshape.301, f32[4,32,32,129]{3,2,1,0:T(8,128)} %divide_add_fusion.1, f32[4,32,33,128]{3,2,1,0:T(8,128)} %divide_add_fusion.3, f32[4,33,32,128]{3,2,1,0:T(8,128)} %divide_add_fusion.5), kind=kLoop, calls=%fused_computation.267 | loop fusion | flops 5242880 | bytes 19922944 | tf_op jit(solution)/shard_map/convert_element_type | solution.py:121
  330.1 7.8 %reshape.302 = bf16[4,2,16,2,16,8,16]{6,5,4,3,2,1,0:T(8,128)(2,1)} reshape(bf16[4,32,32,128]{3,2,1,0:T(8,128)(2,1)S(1)} %get-tuple-element.165) | data formatting | bytes 2097152 | tf_op jit(solution)/shard_map/reshape | solution.py:90
  337.9 9.1 %copy.95 = bf16[4,2,16,2,16,8,16]{6,4,2,5,3,1,0:T(8,128)(2,1)} copy(bf16[4,2,16,2,16,8,16]{6,5,4,3,2,1,0:T(8,128)(2,1)} %reshape.302) | data formatting | bytes 2097152 | tf_op jit(solution)/shard_map/reshape | solution.py:90
  347.0 15.2 %reshape.303 = bf16[32,4,4096]{2,0,1:T(8,128)(2,1)S(1)} reshape(bf16[2,2,8,4,16,16,16]{6,5,4,2,1,0,3:T(8,128)(2,1)} %bitcast.233) | data formatting | bytes 2097152 | tf_op jit(solution)/shard_map/reshape | solution.py:92
  364.1 3.9 reshape.304
  371.2 4.5 all-to-all-start.3
  381.8 14.7 %collective-permute-done.9 = bf16[4,3,32,128]{3,2,1,0:T(8,128)(2,1)S(1)} collective-permute-done((bf16[4,3,32,128]{3,2,1,0:T(8,128)(2,1)S(1)}, bf16[4,3,32,128]{3,2,1,0:T(8,128)(2,1)S(1)}, u32[]{:S(2)}, u32[]{:S(2)}) %collective-permute-start.9) | collective-permute-done | bytes 98336 | tf_op jit(solution)/shard_map/ppermute | solution.py:23
  396.5 4.1 collective-permute-done.8
  400.7 7.0 %collective-permute-start.11 = (bf16[4,38,3,128]{3,2,1,0:T(4,128)(2,1)S(1)}, bf16[4,38,3,128]{3,2,1,0:T(4,128)(2,1)S(1)}, u32[]{:S(2)}, u32[]{:S(2)}) collective-permute-start(bf16[4,38,3,128]{3,2,1,0:T(4,128)(2,1)S(1)} %get-tuple-element.180), channel_id=1, source_target_pairs={{1,0},{2,1},{3,2},{4,3},{5,4},{6,5},{7,6},{8,7},{9,8},{10,9},{11,1... | collective-permute-start | bytes 350216 | tf_op jit(solution)/shard_map/ppermute | solution.py:23
  407.7 25.7 %divide_add_fusion = f32[4,32,32,129]{3,2,1,0:T(8,128)} fusion(f32[4,32,32,3]{3,2,1,0:T(8,128)S(1)} %get-tuple-element.172, f32[4,32,32,128]{3,2,1,0:T(8,128)S(1)} %copy-done.3, f32[4,32,32,134]{3,2,1,0:T(8,128)S(1)} %maximum_multiply_fusion.1, f32[4,32,32,3]{3,2,1,0:T(8,128)S(1)} %get-tuple-element.171, f32[32,32,129]{2,1,0:T(8,128)S(1)} %copy-done.12), kind=kLoop, calls=%fused_computation.91 | loop fusion | flops 80842752 | bytes 17518592 | tf_op jit(solution)/shard_map/add | solution.py:70
  435.6 15.7 %divide_add_fusion.2 = f32[4,32,33,128]{3,2,1,0:T(8,128)} fusion(f32[4,38,38,128]{3,2,1,0:T(8,128)S(1)} %maximum_convert_fusion.1, f32[4,32,38,128]{3,2,1,0:T(8,128)S(1)} %slice_multiply_fusion.6, f32[32,33,128]{2,1,0:T(8,128)S(1)} %copy-done.22), kind=kLoop, calls=%fused_computation.123 | loop fusion | flops 79478784 | bytes 28655616 | tf_op jit(solution)/shard_map/add | solution.py:70
  453.1 5.0 copy.70
  458.2 5.0 reshape.305
  467.6 58.0 %while.21 = (s32[]{:T(128)}, f32[7,2,4,4096]{3,2,1,0:T(4,128)}, bf16[7,2,7,4096]{3,2,1,0:T(8,128)(2,1)}, bf16[128,7]{0,1:T(8,128)(2,1)S(1)}, bf16[128,128]{1,0:T...) while((s32[]{:T(128)}, f32[7,2,4,4096]{3,2,1,0:T(4,128)}, ...), condition=%wide.region_5.6_spmd, body=%wide.region_4.5_spmd.sunk | while | flops 575668224 | bytes 4524901 | solution.py:116
  467.6 4.6 multiply_convert_fusion.9
  475.9 4.6 multiply_convert_fusion.9
  484.1 4.6 multiply_convert_fusion.9
  492.4 4.6 multiply_convert_fusion.9
  497.0 3.6 fusion.179
  500.7 4.6 multiply_convert_fusion.9
  509.0 4.6 multiply_convert_fusion.9
  517.2 4.6 multiply_convert_fusion.9
  529.9 7.0 %all-to-all-start.4 = ((bf16[16,2,4,4096]{3,2,1,0:T(4,128)(2,1)}), bf16[16,2,4,4096]{3,2,1,0:T(4,128)(2,1)}, u32[]{:S(2)}, u32[]{:S(2)}) async-start(bf16[16,2,4,4096]{3,2,1,0:T(4,128)(2,1)} %copy.73), calls=%async_computation.4 | async-start | bytes 2097152 | tf_op jit(solution)/shard_map/all_to_all | solution.py:171
  536.9 14.9 %divide_add_fusion.4 = f32[4,33,32,128]{3,2,1,0:T(8,128)} fusion(f32[4,38,38,128]{3,2,1,0:T(8,128)S(1)} %maximum_convert_fusion.1, f32[4,38,32,128]{3,2,1,0:T(8,128)} %slice_multiply_fusion.14, f32[33,32,128]{2,1,0:T(8,128)} %fusion.102), kind=kLoop, calls=%fused_computation.155 | loop fusion | flops 79478784 | bytes 28655616 | tf_op jit(solution)/shard_map/add | solution.py:70
  555.0 4.7 copy.74
  559.7 13.8 %convolution_bitcast_fusion.8 = f32[4,2,16,2,16,8,16]{6,5,4,2,0,3,1:T(8,128)S(1)} fusion(bf16[4,16,16,16,32,1,1]{4,3,2,1,0,6,5:T(8,128)(2,1)} %bitcast.235, s32[2,2,8]{2,1,0:T(2,128)S(1)} %copy-done.27, pred[2,2,8]{2,1,0:T(4,128)(4,1)S(1)} %copy-done.30), kind=kOutput, calls=%fused_computation.36 | convolution fusion | flops 33556480 | bytes 3145888 | tf_op jit(solution)/shard_map/km,mvc->kvc/dot_general | solution.py:175
  573.5 6.3 %copy.75 = f32[4,2,16,2,16,8,16]{6,5,4,3,2,1,0:T(8,128)} copy(f32[4,2,16,2,16,8,16]{6,5,4,2,0,3,1:T(8,128)S(1)} %convolution_bitcast_fusion.8) | data formatting | bytes 4194304 | tf_op jit(solution)/shard_map/transpose | solution.py:98
  579.8 11.6 %reshape.309 = f32[4,32,32,128]{3,2,1,0:T(8,128)} reshape(f32[4,2,16,2,16,8,16]{6,5,4,3,2,1,0:T(8,128)} %copy.75) | data formatting | bytes 4194304 | tf_op jit(solution)/shard_map/reshape | solution.py:99
  591.4 10.4 %fusion.86 = f32[4,32,32,128]{3,2,1,0:T(8,128)} fusion(f32[4,32,32,128]{3,2,1,0:T(8,128)} %get-tuple-element.166, f32[4,32,32,128]{3,2,1,0:T(8,128)} %reshape.309, f32[4,32,32,129]{3,2,1,0:T(8,128)} %divide_add_fusion, f32[4,32,33,128]{3,2,1,0:T(8,128)} %divide_add_fusion.2, f32[4,33,32,128]{3,2,1,0:T(8,128)} %divide_add_fusion.4, ...), kind=kLoop, calls=%fused_computation.178 | loop fusion | flops 6291456 | bytes 20971520 | tf_op jit(solution)/shard_map/add | solution.py:191
  (190 shorter events, 111.1 us)
Async XLA Ops:
  0.0 17.3 %copy-start.17 = (f32[3,32,32,128]{3,2,1,0:T(8,128)S(1)}, f32[3,32,32,128]{3,2,1,0:T(8,128)}, u32[]{:S(2)}) copy-start(f32[3,32,32,128]{3,2,1,0:T(8,128)} %param.12) | copy-start | bytes 4718596
  1.5 16.0 %copy-start.28 = (pred[2,2,8]{2,1,0:T(4,128)(4,1)}, pred[2,2,8]{2,1,0:T(4,128)(4,1)S(1)}, u32[]{:S(2)}) copy-start(pred[2,2,8]{2,1,0:T(4,128)(4,1)S(1)} %get-tuple-element.191) | copy-start | bytes 100
  1.5 16.0 %copy-start.43 = (pred[2,2,8]{2,1,0:T(4,128)(4,1)}, pred[2,2,8]{2,1,0:T(4,128)(4,1)S(1)}, u32[]{:S(2)}) copy-start(pred[2,2,8]{2,1,0:T(4,128)(4,1)S(1)} %get-tuple-element.192) | copy-start | bytes 100
  1.8 15.7 %copy-start.34 = (pred[32]{0:T(512)(128)(4,1)}, pred[32]{0:T(512)(128)(4,1)S(1)}, u32[]{:S(2)}) copy-start(pred[32]{0:T(512)(128)(4,1)S(1)} %ge.17) | copy-start | bytes 100
  3.4 123.7 %all-to-all-start = ((s32[16,1,2]{2,1,0:T(1,128)}), s32[16,1,2]{2,1,0:T(1,128)}, u32[]{:S(2)}, u32[]{:S(2)}) async-start(s32[16,1,2]{2,1,0:T(1,128)} %bitcast.29), calls=%async_computation | async-start | bytes 16384 | tf_op jit(solution)/shard_map/all_to_all | solution.py:159
  12.4 4.9 copy-start.6
  13.2 130.4 %collective-permute-start.5 = (bf16[4,3,32,128]{3,2,1,0:T(8,128)(2,1)}, bf16[4,3,32,128]{3,2,1,0:T(8,128)(2,1)}, u32[]{:S(2)}, u32[]{:S(2)}) collective-permute-start(bf16[4,3,32,128]{3,2,1,0:T(8,128)(2,1)} %get-tuple-element.186), channel_id=1, source_target_pairs={{16,0},{32,16},{48,32},{64,48},{80,64},{96,80},{112,96},{0,112},{1... | collective-permute-start | bytes 294920 | tf_op jit(solution)/shard_map/ppermute | solution.py:23
  17.3 126.3 %collective-permute-start.4 = (bf16[4,3,32,128]{3,2,1,0:T(8,128)(2,1)}, bf16[4,3,32,128]{3,2,1,0:T(8,128)(2,1)}, u32[]{:S(2)}, u32[]{:S(2)}) collective-permute-start(bf16[4,3,32,128]{3,2,1,0:T(8,128)(2,1)} %get-tuple-element.185), channel_id=1, source_target_pairs={{0,16},{16,32},{32,48},{48,64},{64,80},{80,96},{96,112},{112,0},{1... | collective-permute-start | bytes 294920 | tf_op jit(solution)/shard_map/ppermute | solution.py:21
  18.2 120.0 %collective-permute-start.1 = (bf16[3,3,32,128]{3,2,1,0:T(8,128)(2,1)}, bf16[3,3,32,128]{3,2,1,0:T(8,128)(2,1)S(1)}, u32[]{:S(2)}, u32[]{:S(2)}) collective-permute-start(bf16[3,3,32,128]{3,2,1,0:T(8,128)(2,1)} %get-tuple-element.190), channel_id=1, source_target_pairs={{16,0},{32,16},{48,32},{64,48},{80,64},{96,80},{112,96},{0,112},{1... | collective-permute-start | bytes 221192 | tf_op jit(solution)/shard_map/ppermute | solution.py:23
  22.3 115.8 %collective-permute-start = (bf16[3,3,32,128]{3,2,1,0:T(8,128)(2,1)}, bf16[3,3,32,128]{3,2,1,0:T(8,128)(2,1)S(1)}, u32[]{:S(2)}, u32[]{:S(2)}) collective-permute-start(bf16[3,3,32,128]{3,2,1,0:T(8,128)(2,1)} %get-tuple-element.189), channel_id=1, source_target_pairs={{0,16},{16,32},{32,48},{48,64},{64,80},{80,96},{96,112},{112,0},{1... | collective-permute-start | bytes 221192 | tf_op jit(solution)/shard_map/ppermute | solution.py:21
  28.2 10.4 %copy-start = (f32[4,32,32,128]{3,2,1,0:T(8,128)S(1)}, f32[4,32,32,128]{3,2,1,0:T(8,128)}, u32[]{:S(2)}) copy-start(f32[4,32,32,128]{3,2,1,0:T(8,128)} %param.11) | copy-start | bytes 6291460
  38.6 2.8 copy-start.18
  71.2 15.9 %slice-start = ((f32[3,32,32,128]{3,2,1,0:T(8,128)}), f32[1,32,32,128]{3,2,1,0:T(8,128)S(1)}, s32[]{:S(2)}) async-start(f32[3,32,32,128]{3,2,1,0:T(8,128)} %param.12), calls=%async_computation.5 | async-start | bytes 1048576 | tf_op jit(solution)/shard_map/slice | solution.py:127
  87.0 2.5 copy-start.15
  87.0 2.5 copy-start.25
  87.0 2.5 copy-start.35
  87.0 2.5 copy-start.41
  88.9 2.6 copy-start.13
  88.9 2.6 copy-start.5
  89.5 4.7 copy-start.11
  89.5 3.0 copy-start.4
  94.2 25.8 %copy-start.31 = (s32[2,2,8]{2,1,0:T(2,128)S(1)}, s32[2,2,8]{2,1,0:T(2,128)}, u32[]{:S(2)}) copy-start(s32[2,2,8]{2,1,0:T(2,128)} %param.13) | copy-start | bytes 388
  94.3 25.8 %copy-start.37 = (s32[2,2,8]{2,1,0:T(2,128)S(1)}, s32[2,2,8]{2,1,0:T(2,128)}, u32[]{:S(2)}) copy-start(s32[2,2,8]{2,1,0:T(2,128)} %reduce_sum.22) | copy-start | bytes 388
  94.3 25.7 %copy-start.44 = (pred[2,2,8]{2,1,0:T(4,128)(4,1)S(1)}, pred[2,2,8]{2,1,0:T(4,128)(4,1)}, u32[]{:S(2)}) copy-start(pred[2,2,8]{2,1,0:T(4,128)(4,1)} %copy-done.43) | copy-start | bytes 100
  120.0 168.8 %copy-start.26 = (s32[2,2,8]{2,1,0:T(2,128)}, s32[2,2,8]{2,1,0:T(2,128)S(1)}, u32[]{:S(2)}) copy-start(s32[2,2,8]{2,1,0:T(2,128)S(1)} %fusion.134) | copy-start | bytes 388
  127.1 16.5 %copy-start.7 = (bf16[4,32,32,128]{3,2,1,0:T(8,128)(2,1)S(1)}, bf16[4,32,32,128]{3,2,1,0:T(8,128)(2,1)}, u32[]{:S(2)}) copy-start(bf16[4,32,32,128]{3,2,1,0:T(8,128)(2,1)} %copy-done.6) | copy-start | bytes 3145732
  127.1 57.6 %all-to-all-start.1 = ((bf16[16,2,7,4096]{3,1,2,0:T(2,128)(2,1)}), bf16[16,2,7,4096]{3,1,2,0:T(2,128)(2,1)}, u32[]{:S(2)}, u32[]{:S(2)}) async-start(bf16[16,2,7,4096]{3,1,2,0:T(2,128)(2,1)} %copy.61), calls=%async_computation.1 | async-start | bytes 3670016 | tf_op jit(solution)/shard_map/all_to_all | solution.py:158
  138.2 119.1 %copy-start.32 = (s32[16,1,2]{0,2,1:T(2,128)}, s32[16,1,2]{0,2,1:T(2,128)S(1)}, u32[]{:S(2)}) copy-start(s32[16,1,2]{0,2,1:T(2,128)S(1)} %copy.58) | copy-start | bytes 388
  138.3 19.4 %collective-permute-start.3 = (bf16[3,38,3,128]{3,2,1,0:T(4,128)(2,1)S(1)}, bf16[3,38,3,128]{3,2,1,0:T(4,128)(2,1)S(1)}, u32[]{:S(2)}, u32[]{:S(2)}) collective-permute-start(bf16[3,38,3,128]{3,2,1,0:T(4,128)(2,1)S(1)} %get-tuple-element.188), channel_id=1, source_target_pairs={{1,0},{2,1},{3,2},{4,3},{5,4},{6,5},{7,6},{8,7},{9,8},{10,9},{11,1... | collective-permute-start | bytes 262664 | tf_op jit(solution)/shard_map/ppermute | solution.py:23
  143.6 19.1 %collective-permute-start.2 = (bf16[3,38,3,128]{3,2,1,0:T(4,128)(2,1)S(1)}, bf16[3,38,3,128]{3,2,1,0:T(4,128)(2,1)S(1)}, u32[]{:S(2)}, u32[]{:S(2)}) collective-permute-start(bf16[3,38,3,128]{3,2,1,0:T(4,128)(2,1)S(1)} %get-tuple-element.187), channel_id=1, source_target_pairs={{0,1},{1,2},{2,3},{3,4},{4,5},{5,6},{6,7},{7,8},{8,9},{9,10},{10,1... | collective-permute-start | bytes 262664 | tf_op jit(solution)/shard_map/ppermute | solution.py:21
  144.6 19.6 %collective-permute-start.7 = (bf16[4,38,3,128]{3,2,1,0:T(4,128)(2,1)S(1)}, bf16[4,38,3,128]{3,2,1,0:T(4,128)(2,1)S(1)}, u32[]{:S(2)}, u32[]{:S(2)}) collective-permute-start(bf16[4,38,3,128]{3,2,1,0:T(4,128)(2,1)S(1)} %get-tuple-element.182), channel_id=1, source_target_pairs={{1,0},{2,1},{3,2},{4,3},{5,4},{6,5},{7,6},{8,7},{9,8},{10,9},{11,1... | collective-permute-start | bytes 350216 | tf_op jit(solution)/shard_map/ppermute | solution.py:23
  150.0 14.4 %collective-permute-start.6 = (bf16[4,38,3,128]{3,2,1,0:T(4,128)(2,1)S(1)}, bf16[4,38,3,128]{3,2,1,0:T(4,128)(2,1)S(1)}, u32[]{:S(2)}, u32[]{:S(2)}) collective-permute-start(bf16[4,38,3,128]{3,2,1,0:T(4,128)(2,1)S(1)} %get-tuple-element.181), channel_id=1, source_target_pairs={{0,1},{1,2},{2,3},{3,4},{4,5},{5,6},{6,7},{7,8},{8,9},{9,10},{10,1... | collective-permute-start | bytes 350216 | tf_op jit(solution)/shard_map/ppermute | solution.py:21
  162.9 3.6 copy-start.19
  163.0 3.7 copy-start.21
  163.0 1.8 copy-start.8
  164.1 18.8 %copy-start.23 = (f32[38,32,128]{2,1,0:T(8,128)}, f32[38,32,128]{2,1,0:T(8,128)S(1)}, u32[]{:S(2)}) copy-start(f32[38,32,128]{2,1,0:T(8,128)S(1)} %convert_bitcast_fusion.1) | copy-start | bytes 1867780
  189.7 5.0 copy-start.38
  194.7 4.6 copy-start.45
  194.8 4.6 copy-start.46
  194.8 4.6 copy-start.47
  194.8 4.6 copy-start.48
  261.6 22.6 %all-to-all-start.2 = ((bf16[16,2,4,4096]{3,2,1,0:T(4,128)(2,1)}), bf16[16,2,4,4096]{3,2,1,0:T(4,128)(2,1)}, u32[]{:S(2)}, u32[]{:S(2)}) async-start(bf16[16,2,4,4096]{3,2,1,0:T(4,128)(2,1)} %copy.65), calls=%async_computation.2 | async-start | bytes 2097152 | tf_op jit(solution)/shard_map/all_to_all | solution.py:171
  284.2 4.7 copy-start.29
  309.0 11.6 %copy-start.1 = (f32[4,32,32,128]{3,2,1,0:T(8,128)S(1)}, f32[4,32,32,128]{3,2,1,0:T(8,128)}, u32[]{:S(2)}) copy-start(f32[4,32,32,128]{3,2,1,0:T(8,128)} %param.11) | copy-start | bytes 6291460
  330.1 70.5 %copy-start.9 = (bf16[4,32,32,128]{3,2,1,0:T(8,128)(2,1)}, bf16[4,32,32,128]{3,2,1,0:T(8,128)(2,1)S(1)}, u32[]{:S(2)}) copy-start(bf16[4,32,32,128]{3,2,1,0:T(8,128)(2,1)S(1)} %get-tuple-element.165) | copy-start | bytes 3145732
  347.0 15.2 %copy-start.16 = (bf16[32,3,4096]{2,0,1:T(8,128)(2,1)S(1)}, bf16[32,3,4096]{2,0,1:T(8,128)(2,1)}, u32[]{:S(2)}) copy-start(bf16[32,3,4096]{2,0,1:T(8,128)(2,1)} %reshape.310) | copy-start | bytes 2359300
  347.0 15.2 %copy-start.36 = (pred[32]{0:T(512)(128)(4,1)S(1)}, pred[32]{0:T(512)(128)(4,1)}, u32[]{:S(2)}) copy-start(pred[32]{0:T(512)(128)(4,1)} %copy-done.34) | copy-start | bytes 100
  347.0 15.2 %copy-start.42 = (s32[32]{0:T(128)S(1)}, s32[32]{0:T(128)}, u32[]{:S(2)}) copy-start(s32[32]{0:T(128)} %copy-done.40) | copy-start | bytes 388
  371.2 4.6 copy-start.3
  371.2 81.9 %all-to-all-start.3 = ((bf16[16,2,7,4096]{3,1,2,0:T(2,128)(2,1)}), bf16[16,2,7,4096]{3,1,2,0:T(2,128)(2,1)}, u32[]{:S(2)}, u32[]{:S(2)}) async-start(bf16[16,2,7,4096]{3,1,2,0:T(2,128)(2,1)} %copy.69), calls=%async_computation.3 | async-start | bytes 3670016 | tf_op jit(solution)/shard_map/all_to_all | solution.py:158
  375.7 4.3 copy-start.14
  376.5 20.0 %collective-permute-start.9 = (bf16[4,3,32,128]{3,2,1,0:T(8,128)(2,1)S(1)}, bf16[4,3,32,128]{3,2,1,0:T(8,128)(2,1)S(1)}, u32[]{:S(2)}, u32[]{:S(2)}) collective-permute-start(bf16[4,3,32,128]{3,2,1,0:T(8,128)(2,1)S(1)} %get-tuple-element.184), channel_id=1, source_target_pairs={{16,0},{32,16},{48,32},{64,48},{80,64},{96,80},{112,96},{0,112},{1... | collective-permute-start | bytes 294920 | tf_op jit(solution)/shard_map/ppermute | solution.py:23
  380.0 20.6 %collective-permute-start.8 = (bf16[4,3,32,128]{3,2,1,0:T(8,128)(2,1)S(1)}, bf16[4,3,32,128]{3,2,1,0:T(8,128)(2,1)S(1)}, u32[]{:S(2)}, u32[]{:S(2)}) collective-permute-start(bf16[4,3,32,128]{3,2,1,0:T(8,128)(2,1)S(1)} %get-tuple-element.183), channel_id=1, source_target_pairs={{0,16},{16,32},{32,48},{48,64},{64,80},{80,96},{96,112},{112,0},{1... | collective-permute-start | bytes 294920 | tf_op jit(solution)/shard_map/ppermute | solution.py:21
  380.0 27.7 %copy-start.12 = (f32[32,32,129]{2,1,0:T(8,128)S(1)}, f32[32,32,129]{2,1,0:T(8,128)}, u32[]{:S(2)}) copy-start(f32[32,32,129]{2,1,0:T(8,128)} %copy-done.11) | copy-start | bytes 1585156
  400.7 32.7 %collective-permute-start.11 = (bf16[4,38,3,128]{3,2,1,0:T(4,128)(2,1)S(1)}, bf16[4,38,3,128]{3,2,1,0:T(4,128)(2,1)S(1)}, u32[]{:S(2)}, u32[]{:S(2)}) collective-permute-start(bf16[4,38,3,128]{3,2,1,0:T(4,128)(2,1)S(1)} %get-tuple-element.180), channel_id=1, source_target_pairs={{1,0},{2,1},{3,2},{4,3},{5,4},{6,5},{7,6},{8,7},{9,8},{10,9},{11,1... | collective-permute-start | bytes 350216 | tf_op jit(solution)/shard_map/ppermute | solution.py:23
  407.7 25.7 %copy-start.10 = (bf16[4,32,32,128]{3,2,1,0:T(8,128)(2,1)S(1)}, bf16[4,32,32,128]{3,2,1,0:T(8,128)(2,1)}, u32[]{:S(2)}) copy-start(bf16[4,32,32,128]{3,2,1,0:T(8,128)(2,1)} %copy-done.9) | copy-start | bytes 3145732
  407.7 25.7 %collective-permute-start.10 = (bf16[4,38,3,128]{3,2,1,0:T(4,128)(2,1)S(1)}, bf16[4,38,3,128]{3,2,1,0:T(4,128)(2,1)S(1)}, u32[]{:S(2)}, u32[]{:S(2)}) collective-permute-start(bf16[4,38,3,128]{3,2,1,0:T(4,128)(2,1)S(1)} %get-tuple-element.179), channel_id=1, source_target_pairs={{0,1},{1,2},{2,3},{3,4},{4,5},{5,6},{6,7},{7,8},{8,9},{9,10},{10,1... | collective-permute-start | bytes 350216 | tf_op jit(solution)/shard_map/ppermute | solution.py:21
  435.6 15.7 %copy-start.24 = (f32[38,32,128]{2,1,0:T(8,128)S(1)}, f32[38,32,128]{2,1,0:T(8,128)}, u32[]{:S(2)}) copy-start(f32[38,32,128]{2,1,0:T(8,128)} %copy-done.23) | copy-start | bytes 1867780
  458.2 5.0 copy-start.39
  467.6 58.0 %copy-start.33 = (s32[16,1,2]{0,2,1:T(2,128)S(1)}, s32[16,1,2]{0,2,1:T(2,128)}, u32[]{:S(2)}) copy-start(s32[16,1,2]{0,2,1:T(2,128)} %copy-done.32) | copy-start | bytes 388
  529.9 25.0 %all-to-all-start.4 = ((bf16[16,2,4,4096]{3,2,1,0:T(4,128)(2,1)}), bf16[16,2,4,4096]{3,2,1,0:T(4,128)(2,1)}, u32[]{:S(2)}, u32[]{:S(2)}) async-start(bf16[16,2,4,4096]{3,2,1,0:T(4,128)(2,1)} %copy.73), calls=%async_computation.4 | async-start | bytes 2097152 | tf_op jit(solution)/shard_map/all_to_all | solution.py:171
  555.0 4.7 copy-start.27
  555.0 4.7 copy-start.30
  579.8 11.6 %copy-start.2 = (f32[4,32,32,128]{3,2,1,0:T(8,128)S(1)}, f32[4,32,32,128]{3,2,1,0:T(8,128)}, u32[]{:S(2)}) copy-start(f32[4,32,32,128]{3,2,1,0:T(8,128)} %param.11) | copy-start | bytes 6291460
  (3 other events, 2.7 us)
where the time goes:
time: 608 us; the launch traced here: 602 us
  local copies, waits for them, and re-layouts  193 us (32%)
  matrix products  156 us (26%)
  other arithmetic  153 us (25%)
  starting transfers between devices  60.9 us (10%)
  waiting for transfers between devices  38.1 us (6%)
    add x6, other arithmetic, flux_difference(): weno_face(upper(0), upper(1), upper(2), upper(3), upper(4))  113 us
    dot_general x14, matrix products, apply_pair(): jnp.einsum('hg,bgc->bhc', w_mid, hidden, preferred_element_type=jnp.float32)  64.9 us
    dot_general x14, matrix products, apply_pair(): jnp.einsum('vh,bhc->bvc', w_out, hidden, preferred_element_type=jnp.float32)  50.9 us
    reshape x4, local copies, waits for them, and re-layouts, to_blocks(): field.reshape(channels, size_x // BS, BS, size_y // BS, BS, size_z // BS,...  35.8 us
    reshape x2, local copies, waits for them, and re-layouts, to_blocks(): return shaped.reshape(-1, channels, BS ** 3)  31 us
    ppermute x6, starting transfers between devices, padded_2(): lax.ppermute(head, axis, [((i + 1) % count, i) for i in range(count)])  29.6 us
    dot_general x2, matrix products, sources(): jnp.einsum('km,mvc->kvc', packing.astype(jnp.float32), returned, precisio...  27.6 us
    another operation x5, local copies, waits for them, and re-layouts  27.4 us
  transfers between devices with their start and end apart: 17, of which 7 were waited for; matrix products, arithmetic and copies ran while one was open for 35% of the time, Pallas kernels for 0%

commit v1 on v0

v1 whole, which is shorter than its diff:
```python
import functools

import jax
import jax.numpy as jnp
from jax import lax
from jax.experimental import pallas as pl
from jax.experimental.pallas import tpu as pltpu
from jax.sharding import PartitionSpec as P

BS = 16
EPS = 1e-06
STEP = 0.25
NV = 4
NF = 7
HID = 128
WENO_TYPE = jnp.float32
SILU_TYPE = jnp.float32
VMEM_LIMIT = 56 * 1024 * 1024


def curvature(d1, d2, d3, d4):
    one = lambda x: jnp.asarray(x, d1.dtype)
    g2 = one(0.609375) * (d2 * d2) + one(0.75 * EPS)
    g3 = one(0.609375) * (d3 * d3) + one(0.75 * EPS)
    e0 = d1 - one(1.375) * d2
    e1 = d2 - one(0.625) * d3
    e2 = d4 - one(1.375) * d3
    r0 = reciprocal(e0 * e0 + g2)
    r1 = reciprocal(e1 * e1 + g3)
    r2 = reciprocal(e2 * e2 + g3)
    s1 = d3 - d2
    t0 = s1 - (d2 - d1)
    t2 = (d4 - d3) - s1
    w0 = r0 * r0
    w2 = one(1.5) * (r2 * r2)
    total = one(0.5) * w0 + one(3.0) * (r1 * r1) + w2
    return (w0 * t0 + w2 * t2) * reciprocal(total)


def reciprocal(x):
    return pl.reciprocal(x, approx=True)


def face_flux(fd, vd, alpha, centre):
    m = [alpha * d for d in vd]
    p = [(fd[j] + m[j]).astype(WENO_TYPE) for j in range(4)]
    q = [(fd[j] - m[j]).astype(WENO_TYPE) for j in range(1, 5)]
    bend = (curvature(*p) - curvature(*q[::-1])).astype(jnp.float32)
    rest = (fd[1] - fd[3]) + ((m[1] - m[2]) + (m[3] - m[2])) - bend
    return centre + rest * (1.0 / 6.0)


def roll(x, shift):
    return pltpu.roll(x, shift % x.shape[-1], axis=x.ndim - 1)


def depth_kernel(s_ref, v_ref, band_ref, wsel_ref, wmid_ref, wdeep_ref, wout_ref, out_ref):
    nx, ny = s_ref.shape[1], s_ref.shape[2]
    do_closure(s_ref, v_ref, band_ref, wsel_ref, wmid_ref, wdeep_ref, wout_ref, out_ref)
    tiles = ny // 8

    @pl.loop(0, nx * tiles)
    def _(step):
        i = step // tiles
        y = pl.ds(pl.multiple_of((step % tiles) * 8, 8), 8)
        u = 0.5 * v_ref[2, i, y, :]
        mag = jnp.abs(u)
        alpha = jnp.maximum(mag, roll(mag, -1))
        for k in range(NV):
            v = s_ref[k, i, y, :]
            f = u * v
            f1 = roll(f, -1)
            fd = f1 - f
            vd = roll(v, -1) - v
            fds = [roll(fd, 2), roll(fd, 1), fd, roll(fd, -1), roll(fd, -2)]
            vds = [roll(vd, 2), roll(vd, 1), vd, roll(vd, -1), roll(vd, -2)]
            flux = face_flux(fds, vds, alpha, f + f1)
            out_ref[k, i, y, :] = out_ref[k, i, y, :] - (flux - roll(flux, 1))


GX = 4


def silu_half(h):
    h = h.astype(SILU_TYPE)
    return (h + h * jnp.tanh(h)).astype(jnp.bfloat16)


def do_closure(s_ref, v_ref, band_ref, wsel_ref, wmid_ref, wdeep_ref, wout_ref, out_ref):
    nx, ny, nz = s_ref.shape[1:]
    rows = ny // BS

    @pl.loop(0, (nx // GX) * rows)
    def _(step):
        i0 = (step // rows) * GX
        y = pl.ds(pl.multiple_of((step % rows) * BS, BS), BS)
        feats = []
        for g in range(GX):
            parts = [s_ref[k, i0 + g, y, :].astype(jnp.bfloat16) for k in range(NV)]
            parts += [v_ref[k, i0 + g, y, :].astype(jnp.bfloat16) for k in range(3)]
            parts.append(jnp.zeros_like(parts[0]))
            feats.append(jnp.concatenate(parts, axis=0).T)
        lhs = jnp.concatenate(feats, axis=0)
        total = jnp.zeros((GX * nz, 128), jnp.float32)
        for p in range(BS // 2):
            h = jnp.dot(lhs, wsel_ref[:, p * 256:(p + 1) * 256], preferred_element_type=jnp.float32)
            h = silu_half(h)
            h = silu_half(jnp.dot(h, wmid_ref[...], preferred_element_type=jnp.float32))
            h = silu_half(jnp.dot(h, wdeep_ref[...], preferred_element_type=jnp.float32))
            total = total + jnp.dot(h, wout_ref[p * 256:(p + 1) * 256, :], preferred_element_type=jnp.float32)
        band = band_ref[i0 // BS, step % rows, :]
        for g in range(GX):
            back = total[g * nz:(g + 1) * nz].T
            for k in range(NV):
                out_ref[k, i0 + g, y, :] = jnp.where(band[None, :] > 0, back[k * BS:(k + 1) * BS, :], 0.0)


def cross_kernel(last, *refs):
    if last:
        s_ref, v_ref, r_ref, xlo, xhi, ylo, yhi, uxlo, uxhi, uylo, uyhi, old_ref, out_ref, acc = refs
    else:
        s_ref, v_ref, r_ref, xlo, xhi, ylo, yhi, uxlo, uxhi, uylo, uyhi, out_ref, acc = refs
    nx, ny = s_ref.shape[1], s_ref.shape[2]

    def sweep(n, load_v, load_u, emit):
        u_prev, v_prev = None, None
        fds, vds, us, fs = [], [], [], []
        prev_flux = None
        mags = []
        for j in range(-3, n + 3):
            u = 0.5 * load_u(j)
            v = load_v(j)
            f = u * v
            us.append(u)
            fs.append(f)
            if v_prev is not None:
                fds.append(f - fs[-2])
                vds.append(v - v_prev)
            v_prev = v
            if len(fds) >= 5:
                i = len(us) - 1
                alpha = jnp.maximum(jnp.abs(us[i - 3]), jnp.abs(us[i - 2]))
                flux = face_flux(fds[-5:], vds[-5:], alpha, fs[i - 3] + fs[i - 2])
                if prev_flux is not None:
                    emit(j - 3, flux - prev_flux)
                prev_flux = flux

    ytiles = ny // 8
    xtiles = nx // 8

    @pl.loop(0, xtiles * NV)
    def _(step):
        k = step // xtiles
        x0 = pl.multiple_of((step % xtiles) * 8, 8)
        xs = pl.ds(x0, 8)

        def load_v(j):
            if j < 0:
                return ylo[k, j + 3, xs, :].astype(jnp.float32)
            if j >= ny:
                return yhi[k, j - ny, xs, :].astype(jnp.float32)
            return s_ref.reshape(NV * nx * ny, 128)[pl.ds((k * nx + x0) * ny + j, 8, stride=ny), :]

        def load_u(j):
            if j < 0:
                return uylo[j + 3, xs, :].astype(jnp.float32)
            if j >= ny:
                return uyhi[j - ny, xs, :].astype(jnp.float32)
            return v_ref.reshape(3 * nx * ny, 128)[pl.ds((nx + x0) * ny + j, 8, stride=ny), :]

        def emit(j, value):
            acc.reshape(NV * nx * ny, 128)[pl.ds((k * nx + x0) * ny + j, 8, stride=ny), :] = value

        sweep(ny, load_v, load_u, emit)

    @pl.loop(0, ytiles * NV)
    def _(step):
        k = step // ytiles
        ys = pl.ds(pl.multiple_of((step % ytiles) * 8, 8), 8)

        def load_v(j):
            if j < 0:
                return xlo[k, j + 3, ys, :].astype(jnp.float32)
            if j >= nx:
                return xhi[k, j - nx, ys, :].astype(jnp.float32)
            return s_ref[k, j, ys, :]

        def load_u(j):
            if j < 0:
                return uxlo[j + 3, ys, :].astype(jnp.float32)
            if j >= nx:
                return uxhi[j - nx, ys, :].astype(jnp.float32)
            return v_ref[0, j, ys, :]

        def emit(j, value):
            rate = r_ref[k, j, ys, :] - acc[k, j, ys, :] - value
            stepped = s_ref[k, j, ys, :] + STEP * rate
            if last:
                stepped = 0.75 * old_ref[k, j, ys, :] + 0.25 * stepped
            out_ref[k, j, ys, :] = stepped

        sweep(nx, load_v, load_u, emit)


def vmem(n):
    return [pl.BlockSpec(memory_space=pltpu.VMEM)] * n


def depth_call(state, velocity, band, weights):
    cells = state.size // NV
    return pl.pallas_call(
        depth_kernel,
        out_shape=jax.ShapeDtypeStruct(state.shape, jnp.float32),
        in_specs=vmem(7),
        out_specs=pl.BlockSpec(memory_space=pltpu.VMEM),
        compiler_params=pltpu.CompilerParams(vmem_limit_bytes=VMEM_LIMIT),
        cost_estimate=pl.CostEstimate(flops=cells * 262144, bytes_accessed=6 << 20, transcendentals=0),
        name="depth",
    )(state, velocity, band, *weights)


def cross_call(state, velocity, part, halos, old):
    last = old is not None
    args = (state, velocity, part, *halos) + ((old,) if last else ())
    return pl.pallas_call(
        functools.partial(cross_kernel, last),
        out_shape=jax.ShapeDtypeStruct(state.shape, jnp.float32),
        in_specs=vmem(len(args)),
        out_specs=pl.BlockSpec(memory_space=pltpu.VMEM),
        scratch_shapes=[pltpu.VMEM(state.shape, jnp.float32)],
        compiler_params=pltpu.CompilerParams(vmem_limit_bytes=VMEM_LIMIT),
        name="cross",
    )(*args)


def send(value, axis, up):
    n = lax.axis_size(axis)
    if up:
        return lax.ppermute(value, axis, [(i, (i + 1) % n) for i in range(n)])
    return lax.ppermute(value, axis, [((i + 1) % n, i) for i in range(n)])


def halos_of(field):
    small = field.astype(jnp.bfloat16)
    xlo = send(small[:, -3:], "gx", True)
    xhi = send(small[:, :3], "gx", False)
    ylo = send(small[:, :, -3:].transpose(0, 2, 1, 3), "gy", True)
    yhi = send(small[:, :, :3].transpose(0, 2, 1, 3), "gy", False)
    return xlo, xhi, ylo, yhi


def prepare(w_in, w_mid, w_deep, w_out):
    half = jnp.asarray(0.5, jnp.bfloat16)
    eye = jnp.eye(BS, dtype=jnp.bfloat16)
    padded = jnp.pad(w_in.T * half, ((0, 1), (0, 0)))
    wsel = (padded[:, None, None, :] * eye[None, :, :, None]).reshape(8 * BS, BS * HID)
    two = jnp.eye(2, dtype=jnp.bfloat16)
    wmid = jnp.kron(two, w_mid.T * half)
    wdeep = jnp.kron(two, w_deep.T * half)
    wout = (w_out.T[None, :, :, None] * eye[:, None, None, :]).reshape(BS * HID, NV * BS)
    wout = jnp.pad(wout, ((0, 0), (0, 128 - NV * BS)))
    return wsel, wmid, wdeep, wout


def shards(state, velocity, routes, w_in, w_mid, w_deep, w_out):
    weights = prepare(w_in, w_mid, w_deep, w_out)
    band = jnp.repeat((routes >= 0).astype(jnp.float32), BS, axis=2)
    vx = velocity[0].astype(jnp.bfloat16)
    vy = velocity[1].astype(jnp.bfloat16)
    speeds = (
        send(vx[-3:], "gx", True),
        send(vx[:3], "gx", False),
        send(vy[:, -3:].transpose(1, 0, 2), "gy", True),
        send(vy[:, :3].transpose(1, 0, 2), "gy", False),
    )

    halos = halos_of(state) + speeds
    part = depth_call(state, velocity, band, weights)
    first = cross_call(state, velocity, part, halos, None)
    halos = halos_of(first) + speeds
    part = depth_call(first, velocity, band, weights)
    return cross_call(first, velocity, part, halos, state)


def solution(mesh):
    placed = (
        P(None, "gx", "gy", None),
        P(None, "gx", "gy", None),
        P("gx", "gy", None),
        P(),
        P(),
        P(),
        P(),
    )
    return jax.shard_map(
        shards, mesh=mesh, in_specs=placed, out_specs=P(None, "gx", "gy", None), check_vma=False
    )
```

time: 608 us -> 259 us (0.43)
  Pallas kernels: 0 us -> 213 us
  local copies, waits for them, and re-layouts: 193 us -> 17.2 us
  matrix products: 156 us -> 0 us
  other arithmetic: 153 us -> 0.51 us
  waiting for transfers between devices: 38.1 us -> 0.03 us
  starting transfers between devices: 60.9 us -> 27.2 us
    pallas_call x0 -> x4, Pallas kernels: none -> 213 us  [the longest x2 168 us: depth_call(): pl.pallas_call(depth_kernel, out_shape=jax.ShapeDtypeStruct(state.shape,...]
    dot_general x36 -> x0, matrix products: 156 us -> none  [the longest x14 64.9 us: apply_pair(): jnp.einsum('hg,bgc->bhc', w_mid, hidden, preferred_element_type=jnp.float32)]
    add x10 -> x0, other arithmetic: 123 us -> none  [the longest x6 113 us: flux_difference(): weno_face(upper(0), upper(1), upper(2), upper(3), upper(4))]
    reshape x14 -> x1, local copies, waits for them, and re-layouts: 114 us -> 0.68 us  [shards(): band = jnp.repeat((routes >= 0).astype(jnp.float32), BS, axis=2)]
    ppermute x12, waiting for transfers between devices: 31.8 us -> 0.03 us  [the longest x6 0.02 us: send(): return lax.ppermute(value, axis, [((i + 1) % n, i) for i in range(n)])]
    all_to_all x5 -> x0, starting transfers between devices: 31.2 us -> none  [the longest x2 12.5 us: sources(): lax.all_to_all(outgoing, 'gy', split_axis=0, concat_axis=0, tiled=True)]
    another operation x5 -> x0, local copies, waits for them, and re-layouts: 27.4 us -> none
    convert_element_type x5 -> x3, other arithmetic: 13.9 us -> 0.02 us  [the longest x1 0.01 us: prepare(): eye = jnp.eye(BS, dtype=jnp.bfloat16)]
  transfers between devices with their start and end apart: 17 -> 12, of which waited for: 7 -> 0; matrix products, arithmetic and copies ran while one was open for 35% -> 4% of each run, Pallas kernels for 0% -> 65%
where the time goes in v1:
time: 259 us; the launch traced here: 258 us
  Pallas kernels  213 us (82%)
  starting transfers between devices  27.2 us (11%)
  local copies, waits for them, and re-layouts  17.2 us (7%)
    pallas_call x2, Pallas kernels, depth_call(): pl.pallas_call(depth_kernel, out_shape=jax.ShapeDtypeStruct(state.shape,...  168 us
    pallas_call x2, Pallas kernels, cross_call(): pl.pallas_call(functools.partial(cross_kernel, last), out_shape=jax.Shape...  44.6 us
    ppermute x6, starting transfers between devices, send(): return lax.ppermute(value, axis, [((i + 1) % n, i) for i in range(n)])  26.9 us
    unnamed x28, local copies, waits for them, and re-layouts  7.27 us
  transfers between devices with their start and end apart: 12, of which 0 were waited for; matrix products, arithmetic and copies ran while one was open for 4% of the time, Pallas kernels for 65%

profile of v1, /device:TPU:0, one launch (start us, length us, event | category | flops | bytes accessed | tf_op | source)
XLA Modules:
  0.0 258.2 jit_solution(9000524307683433594)
XLA Ops:
  0.0 2.5 copy.50
  2.5 5.0 %collective-permute-start.7 = (bf16[3,32,128]{2,1,0:T(8,128)(2,1)S(1)}, bf16[3,32,128]{2,1,0:T(8,128)(2,1)S(1)}, u32[]{:S(2)}, u32[]{:S(2)}) collective-permute-start(bf16[3,32,128]{2,1,0:T(8,128)(2,1)S(1)} %get-tuple-element.15), channel_id=1, source_target_pairs={{1,0},{2,1},{3,2},{4,3},{5,4},{6,5},{7,6},{8,7},{9,8},{10,9},{11,1... | collective-permute-start | bytes 73736 | tf_op jit(solution)/shard_map/ppermute | solution.py:240
  7.5 0.0 collective-permute-start.6
  7.5 4.2 %collective-permute-start.5 = (bf16[3,32,128]{2,0,1:T(4,128)(2,1)S(1)}, bf16[3,32,128]{2,0,1:T(4,128)(2,1)S(1)}, u32[]{:S(2)}, u32[]{:S(2)}) collective-permute-start(bf16[3,32,128]{2,0,1:T(4,128)(2,1)S(1)} %get-tuple-element.13), channel_id=1, source_target_pairs={{16,0},{32,16},{48,32},{64,48},{80,64},{96,80},{112,96},{0,112},{1... | collective-permute-start | bytes 73736 | tf_op jit(solution)/shard_map/ppermute | solution.py:240
  11.8 0.0 collective-permute-start.4
  11.8 0.0 copy-done
  11.8 1.2 copy.49
  13.0 0.0 copy-start.10
  13.0 0.1 fusion.2
  13.1 4.2 %collective-permute-start.1 = (bf16[4,3,32,128]{3,1,2,0:T(4,128)(2,1)S(1)}, bf16[4,3,32,128]{3,1,2,0:T(4,128)(2,1)S(1)}, u32[]{:S(2)}, u32[]{:S(2)}) collective-permute-start(bf16[4,3,32,128]{3,1,2,0:T(4,128)(2,1)S(1)} %get-tuple-element.11), channel_id=1, source_target_pairs={{16,0},{32,16},{48,32},{64,48},{80,64},{96,80},{112,96},{0,112},{1... | collective-permute-start | bytes 294920 | tf_op jit(solution)/shard_map/ppermute | solution.py:240
  17.4 0.0 copy-done.9
  17.4 0.1 copy.22
  17.5 0.0 copy-done.7
  17.5 0.1 copy.23
  17.6 0.0 copy-done.8
  17.6 0.1 copy.24
  17.7 0.1 broadcast_multiply_fusion.1
  17.9 0.3 broadcast_multiply_fusion.2
  18.1 0.7 copy_bitcast_fusion.2
  18.9 0.1 broadcast_multiply_fusion
  19.0 0.1 broadcast_in_dim.8
  19.1 0.7 reshape.52.band_ref
  19.8 0.1 copy.52
  19.8 0.3 copy.25
  20.1 0.9 pad.9.wout_ref
  21.0 1.0 copy.51
  22.0 0.0 collective-permute-done.5
  22.0 5.1 %collective-permute-start.3 = (bf16[4,3,32,128]{3,2,1,0:T(8,128)(2,1)S(1)}, bf16[4,3,32,128]{3,2,1,0:T(8,128)(2,1)S(1)}, u32[]{:S(2)}, u32[]{:S(2)}) collective-permute-start(bf16[4,3,32,128]{3,2,1,0:T(8,128)(2,1)S(1)} %get-tuple-element.9), channel_id=1, source_target_pairs={{1,0},{2,1},{3,2},{4,3},{5,4},{6,5},{7,6},{8,7},{9,8},{10,9},{11,1... | collective-permute-start | bytes 294920 | tf_op jit(solution)/shard_map/ppermute | solution.py:240
  27.1 0.0 collective-permute-done.4
  27.1 0.0 collective-permute-start.2
  27.1 0.0 collective-permute-done.1
  27.1 0.3 collective-permute-start
  27.4 84.2 %depth.2.refs_2_ = f32[4,32,32,128]{3,2,1,0:T(8,128)} custom-call(f32[4,32,32,128]{3,2,1,0:T(8,128)} %refs_11_.1, f32[3,32,32,128]{3,2,1,0:T(8,128)} %refs_1_.3, f32[2,2,128]{2,1,0:T(2,128)} %reshape.52.band_ref, bf16[128,2048]{1,0:T(8,128)(2,1)} %bitcast.50, bf16[256,256]{1,0:T(8,128)(2,1)} %get-tuple-element.20.wmid_ref, ...), custom_call_target="tpu_custom_call" | custom-call | flops 34359738368 | bytes 6291456 | tf_op jit(solution)/shard_map/depth/pallas_call | solution.py:211
  111.6 0.6 copy.31.refs_8_
  112.2 0.6 copy.30.refs_7_
  112.8 0.6 copy.29.refs_4_
  113.5 0.0 collective-permute-done
  113.5 0.6 copy.28.refs_3_
  114.1 0.0 collective-permute-done.7.refs_10_
  114.1 0.0 collective-permute-done.6.refs_9_
  114.1 0.0 copy-start.6
  114.1 0.0 collective-permute-done.3.refs_6_
  114.2 0.0 collective-permute-done.2.refs_5_
  114.2 0.6 copy-done.5
  114.7 0.0 copy-done.6
  114.7 0.1 copy-done.1
  114.8 0.7 copy-done.4
  115.4 21.9 %cross.2.s_ref.refs_0_ = f32[4,32,32,128]{3,2,1,0:T(8,128)} custom-call(f32[4,32,32,128]{3,2,1,0:T(8,128)} %refs_11_.1, f32[3,32,32,128]{3,2,1,0:T(8,128)} %refs_1_.3, f32[4,32,32,128]{3,2,1,0:T(8,128)} %depth.2.refs_2_, bf16[4,3,32,128]{3,2,1,0:T(8,128)(2,1)} %copy.28.refs_3_, bf16[4,3,32,128]{3,2,1,0:T(8,128)(2,1)} %copy.29.refs_4_, ...), custom_call_target="tpu_custom_call" | custom-call | tf_op jit(solution)/shard_map/cross/pallas_call | solution.py:225
  137.3 2.8 %copy.48 = bf16[4,32,32,128]{3,1,2,0:T(8,128)(2,1)S(1)} copy(f32[4,32,32,128]{3,2,1,0:T(8,128)} %cross.2.s_ref.refs_0_) | data formatting | bytes 3145728 | tf_op jit(solution)/shard_map/cross/pallas_call | solution.py:225
  140.1 0.1 fusion.1
  140.2 5.2 %collective-permute-start.11 = (bf16[4,3,32,128]{3,2,1,0:T(8,128)(2,1)S(1)}, bf16[4,3,32,128]{3,2,1,0:T(8,128)(2,1)S(1)}, u32[]{:S(2)}, u32[]{:S(2)}) collective-permute-start(bf16[4,3,32,128]{3,2,1,0:T(8,128)(2,1)S(1)} %get-tuple-element.5), channel_id=1, source_target_pairs={{1,0},{2,1},{3,2},{4,3},{5,4},{6,5},{7,6},{8,7},{9,8},{10,9},{11,1... | collective-permute-start | bytes 294920 | tf_op jit(solution)/shard_map/ppermute | solution.py:240
  145.4 0.0 collective-permute-start.10
  145.4 3.2 %collective-permute-start.9 = (bf16[4,3,32,128]{3,1,2,0:T(4,128)(2,1)S(1)}, bf16[4,3,32,128]{3,1,2,0:T(4,128)(2,1)S(1)}, u32[]{:S(2)}, u32[]{:S(2)}) collective-permute-start(bf16[4,3,32,128]{3,1,2,0:T(4,128)(2,1)S(1)} %get-tuple-element.7), channel_id=1, source_target_pairs={{16,0},{32,16},{48,32},{64,48},{80,64},{96,80},{112,96},{0,112},{1... | collective-permute-start | bytes 294920 | tf_op jit(solution)/shard_map/ppermute | solution.py:240
  148.7 0.0 collective-permute-start.8
  148.7 84.2 %depth.3.refs_2_ = f32[4,32,32,128]{3,2,1,0:T(8,128)} custom-call(f32[4,32,32,128]{3,2,1,0:T(8,128)} %cross.2.s_ref.refs_0_, f32[3,32,32,128]{3,2,1,0:T(8,128)} %refs_1_.3, f32[2,2,128]{2,1,0:T(2,128)} %reshape.52.band_ref, bf16[128,2048]{1,0:T(8,128)(2,1)} %bitcast.51, bf16[256,256]{1,0:T(8,128)(2,1)} %get-tuple-element.20.wmid_ref, ...), custom_call_target="tpu_custom_call" | custom-call | flops 34359738368 | bytes 6291456 | tf_op jit(solution)/shard_map/depth/pallas_call | solution.py:211
  232.9 0.0 collective-permute-done.9
  232.9 0.6 copy.34.refs_4_
  233.5 0.0 collective-permute-done.8
  233.5 0.7 copy.33.refs_3_
  234.2 0.0 collective-permute-done.11.refs_6_
  234.2 0.0 collective-permute-done.10.refs_5_
  234.2 0.6 copy-done.2
  234.8 0.6 copy-done.3
  235.4 22.8 %cross.3 = f32[4,32,32,128]{3,2,1,0:T(8,128)} custom-call(f32[4,32,32,128]{3,2,1,0:T(8,128)} %cross.2.s_ref.refs_0_, f32[3,32,32,128]{3,2,1,0:T(8,128)} %refs_1_.3, f32[4,32,32,128]{3,2,1,0:T(8,128)} %depth.3.refs_2_, bf16[4,3,32,128]{3,2,1,0:T(8,128)(2,1)} %copy.33.refs_3_, bf16[4,3,32,128]{3,2,1,0:T(8,128)(2,1)} %copy.34.refs_4_, ...), custom_call_target="tpu_custom_call" | custom-call | tf_op jit(solution)/shard_map/cross/pallas_call | solution.py:225
  (24 shorter events, 0.1 us)
Async XLA Ops:
  0.0 11.8 %copy-start = (f32[4,32,32,128]{3,2,1,0:T(8,128)S(1)}, f32[4,32,32,128]{3,2,1,0:T(8,128)}, u32[]{:S(2)}) copy-start(f32[4,32,32,128]{3,2,1,0:T(8,128)} %refs_11_.1) | copy-start | bytes 6291460
  2.5 111.6 %collective-permute-start.7 = (bf16[3,32,128]{2,1,0:T(8,128)(2,1)S(1)}, bf16[3,32,128]{2,1,0:T(8,128)(2,1)S(1)}, u32[]{:S(2)}, u32[]{:S(2)}) collective-permute-start(bf16[3,32,128]{2,1,0:T(8,128)(2,1)S(1)} %get-tuple-element.15), channel_id=1, source_target_pairs={{1,0},{2,1},{3,2},{4,3},{5,4},{6,5},{7,6},{8,7},{9,8},{10,9},{11,1... | collective-permute-start | bytes 73736 | tf_op jit(solution)/shard_map/ppermute | solution.py:240
  7.5 9.9 %copy-start.9 = (bf16[128,7]{0,1:T(8,128)(2,1)S(1)}, bf16[128,7]{0,1:T(8,128)(2,1)}, u32[]{:S(2)}) copy-start(bf16[128,7]{0,1:T(8,128)(2,1)} %param.10) | copy-start | bytes 5380
  7.5 10.0 %copy-start.7 = (bf16[128,128]{1,0:T(8,128)(2,1)S(1)}, bf16[128,128]{1,0:T(8,128)(2,1)}, u32[]{:S(2)}) copy-start(bf16[128,128]{1,0:T(8,128)(2,1)} %param.11) | copy-start | bytes 98308
  7.5 106.6 %collective-permute-start.6 = (bf16[3,32,128]{2,1,0:T(8,128)(2,1)S(1)}, bf16[3,32,128]{2,1,0:T(8,128)(2,1)S(1)}, u32[]{:S(2)}, u32[]{:S(2)}) collective-permute-start(bf16[3,32,128]{2,1,0:T(8,128)(2,1)S(1)} %get-tuple-element.16), channel_id=1, source_target_pairs={{0,1},{1,2},{2,3},{3,4},{4,5},{5,6},{6,7},{7,8},{8,9},{9,10},{10,1... | collective-permute-start | bytes 73736 | tf_op jit(solution)/shard_map/ppermute | solution.py:239
  7.5 14.4 %collective-permute-start.5 = (bf16[3,32,128]{2,0,1:T(4,128)(2,1)S(1)}, bf16[3,32,128]{2,0,1:T(4,128)(2,1)S(1)}, u32[]{:S(2)}, u32[]{:S(2)}) collective-permute-start(bf16[3,32,128]{2,0,1:T(4,128)(2,1)S(1)} %get-tuple-element.13), channel_id=1, source_target_pairs={{16,0},{32,16},{48,32},{64,48},{80,64},{96,80},{112,96},{0,112},{1... | collective-permute-start | bytes 73736 | tf_op jit(solution)/shard_map/ppermute | solution.py:240
  11.8 5.8 %copy-start.8 = (bf16[128,128]{1,0:T(8,128)(2,1)S(1)}, bf16[128,128]{1,0:T(8,128)(2,1)}, u32[]{:S(2)}) copy-start(bf16[128,128]{1,0:T(8,128)(2,1)} %param.12) | copy-start | bytes 98308
  11.8 6.0 %copy-start.11 = (bf16[4,128]{1,0:T(4,128)(2,1)S(1)}, bf16[4,128]{1,0:T(4,128)(2,1)}, u32[]{:S(2)}) copy-start(bf16[4,128]{1,0:T(4,128)(2,1)} %param.13) | copy-start | bytes 3076
  11.8 15.3 %collective-permute-start.4 = (bf16[3,32,128]{2,0,1:T(4,128)(2,1)S(1)}, bf16[3,32,128]{2,0,1:T(4,128)(2,1)S(1)}, u32[]{:S(2)}, u32[]{:S(2)}) collective-permute-start(bf16[3,32,128]{2,0,1:T(4,128)(2,1)S(1)} %get-tuple-element.14), channel_id=1, source_target_pairs={{0,16},{16,32},{32,48},{48,64},{64,80},{80,96},{96,112},{112,0},{1... | collective-permute-start | bytes 73736 | tf_op jit(solution)/shard_map/ppermute | solution.py:239
  13.0 6.0 %copy-start.10 = (s32[2,2,8]{2,1,0:T(2,128)S(1)}, s32[2,2,8]{2,1,0:T(2,128)}, u32[]{:S(2)}) copy-start(s32[2,2,8]{2,1,0:T(2,128)} %param.9) | copy-start | bytes 388
  13.1 14.0 %collective-permute-start.1 = (bf16[4,3,32,128]{3,1,2,0:T(4,128)(2,1)S(1)}, bf16[4,3,32,128]{3,1,2,0:T(4,128)(2,1)S(1)}, u32[]{:S(2)}, u32[]{:S(2)}) collective-permute-start(bf16[4,3,32,128]{3,1,2,0:T(4,128)(2,1)S(1)} %get-tuple-element.11), channel_id=1, source_target_pairs={{16,0},{32,16},{48,32},{64,48},{80,64},{96,80},{112,96},{0,112},{1... | collective-permute-start | bytes 294920 | tf_op jit(solution)/shard_map/ppermute | solution.py:240
  22.0 92.1 %collective-permute-start.3 = (bf16[4,3,32,128]{3,2,1,0:T(8,128)(2,1)S(1)}, bf16[4,3,32,128]{3,2,1,0:T(8,128)(2,1)S(1)}, u32[]{:S(2)}, u32[]{:S(2)}) collective-permute-start(bf16[4,3,32,128]{3,2,1,0:T(8,128)(2,1)S(1)} %get-tuple-element.9), channel_id=1, source_target_pairs={{1,0},{2,1},{3,2},{4,3},{5,4},{6,5},{7,6},{8,7},{9,8},{10,9},{11,1... | collective-permute-start | bytes 294920 | tf_op jit(solution)/shard_map/ppermute | solution.py:240
  27.1 87.0 %collective-permute-start.2 = (bf16[4,3,32,128]{3,2,1,0:T(8,128)(2,1)S(1)}, bf16[4,3,32,128]{3,2,1,0:T(8,128)(2,1)S(1)}, u32[]{:S(2)}, u32[]{:S(2)}) collective-permute-start(bf16[4,3,32,128]{3,2,1,0:T(8,128)(2,1)S(1)} %get-tuple-element.10), channel_id=1, source_target_pairs={{0,1},{1,2},{2,3},{3,4},{4,5},{5,6},{6,7},{7,8},{8,9},{9,10},{10,1... | collective-permute-start | bytes 294920 | tf_op jit(solution)/shard_map/ppermute | solution.py:239
  27.1 86.3 %collective-permute-start = (bf16[4,3,32,128]{3,1,2,0:T(4,128)(2,1)S(1)}, bf16[4,3,32,128]{3,1,2,0:T(4,128)(2,1)S(1)}, u32[]{:S(2)}, u32[]{:S(2)}) collective-permute-start(bf16[4,3,32,128]{3,1,2,0:T(4,128)(2,1)S(1)} %get-tuple-element.12), channel_id=1, source_target_pairs={{0,16},{16,32},{32,48},{48,64},{64,80},{80,96},{96,112},{112,0},{1... | collective-permute-start | bytes 294920 | tf_op jit(solution)/shard_map/ppermute | solution.py:239
  114.1 0.6 copy-start.5
  114.1 0.6 copy-start.6
  114.1 0.6 copy-start.1
  114.8 0.7 copy-start.4
  140.2 93.9 %collective-permute-start.11 = (bf16[4,3,32,128]{3,2,1,0:T(8,128)(2,1)S(1)}, bf16[4,3,32,128]{3,2,1,0:T(8,128)(2,1)S(1)}, u32[]{:S(2)}, u32[]{:S(2)}) collective-permute-start(bf16[4,3,32,128]{3,2,1,0:T(8,128)(2,1)S(1)} %get-tuple-element.5), channel_id=1, source_target_pairs={{1,0},{2,1},{3,2},{4,3},{5,4},{6,5},{7,6},{8,7},{9,8},{10,9},{11,1... | collective-permute-start | bytes 294920 | tf_op jit(solution)/shard_map/ppermute | solution.py:240
  145.4 88.8 %collective-permute-start.10 = (bf16[4,3,32,128]{3,2,1,0:T(8,128)(2,1)S(1)}, bf16[4,3,32,128]{3,2,1,0:T(8,128)(2,1)S(1)}, u32[]{:S(2)}, u32[]{:S(2)}) collective-permute-start(bf16[4,3,32,128]{3,2,1,0:T(8,128)(2,1)S(1)} %get-tuple-element.6), channel_id=1, source_target_pairs={{0,1},{1,2},{2,3},{3,4},{4,5},{5,6},{6,7},{7,8},{8,9},{9,10},{10,1... | collective-permute-start | bytes 294920 | tf_op jit(solution)/shard_map/ppermute | solution.py:239
  145.4 87.5 %collective-permute-start.9 = (bf16[4,3,32,128]{3,1,2,0:T(4,128)(2,1)S(1)}, bf16[4,3,32,128]{3,1,2,0:T(4,128)(2,1)S(1)}, u32[]{:S(2)}, u32[]{:S(2)}) collective-permute-start(bf16[4,3,32,128]{3,1,2,0:T(4,128)(2,1)S(1)} %get-tuple-element.7), channel_id=1, source_target_pairs={{16,0},{32,16},{48,32},{64,48},{80,64},{96,80},{112,96},{0,112},{1... | collective-permute-start | bytes 294920 | tf_op jit(solution)/shard_map/ppermute | solution.py:240
  148.7 84.9 %collective-permute-start.8 = (bf16[4,3,32,128]{3,1,2,0:T(4,128)(2,1)S(1)}, bf16[4,3,32,128]{3,1,2,0:T(4,128)(2,1)S(1)}, u32[]{:S(2)}, u32[]{:S(2)}) collective-permute-start(bf16[4,3,32,128]{3,1,2,0:T(4,128)(2,1)S(1)} %get-tuple-element.8), channel_id=1, source_target_pairs={{0,16},{16,32},{32,48},{48,64},{64,80},{80,96},{96,112},{112,0},{1... | collective-permute-start | bytes 294920 | tf_op jit(solution)/shard_map/ppermute | solution.py:239
  234.2 0.6 copy-start.2
  234.8 0.6 copy-start.3

commit v2 on v1

v2 whole, which is shorter than its diff:
```python
import functools

import jax
import jax.numpy as jnp
from jax import lax
from jax.experimental import pallas as pl
from jax.experimental.pallas import tpu as pltpu
from jax.sharding import PartitionSpec as P

BS = 16
EPS = 1e-06
STEP = 0.25
NV = 4
NF = 7
HID = 128
PAIRS = 16
CHUNK = 8
EARLY = 8
WENO_TYPE = jnp.float32
SILU_TYPE = jnp.bfloat16
VMEM_LIMIT = 60 * 1024 * 1024


def reciprocal(x):
    return pl.reciprocal(x, approx=True)


def curvature(d1, d2, d3, d4):
    one = lambda x: jnp.asarray(x, d1.dtype)
    g2 = one(0.609375) * (d2 * d2) + one(0.75 * EPS)
    g3 = one(0.609375) * (d3 * d3) + one(0.75 * EPS)
    e0 = d1 - one(1.375) * d2
    e1 = d2 - one(0.625) * d3
    e2 = d4 - one(1.375) * d3
    r0 = reciprocal(e0 * e0 + g2)
    r1 = reciprocal(e1 * e1 + g3)
    r2 = reciprocal(e2 * e2 + g3)
    s1 = d3 - d2
    t0 = s1 - (d2 - d1)
    t2 = (d4 - d3) - s1
    w0 = r0 * r0
    w2 = one(1.5) * (r2 * r2)
    total = one(0.5) * w0 + one(3.0) * (r1 * r1) + w2
    return (w0 * t0 + w2 * t2) * reciprocal(total)


def face_flux(fd, vd, alpha, centre):
    m = [alpha * d for d in vd]
    p = [(fd[j] + m[j]).astype(WENO_TYPE) for j in range(4)]
    q = [(fd[j] - m[j]).astype(WENO_TYPE) for j in range(1, 5)]
    bend = (curvature(*p) - curvature(*q[::-1])).astype(jnp.float32)
    rest = (fd[1] - fd[3]) + ((m[1] - m[2]) + (m[3] - m[2])) - bend
    return centre + rest * (1.0 / 6.0)


def sweep(n, load_v, load_u, emit):
    vs, us, fs, fds, vds = [], [], [], [], []
    previous = None
    for j in range(-3, n + 3):
        u, v = load_u(j), load_v(j)
        us.append(u)
        vs.append(v)
        fs.append(u * v)
        if len(vs) > 1:
            fds.append(fs[-1] - fs[-2])
            vds.append(vs[-1] - vs[-2])
        if len(fds) >= 5:
            alpha = jnp.maximum(jnp.abs(us[-4]), jnp.abs(us[-3]))
            flux = face_flux(fds[-5:], vds[-5:], alpha, fs[-4] + fs[-3])
            if previous is not None:
                emit(j - 3, flux - previous)
            previous = flux
        yield


def silu_half(h):
    h = h.astype(SILU_TYPE)
    return (h + h * jnp.tanh(h)).astype(jnp.bfloat16)


def closure_part(pair, planes, st_ref, vt_ref, weights, tot_ref):
    wsel_ref, wmid_ref, wdeep_ref, wout_ref = weights
    for lo in range(planes[0], planes[1], CHUNK):
        size = min(CHUNK, planes[1] - lo)
        rows = size * 128
        span = pl.ds(lo, size)
        lhs = jnp.concatenate([st_ref[span].reshape(rows, 128), vt_ref[span].reshape(rows, 128)], axis=1)
        h = silu_half(jnp.dot(lhs, wsel_ref[pair], preferred_element_type=jnp.float32))
        yield
        h = silu_half(jnp.dot(h, wmid_ref[...], preferred_element_type=jnp.float32))
        yield
        h = silu_half(jnp.dot(h, wdeep_ref[...], preferred_element_type=jnp.float32))
        yield
        out = jnp.dot(h, wout_ref[pair], preferred_element_type=jnp.float32)
        tot_ref[span] = tot_ref[span] + out.reshape(size, 128, 128)
        yield


def together(*parts):
    done = [0] * len(parts)
    while any(d < n for d, (_, n) in zip(done, parts)):
        i = min(range(len(parts)), key=lambda a: (done[a] + 0.5) / parts[a][1] if done[a] < parts[a][1] else 9.0)
        next(parts[i][0], None)
        done[i] += 1
    for gen, _ in parts:
        for _ in gen:
            pass


def depth_kernel(opening, *refs):
    if opening:
        s_ref, v_ref, band_ref, *weights = refs[:7]
        rt_ref, stb_ref, vtb_ref, ut_ref, st, tot = refs[7:]
    else:
        s_ref, vtb_ref, ut_ref, band_ref, *weights = refs[:8]
        rt_ref, stb_ref, st, tot = refs[8:]
    nx, ny = s_ref.shape[1], s_ref.shape[2]

    @pl.loop(0, nx, unroll=2)
    def _(x):
        t = jnp.concatenate([s_ref[k, x] for k in range(NV)], axis=0).T
        st[x] = t
        stb_ref[x] = t.astype(jnp.bfloat16)
        if opening:
            w = v_ref[2, x]
            vt = jnp.concatenate([v_ref[0, x], v_ref[1, x], w, jnp.zeros_like(w)], axis=0).T
            vtb_ref[x] = vt.astype(jnp.bfloat16)
            ut_ref[x] = jnp.concatenate([0.5 * w] * NV, axis=0).T

    @pl.loop(0, EARLY)
    def _(x):
        tot[x] = jnp.zeros((128, 128), jnp.float32)

    st2 = st.reshape(nx * 128, 128)
    ut2 = ut_ref.reshape(nx * 128, 128)
    rt2 = rt_ref.reshape(nx * 128, 128)

    @pl.loop(0, PAIRS)
    def _(step):
        x0 = (step // 4) * 8
        z0 = (step % 4) * 32

        def at(j):
            return pl.ds(x0 * 128 + ((z0 + j) & 127), 8, stride=128)

        def emit(j, value):
            rt2[at(j), :] = -value

        column = sweep(32, lambda j: st2[at(j), :], lambda j: ut2[at(j), :], emit)
        closure = closure_part(step, (0, EARLY), stb_ref, vtb_ref, weights, tot)
        together((closure, -(-EARLY // CHUNK) * 4), (column, 38))

    @pl.loop(0, EARLY)
    def _(x):
        rt_ref[x] = rt_ref[x] + jnp.where(band_ref[x // BS] > 0, tot[x], 0.0)


def cross_kernel(last, *refs):
    s_ref, v_ref, rt_ref, stb_ref, vtb_ref, band_ref, *weights = refs[:10]
    xlo, xhi, ylo, yhi, uxlo, uxhi, uylo, uyhi = refs[10:18]
    if last:
        old_ref, out_ref, dx, dy, tot = refs[18:]
    else:
        out_ref, *slabs = refs[18:23]
        dx, dy, tot = refs[23:]
    nx, ny = s_ref.shape[1], s_ref.shape[2]
    s2 = s_ref.reshape(NV * nx * ny, 128)
    v2 = v_ref.reshape(3 * nx * ny, 128)
    dy2 = dy.reshape(NV * nx * ny, 128)

    @pl.loop(EARLY, nx)
    def _(x):
        tot[x] = jnp.zeros((128, 128), jnp.float32)

    @pl.loop(0, PAIRS)
    def _(step):
        k = step // 4
        c0 = pl.multiple_of((step % 4) * 8, 8)
        cs = pl.ds(c0, 8)

        def wide(ref, *index):
            return ref[(*index, cs, slice(None))].astype(jnp.float32)

        def yv(j):
            if j < 0:
                return wide(ylo, k, j + 3)
            if j >= ny:
                return wide(yhi, k, j - ny)
            return s2[pl.ds((k * nx + c0) * ny + j, 8, stride=ny), :]

        def yu(j):
            if j < 0:
                return 0.5 * wide(uylo, j + 3)
            if j >= ny:
                return 0.5 * wide(uyhi, j - ny)
            return 0.5 * v2[pl.ds((nx + c0) * ny + j, 8, stride=ny), :]

        def yemit(j, value):
            dy2[pl.ds((k * nx + c0) * ny + j, 8, stride=ny), :] = value

        def xv(j):
            if j < 0:
                return wide(xlo, k, j + 3)
            if j >= nx:
                return wide(xhi, k, j - nx)
            return s_ref[k, j, cs, :]

        def xu(j):
            if j < 0:
                return 0.5 * wide(uxlo, j + 3)
            if j >= nx:
                return 0.5 * wide(uxhi, j - nx)
            return 0.5 * v_ref[0, j, cs, :]

        def xemit(j, value):
            dx[k, j, cs, :] = value

        closure = closure_part(step, (EARLY, nx), stb_ref, vtb_ref, weights, tot)
        together(
            (closure, -(-(nx - EARLY) // CHUNK) * 4),
            (sweep(ny, yv, yu, yemit), ny + 6),
            (sweep(nx, xv, xu, xemit), nx + 6),
        )

    def finish(x, rate_t):
        back = rate_t.T
        for k in range(NV):
            rate = back[k * ny : (k + 1) * ny] - (dx[k, x] + dy[k, x])
            stepped = s_ref[k, x] + STEP * rate
            if last:
                stepped = 0.75 * old_ref[k, x] + 0.25 * stepped
            out_ref[k, x] = stepped

    @pl.loop(0, EARLY)
    def _(x):
        finish(x, rt_ref[x])

    @pl.loop(EARLY, nx)
    def _(x):
        finish(x, rt_ref[x] + jnp.where(band_ref[x // BS] > 0, tot[x], 0.0))

    if not last:
        cut_slabs(out_ref, [(k, k) for k in range(NV)], *slabs)


def cut_slabs(ref, which, to_lo_x, to_hi_x, to_lo_y, to_hi_y):
    lead, nx, ny = ref.shape[:3]
    flat = ref.reshape(lead * nx * ny, 128)
    for src, dst in which:
        for j in range(3):
            to_lo_x[dst, j] = ref[src, j].astype(jnp.bfloat16)
            to_hi_x[dst, j] = ref[src, nx - 3 + j].astype(jnp.bfloat16)
            for target, y in ((to_lo_y, j), (to_hi_y, ny - 3 + j)):
                target[dst, j] = flat[pl.ds(src * nx * ny + y, nx, stride=ny), :].astype(jnp.bfloat16)


def slab_kernel(s_ref, v_ref, *slabs):
    cut_slabs(s_ref, [(k, k) for k in range(NV)], *slabs)
    nx, ny = v_ref.shape[1], v_ref.shape[2]
    flat = v_ref.reshape(3 * nx * ny, 128)
    for j in range(3):
        slabs[0][NV, j] = v_ref[0, j].astype(jnp.bfloat16)
        slabs[1][NV, j] = v_ref[0, nx - 3 + j].astype(jnp.bfloat16)
        slabs[2][NV, j] = flat[pl.ds(nx * ny + j, nx, stride=ny), :].astype(jnp.bfloat16)
        slabs[3][NV, j] = flat[pl.ds(nx * ny + ny - 3 + j, nx, stride=ny), :].astype(jnp.bfloat16)


VM = pl.BlockSpec(memory_space=pltpu.VMEM)
PARAMS = pltpu.CompilerParams(vmem_limit_bytes=VMEM_LIMIT)


def slab_shapes(count, n):
    return [jax.ShapeDtypeStruct((count, 3, n, 128), jnp.bfloat16)] * 4


def slab_call(state, velocity):
    n = state.shape[1]
    return pl.pallas_call(
        slab_kernel,
        out_shape=slab_shapes(NV + 1, n),
        in_specs=[VM] * 2,
        out_specs=[VM] * 4,
        compiler_params=PARAMS,
        name="slabs",
    )(state, velocity)


def depth_call(opening, state, extra, band, weights):
    n = state.shape[1]
    plane = lambda dtype: jax.ShapeDtypeStruct((n, 128, 128), dtype)
    shapes = [plane(jnp.float32), plane(jnp.bfloat16)]
    if opening:
        shapes += [plane(jnp.bfloat16), plane(jnp.float32)]
    args = (state, *extra, band, *weights)
    return pl.pallas_call(
        functools.partial(depth_kernel, opening),
        out_shape=shapes,
        in_specs=[VM] * len(args),
        out_specs=[VM] * len(shapes),
        scratch_shapes=[pltpu.VMEM((n, 128, 128), jnp.float32), pltpu.VMEM((EARLY, 128, 128), jnp.float32)],
        compiler_params=PARAMS,
        cost_estimate=pl.CostEstimate(flops=1 << 34, bytes_accessed=8 << 20, transcendentals=0),
        name="depth",
    )(*args)


def cross_call(state, velocity, parts, band, weights, halos, old):
    n = state.shape[1]
    last = old is not None
    args = (state, velocity, *parts, band, *weights, *halos) + ((old,) if last else ())
    shapes = [jax.ShapeDtypeStruct(state.shape, jnp.float32)]
    if not last:
        shapes += slab_shapes(NV, n)
    return pl.pallas_call(
        functools.partial(cross_kernel, last),
        out_shape=shapes,
        in_specs=[VM] * len(args),
        out_specs=[VM] * len(shapes),
        scratch_shapes=[pltpu.VMEM(state.shape, jnp.float32)] * 2 + [pltpu.VMEM((n, 128, 128), jnp.float32)],
        compiler_params=PARAMS,
        cost_estimate=pl.CostEstimate(flops=1 << 35, bytes_accessed=12 << 20, transcendentals=0),
        name="cross",
    )(*args)


def send(value, axis, up):
    n = lax.axis_size(axis)
    if up:
        return lax.ppermute(value, axis, [(i, (i + 1) % n) for i in range(n)])
    return lax.ppermute(value, axis, [((i + 1) % n, i) for i in range(n)])


def exchange(to_lo_x, to_hi_x, to_lo_y, to_hi_y):
    return [
        send(to_hi_x, "gx", True),
        send(to_lo_x, "gx", False),
        send(to_hi_y, "gy", True),
        send(to_lo_y, "gy", False),
    ]


def prepare(w_in, w_mid, w_deep, w_out, ny):
    half = jnp.asarray(0.5, jnp.bfloat16)
    zero = jnp.asarray(0.0, jnp.bfloat16)
    two = jnp.eye(2, dtype=jnp.bfloat16)
    wide = jnp.tile(jnp.pad(w_in.T * half, ((0, 1), (0, 0))), (1, 2))
    shape = (PAIRS, 8, ny, 2 * HID)
    row = 2 * lax.broadcasted_iota(jnp.int32, shape, 0) + lax.broadcasted_iota(jnp.int32, shape, 3) // HID
    hit = row == lax.broadcasted_iota(jnp.int32, shape, 2)
    wsel = jnp.where(hit, wide[None, :, None, :], zero).reshape(PAIRS, 8 * ny, 2 * HID)
    wmid = jnp.kron(two, w_mid.T * half)
    wdeep = jnp.kron(two, w_deep.T * half)
    shape = (PAIRS, 2 * HID, NV * ny)
    row = 2 * lax.broadcasted_iota(jnp.int32, shape, 0) + lax.broadcasted_iota(jnp.int32, shape, 1) // HID
    hit = row == lax.broadcasted_iota(jnp.int32, shape, 2) % ny
    wout = jnp.where(hit, jnp.tile(jnp.repeat(w_out.T, ny, axis=1), (2, 1))[None], zero)
    return wsel, wmid, wdeep, wout


def shards(state, velocity, routes, w_in, w_mid, w_deep, w_out):
    ny = state.shape[2]
    cut = slab_call(state, velocity)
    halos = exchange(*cut)
    speeds = [h[NV] for h in halos]
    weights = prepare(w_in, w_mid, w_deep, w_out, ny)
    member = (routes >= 0).astype(jnp.float32)
    band = jnp.repeat(member.transpose(0, 2, 1), BS, axis=1)
    band = jnp.tile(jnp.repeat(band, BS, axis=2), (1, 1, NV))

    rt, stb, vtb, ut = depth_call(True, state, (velocity,), band, weights)
    first, *cut = cross_call(state, velocity, (rt, stb, vtb), band, weights, halos + speeds, None)
    halos = exchange(*cut)
    rt, stb = depth_call(False, first, (vtb, ut), band, weights)
    return cross_call(first, velocity, (rt, stb, vtb), band, weights, halos + speeds, state)[0]


def solution(mesh):
    placed = (
        P(None, "gx", "gy", None),
        P(None, "gx", "gy", None),
        P("gx", "gy", None),
        P(),
        P(),
        P(),
        P(),
    )
    return jax.shard_map(
        shards, mesh=mesh, in_specs=placed, out_specs=P(None, "gx", "gy", None), check_vma=False
    )
```

time: 259 us -> 199 us (0.77)
  Pallas kernels: 213 us -> 169 us
  local copies, waits for them, and re-layouts: 17.2 us -> 5.48 us
  starting transfers between devices: 27.2 us -> 20 us
  other arithmetic: 0.51 us -> 3.9 us
    pallas_call x4 -> x5, Pallas kernels: 213 us -> 169 us  [the longest x2 110 us: cross_call(): pl.pallas_call(functools.partial(cross_kernel, last), out_shape=shapes, i...]
    ppermute x6 -> x4, starting transfers between devices: 26.9 us -> 18 us  [send(): return lax.ppermute(value, axis, [((i + 1) % n, i) for i in range(n)])]
    unnamed x28 -> x26, local copies, waits for them, and re-layouts: 7.27 us -> 0.74 us
    ppermute x6 -> x0, local copies, waits for them, and re-layouts: 3.8 us -> none  [the longest x3 1.9 us: send(): return lax.ppermute(value, axis, [(i, (i + 1) % n) for i in range(n)])]
    select_n x0 -> x2, other arithmetic: none -> 3.59 us  [the longest x1 1.93 us: prepare(): jnp.where(hit, wide[None, :, None, :], zero).reshape(PAIRS, 8 * ny, 2 * HID)]
    pallas_call x1 -> x0, local copies, waits for them, and re-layouts: 2.81 us -> none  [cross_call(): pl.pallas_call(functools.partial(cross_kernel, last), out_shape=jax.Shape...]
    squeeze x0 -> x4, local copies, waits for them, and re-layouts: none -> 2.64 us  [shards(): speeds = [h[NV] for h in halos]]
  transfers between devices with their start and end apart: 12 -> 8, of which waited for: 0 -> 0; matrix products, arithmetic and copies ran while one was open for 4% -> 4% of each run, Pallas kernels for 65% -> 28%
where the time goes in v2:
time: 199 us
  Pallas kernels  169 us (85%)
  starting transfers between devices  20 us (10%)
  local copies, waits for them, and re-layouts  5.48 us (3%)
  other arithmetic  3.9 us (2%)
    pallas_call x2, Pallas kernels, cross_call(): pl.pallas_call(functools.partial(cross_kernel, last), out_shape=shapes, i...  110 us
    pallas_call x2, Pallas kernels, depth_call(): pl.pallas_call(functools.partial(depth_kernel, opening), out_shape=shapes...  56.2 us
    ppermute x4, starting transfers between devices, send(): return lax.ppermute(value, axis, [((i + 1) % n, i) for i in range(n)])  18 us
  transfers between devices with their start and end apart: 8, of which 0 were waited for; matrix products, arithmetic and copies ran while one was open for 4% of the time, Pallas kernels for 28%

profile of v2, /device:TPU:0, one launch (start us, length us, event | category | flops | bytes accessed | tf_op | source)
XLA Modules:
  0.0 199.1 jit_solution(2627990624377608205)
XLA Ops:
  0.0 0.0 copy-start.6
  0.0 0.0 copy-start.7
  0.0 0.0 copy-start
  0.0 0.0 copy-start.1
  0.0 0.0 copy-start.8
  0.0 3.2 %slabs.1 = (bf16[5,3,32,128]{3,2,1,0:T(8,128)(2,1)}, bf16[5,3,32,128]{3,2,1,0:T(8,128)(2,1)}, bf16[5,3,32,128]{3,2,1,0:T(8,128)(2,1)}, bf16[5,3,32,128]{3,2,1,0:T(8,128)(2,1)}) custom-call(f32[4,32,32,128]{3,2,1,0:T(8,128)} %refs_18_.1, f32[3,32,32,128]{3,2,1,0:T(8,128)} %refs_1_.5), custom_call_target="tpu_custom_call" | custom-call | tf_op jit(solution)/shard_map/slabs/pallas_call | solution.py:278
  3.2 2.0 %collective-permute-start = (bf16[5,3,32,128]{3,2,1,0:T(8,128)(2,1)}, bf16[5,3,32,128]{3,2,1,0:T(8,128)(2,1)S(1)}, u32[]{:S(2)}, u32[]{:S(2)}) collective-permute-start(bf16[5,3,32,128]{3,2,1,0:T(8,128)(2,1)} %get-tuple-element.23), channel_id=1, source_target_pairs={{0,16},{16,32},{32,48},{48,64},{64,80},{80,96},{96,112},{112,0},{1... | collective-permute-start | bytes 368648 | tf_op jit(solution)/shard_map/ppermute | solution.py:329
  5.2 3.1 %collective-permute-start.1 = (bf16[5,3,32,128]{3,2,1,0:T(8,128)(2,1)}, bf16[5,3,32,128]{3,2,1,0:T(8,128)(2,1)S(1)}, u32[]{:S(2)}, u32[]{:S(2)}) collective-permute-start(bf16[5,3,32,128]{3,2,1,0:T(8,128)(2,1)} %get-tuple-element.24), channel_id=1, source_target_pairs={{16,0},{32,16},{48,32},{64,48},{80,64},{96,80},{112,96},{0,112},{1... | collective-permute-start | bytes 368648 | tf_op jit(solution)/shard_map/ppermute | solution.py:330
  8.3 0.0 collective-permute-start.2
  8.3 5.4 %collective-permute-start.3 = (bf16[5,3,32,128]{3,2,1,0:T(8,128)(2,1)}, bf16[5,3,32,128]{3,2,1,0:T(8,128)(2,1)S(1)}, u32[]{:S(2)}, u32[]{:S(2)}) collective-permute-start(bf16[5,3,32,128]{3,2,1,0:T(8,128)(2,1)} %get-tuple-element.26), channel_id=1, source_target_pairs={{1,0},{2,1},{3,2},{4,3},{5,4},{6,5},{7,6},{8,7},{9,8},{10,9},{11,1... | collective-permute-start | bytes 368648 | tf_op jit(solution)/shard_map/ppermute | solution.py:330
  13.7 0.0 copy-done.6
  13.7 0.0 copy-done.7
  13.8 0.1 iota.78
  13.9 0.1 broadcast_in_dim.43
  13.9 0.1 reshape.41
  14.0 0.0 copy-done
  14.0 0.1 copy.12
  14.2 0.0 copy-done.1
  14.2 0.1 copy.13
  14.3 0.0 copy-done.8
  14.3 0.1 copy.14
  14.5 0.8 copy.15.refs_2_.refs_5_.refs_3_
  15.2 0.3 broadcast_multiply_fusion
  15.5 0.7 copy_bitcast_fusion
  16.2 1.9 fusion.refs_3_.refs_6_.refs_4_
  18.2 1.7 fusion.1.refs_6_.refs_9_.refs_7_
  19.8 28.9 %depth.2 = (f32[32,128,128]{2,1,0:T(8,128)}, bf16[32,128,128]{2,1,0:T(8,128)(2,1)}, bf16[32,128,128]{2,1,0:T(8,128)(2,1)}, f32[32,128,128]{2,1,0:T(8,128)}) custom-call(f32[4,32,32,128]{3,2,1,0:T(8,128)} %refs_18_.1, f32[3,32,32,128]{3,2,1,0:T(8,128)} %refs_1_.5, f32[2,128,128]{2,1,0:T(8,128)} %copy.15.refs_2_.refs_5_.refs_3_, ...), custom_call_target="tpu_custom_call" | custom-call | flops 17179869184 | bytes 8388608 | tf_op jit(solution)/shard_map/depth/pallas_call | solution.py:295
  48.7 0.0 collective-permute-done.refs_10_
  48.7 0.0 copy-start.2
  48.8 0.7 slice_bitcast_fusion.3.refs_14_
  49.4 0.0 collective-permute-done.1.refs_11_
  49.4 0.0 copy-start.3
  49.4 0.6 slice_bitcast_fusion.2.refs_15_
  50.1 0.0 collective-permute-done.2.refs_12_
  50.1 0.0 copy-start.4
  50.1 0.7 slice_bitcast_fusion.1.refs_16_
  50.8 0.0 collective-permute-done.3.refs_13_
  50.8 0.0 copy-start.5
  50.8 0.7 slice_bitcast_fusion.refs_17_
  51.4 0.0 copy-done.2
  51.4 0.0 copy-done.3
  51.4 0.0 copy-done.4
  51.4 0.0 copy-done.5
  51.4 54.8 %cross.2 = (f32[4,32,32,128]{3,2,1,0:T(8,128)}, bf16[4,3,32,128]{3,2,1,0:T(8,128)(2,1)}, bf16[4,3,32,128]{3,2,1,0:T(8,128)(2,1)}, bf16[4,3,32,128]{3,2,1,0:T(8,128)(2,1)}, bf16[4,3,32,128]{3,2,1,0:T(8,128)(2,1)}) custom-call(f32[4,32,32,128]{3,2,1,0:T(8,128)} %refs_18_.1, f32[3,32,32,128]{3,2,1,0:T(8,128)} %refs_1_.5, ...), custom_call_target="tpu_custom_call" | custom-call | flops 34359738368 | bytes 12582912 | tf_op jit(solution)/shard_map/cross/pallas_call | solution.py:314
  106.3 0.0 collective-permute-start.4
  106.3 4.1 %collective-permute-start.5 = (bf16[4,3,32,128]{3,2,1,0:T(8,128)(2,1)}, bf16[4,3,32,128]{3,2,1,0:T(8,128)(2,1)S(1)}, u32[]{:S(2)}, u32[]{:S(2)}) collective-permute-start(bf16[4,3,32,128]{3,2,1,0:T(8,128)(2,1)} %get-tuple-element.32), channel_id=1, source_target_pairs={{16,0},{32,16},{48,32},{64,48},{80,64},{96,80},{112,96},{0,112},{1... | collective-permute-start | bytes 294920 | tf_op jit(solution)/shard_map/ppermute | solution.py:330
  110.4 0.0 collective-permute-start.6
  110.5 5.4 %collective-permute-start.7 = (bf16[4,3,32,128]{3,2,1,0:T(8,128)(2,1)}, bf16[4,3,32,128]{3,2,1,0:T(8,128)(2,1)S(1)}, u32[]{:S(2)}, u32[]{:S(2)}) collective-permute-start(bf16[4,3,32,128]{3,2,1,0:T(8,128)(2,1)} %get-tuple-element.34), channel_id=1, source_target_pairs={{1,0},{2,1},{3,2},{4,3},{5,4},{6,5},{7,6},{8,7},{9,8},{10,9},{11,1... | collective-permute-start | bytes 294920 | tf_op jit(solution)/shard_map/ppermute | solution.py:330
  115.8 27.2 %depth.3 = (f32[32,128,128]{2,1,0:T(8,128)}, bf16[32,128,128]{2,1,0:T(8,128)(2,1)}) custom-call(f32[4,32,32,128]{3,2,1,0:T(8,128)} %get-tuple-element.27.refs_0_, bf16[32,128,128]{2,1,0:T(8,128)(2,1)} %get-tuple-element.22.refs_4_.refs_1_, f32[32,128,128]{2,1,0:T(8,128)} %get-tuple-element.28.refs_2_, f32[2,128,128]{2,1,0:T(8,128)} %copy.15.refs_2_.refs_5_.refs_3_, ...), custom_call_target="tpu_custom_call" | custom-call | flops 17179869184 | bytes 8388608 | tf_op jit(solution)/shard_map/depth/pallas_call | solution.py:295
  143.1 0.0 collective-permute-done.4.refs_10_
  143.1 0.0 copy-start.9
  143.1 0.0 collective-permute-done.5.refs_11_
  143.1 0.0 copy-start.10
  143.1 0.0 collective-permute-done.6.refs_12_
  143.1 0.0 copy-start.11
  143.1 0.0 collective-permute-done.7.refs_13_
  143.1 0.0 copy-start.12
  143.1 0.6 copy-done.9
  143.7 0.1 copy-done.10
  143.8 0.0 copy-done.11
  143.8 0.0 copy-done.12
  143.8 55.3 %cross.3 = f32[4,32,32,128]{3,2,1,0:T(8,128)} custom-call(f32[4,32,32,128]{3,2,1,0:T(8,128)} %get-tuple-element.27.refs_0_, f32[3,32,32,128]{3,2,1,0:T(8,128)} %refs_1_.5, f32[32,128,128]{2,1,0:T(8,128)} %get-tuple-element.29.refs_2_, bf16[32,128,128]{2,1,0:T(8,128)(2,1)} %get-tuple-element.30.refs_3_, ...), custom_call_target="tpu_custom_call" | custom-call | flops 34359738368 | bytes 12582912 | tf_op jit(solution)/shard_map/cross/pallas_call | solution.py:314
  (18 shorter events, 0.1 us)
Async XLA Ops:
  0.0 13.7 %copy-start.6 = (s32[2,2,8]{2,1,0:T(2,128)S(1)}, s32[2,2,8]{2,1,0:T(2,128)}, u32[]{:S(2)}) copy-start(s32[2,2,8]{2,1,0:T(2,128)} %param.9) | copy-start | bytes 388
  0.0 13.7 %copy-start.7 = (bf16[128,7]{0,1:T(8,128)(2,1)S(1)}, bf16[128,7]{0,1:T(8,128)(2,1)}, u32[]{:S(2)}) copy-start(bf16[128,7]{0,1:T(8,128)(2,1)} %param.10) | copy-start | bytes 5380
  0.0 14.0 %copy-start = (bf16[128,128]{1,0:T(8,128)(2,1)S(1)}, bf16[128,128]{1,0:T(8,128)(2,1)}, u32[]{:S(2)}) copy-start(bf16[128,128]{1,0:T(8,128)(2,1)} %param.11) | copy-start | bytes 98308
  0.0 14.2 %copy-start.1 = (bf16[128,128]{1,0:T(8,128)(2,1)S(1)}, bf16[128,128]{1,0:T(8,128)(2,1)}, u32[]{:S(2)}) copy-start(bf16[128,128]{1,0:T(8,128)(2,1)} %param.12) | copy-start | bytes 98308
  0.0 14.3 %copy-start.8 = (bf16[4,128]{1,0:T(4,128)(2,1)S(1)}, bf16[4,128]{1,0:T(4,128)(2,1)}, u32[]{:S(2)}) copy-start(bf16[4,128]{1,0:T(4,128)(2,1)} %param.13) | copy-start | bytes 3076
  3.2 45.6 %collective-permute-start = (bf16[5,3,32,128]{3,2,1,0:T(8,128)(2,1)}, bf16[5,3,32,128]{3,2,1,0:T(8,128)(2,1)S(1)}, u32[]{:S(2)}, u32[]{:S(2)}) collective-permute-start(bf16[5,3,32,128]{3,2,1,0:T(8,128)(2,1)} %get-tuple-element.23), channel_id=1, source_target_pairs={{0,16},{16,32},{32,48},{48,64},{64,80},{80,96},{96,112},{112,0},{1... | collective-permute-start | bytes 368648 | tf_op jit(solution)/shard_map/ppermute | solution.py:329
  5.2 44.3 %collective-permute-start.1 = (bf16[5,3,32,128]{3,2,1,0:T(8,128)(2,1)}, bf16[5,3,32,128]{3,2,1,0:T(8,128)(2,1)S(1)}, u32[]{:S(2)}, u32[]{:S(2)}) collective-permute-start(bf16[5,3,32,128]{3,2,1,0:T(8,128)(2,1)} %get-tuple-element.24), channel_id=1, source_target_pairs={{16,0},{32,16},{48,32},{64,48},{80,64},{96,80},{112,96},{0,112},{1... | collective-permute-start | bytes 368648 | tf_op jit(solution)/shard_map/ppermute | solution.py:330
  8.3 41.8 %collective-permute-start.2 = (bf16[5,3,32,128]{3,2,1,0:T(8,128)(2,1)}, bf16[5,3,32,128]{3,2,1,0:T(8,128)(2,1)S(1)}, u32[]{:S(2)}, u32[]{:S(2)}) collective-permute-start(bf16[5,3,32,128]{3,2,1,0:T(8,128)(2,1)} %get-tuple-element.25), channel_id=1, source_target_pairs={{0,1},{1,2},{2,3},{3,4},{4,5},{5,6},{6,7},{7,8},{8,9},{9,10},{10,1... | collective-permute-start | bytes 368648 | tf_op jit(solution)/shard_map/ppermute | solution.py:329
  8.3 42.4 %collective-permute-start.3 = (bf16[5,3,32,128]{3,2,1,0:T(8,128)(2,1)}, bf16[5,3,32,128]{3,2,1,0:T(8,128)(2,1)S(1)}, u32[]{:S(2)}, u32[]{:S(2)}) collective-permute-start(bf16[5,3,32,128]{3,2,1,0:T(8,128)(2,1)} %get-tuple-element.26), channel_id=1, source_target_pairs={{1,0},{2,1},{3,2},{4,3},{5,4},{6,5},{7,6},{8,7},{9,8},{10,9},{11,1... | collective-permute-start | bytes 368648 | tf_op jit(solution)/shard_map/ppermute | solution.py:330
  48.7 2.7 %copy-start.2 = (bf16[5,3,32,128]{3,2,1,0:T(8,128)(2,1)}, bf16[5,3,32,128]{3,2,1,0:T(8,128)(2,1)S(1)}, u32[]{:S(2)}) copy-start(bf16[5,3,32,128]{3,2,1,0:T(8,128)(2,1)S(1)} %collective-permute-done.refs_10_) | copy-start | bytes 368644
  49.4 2.0 %copy-start.3 = (bf16[5,3,32,128]{3,2,1,0:T(8,128)(2,1)}, bf16[5,3,32,128]{3,2,1,0:T(8,128)(2,1)S(1)}, u32[]{:S(2)}) copy-start(bf16[5,3,32,128]{3,2,1,0:T(8,128)(2,1)S(1)} %collective-permute-done.1.refs_11_) | copy-start | bytes 368644
  50.1 1.3 copy-start.4
  50.8 0.7 copy-start.5
  106.3 36.8 %collective-permute-start.4 = (bf16[4,3,32,128]{3,2,1,0:T(8,128)(2,1)}, bf16[4,3,32,128]{3,2,1,0:T(8,128)(2,1)S(1)}, u32[]{:S(2)}, u32[]{:S(2)}) collective-permute-start(bf16[4,3,32,128]{3,2,1,0:T(8,128)(2,1)} %get-tuple-element.31), channel_id=1, source_target_pairs={{0,16},{16,32},{32,48},{48,64},{64,80},{80,96},{96,112},{112,0},{1... | collective-permute-start | bytes 294920 | tf_op jit(solution)/shard_map/ppermute | solution.py:329
  106.3 36.7 %collective-permute-start.5 = (bf16[4,3,32,128]{3,2,1,0:T(8,128)(2,1)}, bf16[4,3,32,128]{3,2,1,0:T(8,128)(2,1)S(1)}, u32[]{:S(2)}, u32[]{:S(2)}) collective-permute-start(bf16[4,3,32,128]{3,2,1,0:T(8,128)(2,1)} %get-tuple-element.32), channel_id=1, source_target_pairs={{16,0},{32,16},{48,32},{64,48},{80,64},{96,80},{112,96},{0,112},{1... | collective-permute-start | bytes 294920 | tf_op jit(solution)/shard_map/ppermute | solution.py:330
  110.4 32.6 %collective-permute-start.6 = (bf16[4,3,32,128]{3,2,1,0:T(8,128)(2,1)}, bf16[4,3,32,128]{3,2,1,0:T(8,128)(2,1)S(1)}, u32[]{:S(2)}, u32[]{:S(2)}) collective-permute-start(bf16[4,3,32,128]{3,2,1,0:T(8,128)(2,1)} %get-tuple-element.33), channel_id=1, source_target_pairs={{0,1},{1,2},{2,3},{3,4},{4,5},{5,6},{6,7},{7,8},{8,9},{9,10},{10,1... | collective-permute-start | bytes 294920 | tf_op jit(solution)/shard_map/ppermute | solution.py:329
  110.5 32.7 %collective-permute-start.7 = (bf16[4,3,32,128]{3,2,1,0:T(8,128)(2,1)}, bf16[4,3,32,128]{3,2,1,0:T(8,128)(2,1)S(1)}, u32[]{:S(2)}, u32[]{:S(2)}) collective-permute-start(bf16[4,3,32,128]{3,2,1,0:T(8,128)(2,1)} %get-tuple-element.34), channel_id=1, source_target_pairs={{1,0},{2,1},{3,2},{4,3},{5,4},{6,5},{7,6},{8,7},{9,8},{10,9},{11,1... | collective-permute-start | bytes 294920 | tf_op jit(solution)/shard_map/ppermute | solution.py:330
  143.1 0.7 copy-start.9
  143.1 0.7 copy-start.10
  143.1 0.7 copy-start.11
  143.1 0.7 copy-start.12

commit v3 on v2

v3 whole, which is shorter than its diff:
```python
import functools

import jax
import jax.numpy as jnp
from jax import lax
from jax.experimental import pallas as pl
from jax.experimental.pallas import tpu as pltpu
from jax.sharding import PartitionSpec as P

BS = 16
EPS = 1e-06
STEP = 0.25
NV = 4
NF = 7
HID = 128
PAIRS = 16
DEPTH_SIZE = 4
CROSS_SIZE = 8
EARLY = 8
WENO_TYPE = jnp.bfloat16
SILU_TYPE = jnp.bfloat16
TILE = 16
VMEM_LIMIT = 60 * 1024 * 1024


def reciprocal(x):
    return pl.reciprocal(x, approx=True)


def curvature(d1, d2, d3, d4):
    one = lambda x: jnp.asarray(x, d1.dtype)
    g2 = one(0.609375) * (d2 * d2) + one(0.75 * EPS)
    g3 = one(0.609375) * (d3 * d3) + one(0.75 * EPS)
    e0 = d1 - one(1.375) * d2
    e1 = d3 - one(0.625) * d2
    e2 = d4 - one(1.375) * d3
    r0 = reciprocal(e0 * e0 + g2)
    r1 = reciprocal(e1 * e1 + g2)
    r2 = reciprocal(e2 * e2 + g3)
    t0 = e0 + e1
    t2 = e2 + (d2 - one(0.625) * d3)
    w0 = r0 * r0
    w2 = one(1.5) * (r2 * r2)
    total = one(0.5) * w0 + one(3.0) * (r1 * r1) + w2
    return (w0 * t0 + w2 * t2) * reciprocal(total)


def face_flux(fd, vd, second, alpha, centre):
    rough = alpha.astype(WENO_TYPE)
    m = [rough * d for d in vd]
    p = [fd[j] + m[j] for j in range(4)]
    q = [fd[j] - m[j] for j in range(1, 5)]
    bend = (curvature(*p) - curvature(*q[::-1])).astype(jnp.float32)
    before, after, v_before, v_after = second
    rest = (before - after) + alpha * (v_after - v_before) - bend
    return centre + rest * (1.0 / 6.0)


class Sweep:
    def __init__(self, n, load_v, load_u, emit):
        self.last, self.load_v, self.load_u, self.emit = n + 3, load_v, load_u, emit

    def points(self):
        return range(-3, self.last)

    def advance(self, state, j):
        us, fs, vs, fds, vds, frough, vrough, vseconds, before = state
        u, v = self.load_u(j), self.load_v(j)
        f = u * v
        if vs:
            fds = fds + [f - fs[-1]]
            vds = vds + [v - vs[-1]]
            frough = frough + [fds[-1].astype(WENO_TYPE)]
            vrough = vrough + [vds[-1].astype(WENO_TYPE)]
        if len(vds) > 1:
            vseconds = vseconds + [vds[-1] - vds[-2]]
        us, fs = us + [u], fs + [f]
        if len(frough) == 5:
            alpha = jnp.maximum(jnp.abs(us[0]), jnp.abs(us[1]))
            second = (fds[-4], fds[-2], vseconds[-3], vseconds[-2])
            flux = face_flux(frough, vrough, second, alpha, fs[0] + fs[1])
            if before:
                self.emit(j - 3, flux - before[0])
            before = [flux]
        return us[-3:], fs[-3:], [v], fds[-4:], vds[-1:], frough[-4:], vrough[-4:], vseconds[-3:], before


def silu_half(h):
    h = h.astype(SILU_TYPE)
    return (h + h * jnp.tanh(h)).astype(jnp.bfloat16)


def closure_part(pair, planes, size, st_ref, vt_ref, weights, tot_ref, hidden, keys, accs):
    wsel_ref, wmid_ref, wdeep_ref, wout_ref = weights
    chunks = (planes[1] - planes[0]) // size
    half = size * 64
    zero = jnp.zeros((2 * HID, 2 * HID), jnp.float32)
    layers = (
        lambda: jnp.where(keys[0] == 2 * pair, wsel_ref[...], zero).astype(jnp.bfloat16),
        lambda: wmid_ref[...],
        lambda: wdeep_ref[...],
        lambda: jnp.concatenate(
            [jnp.where(keys[1][:, :128] == 2 * pair, wout_ref[...], zero[:, :128]), zero[:, 128:]], axis=1
        ).astype(jnp.bfloat16),
    )
    waiting = None

    def push(layer):
        for m in range(2):
            pltpu.matmul_push_rhs(layers[layer](), layer % 2, m)

    def take(layer, c, r):
        for m in range(2):
            sums = pltpu.matmul_pop(accs[2 * m + r])
            if layer < 3:
                hidden[c, pl.ds(m * half, half), :] = silu_half(sums)
            else:
                span = pl.ds(planes[0] + c * size + m * size // 2, size // 2)
                tot_ref[span] = tot_ref[span] + sums[:, :128].reshape(size // 2, 128, 128)

    push(0)
    for layer in range(4):
        for c in range(chunks):
            r = (layer * chunks + c) % 2
            for m in range(2):
                if layer == 0:
                    span = pl.ds(planes[0] + c * size + m * size // 2, size // 2)
                    lhs = jnp.concatenate([st_ref[span].reshape(half, 128), vt_ref[span].reshape(half, 128)], axis=1)
                else:
                    lhs = hidden[c, pl.ds(m * half, half), :]
                pltpu.matmul_acc_lhs(accs[2 * m + r], lhs, layer % 2 if c == 0 else None)
            if c == 0 and layer < 3:
                push(layer + 1)
            if waiting is not None:
                take(*waiting)
            waiting = (layer, c, r)
            yield
    take(*waiting)
    yield


def together(closure, steps, sweeps):
    work = [(sweep, j) for sweep in sweeps for j in sweep.points()]
    costs = [1.0 if j > 1 else 0.15 for _, j in work]
    total, spent, at = sum(costs), 0.0, 0
    state, owner = None, None
    for i in range(steps):
        next(closure, None)
        while at < len(work) and (i == steps - 1 or spent + costs[at] / 2 < total * (i + 1) / steps):
            sweep, j = work[at]
            if sweep is not owner:
                state, owner = ([],) * 9, sweep
            state = sweep.advance(state, j)
            spent += costs[at]
            at += 1


def depth_kernel(opening, *refs):
    if opening:
        s_ref, v_ref, band_ref, *weights = refs[:7]
        rt_ref, stb_ref, vtb_ref, ut_ref, st, tot, hidden, keys = refs[7:]
    else:
        s_ref, vtb_ref, ut_ref, band_ref, *weights = refs[:8]
        rt_ref, stb_ref, st, tot, hidden, keys = refs[8:]
    nx, ny = s_ref.shape[1], s_ref.shape[2]

    @pl.loop(0, nx, unroll=4)
    def _(x):
        t = jnp.concatenate([s_ref[k, x] for k in range(NV)], axis=0).T
        st[x] = t
        stb_ref[x] = t.astype(jnp.bfloat16)
        if opening:
            w = v_ref[2, x]
            vt = jnp.concatenate([v_ref[0, x], v_ref[1, x], w, jnp.zeros_like(w)], axis=0).T
            vtb_ref[x] = vt.astype(jnp.bfloat16)
            ut_ref[x] = jnp.concatenate([0.5 * w] * NV, axis=0).T

    @pl.loop(0, EARLY, unroll=4)
    def _(x):
        tot[x] = jnp.zeros((128, 128), jnp.float32)

    st2 = st.reshape(nx * 128, 128)
    ut2 = ut_ref.reshape(nx * 128, 128)
    rt2 = rt_ref.reshape(nx * 128, 128)

    set_keys(keys)

    def main(*accs):
        @pl.loop(0, PAIRS)
        def _(step):
            x0 = (step // 8) * TILE
            z0 = (step % 8) * 16

            def at(j):
                return pl.ds(x0 * 128 + ((z0 + j) & 127), TILE, stride=128)

            def emit(j, value):
                rt2[at(j), :] = -value

            column = Sweep(16, lambda j: st2[at(j), :], lambda j: ut2[at(j), :], emit)
            closure = closure_part(step, (0, EARLY), DEPTH_SIZE, stb_ref, vtb_ref, weights, tot, hidden, keys, accs)
            together(closure, EARLY // DEPTH_SIZE * 4 + 1, (column,))

    with_sums(DEPTH_SIZE, main)

    @pl.loop(0, EARLY, unroll=4)
    def _(x):
        rt_ref[x] = rt_ref[x] + jnp.where(band_ref[x // BS] > 0, tot[x], 0.0)


def cross_kernel(last, *refs):
    s_ref, v_ref, rt_hbm, stb_ref, vtb_ref, band_ref, *weights = refs[:10]
    xlo, xhi, ylo, yhi = refs[10:14]
    rest = refs[14:] if not last else refs[18:]
    uxlo, uxhi, uylo, uyhi = (r.at[NV] for r in (refs[10:14] if not last else refs[14:18]))
    if last:
        old_hbm, out_hbm, dx, dy, tot, hidden, keys, rt_ref, out_ref, sems, old_ref = rest
    else:
        out_hbm, *slabs = rest[:5]
        dx, dy, tot, hidden, keys, rt_ref, out_ref, sems = rest[5:]
    nx, ny = s_ref.shape[1], s_ref.shape[2]
    s2 = s_ref.reshape(NV * nx * ny, 128)
    v2 = v_ref.reshape(3 * nx * ny, 128)
    dy2 = dy.reshape(NV * nx * ny, 128)
    coming = [pltpu.make_async_copy(rt_hbm, rt_ref, sems.at[0])]
    if last:
        coming.append(pltpu.make_async_copy(old_hbm, old_ref, sems.at[1]))
    for copy in coming:
        copy.start()

    @pl.loop(EARLY, nx, unroll=4)
    def _(x):
        tot[x] = jnp.zeros((128, 128), jnp.float32)

    set_keys(keys)

    def main(*accs):
        @pl.loop(0, PAIRS)
        def _(step):
            k = step // 4
            c0 = pl.multiple_of((step // 2 % 2) * TILE, TILE)
            cs = pl.ds(c0, TILE)
            base = (step % 2) * 16

            def wide(ref, *index):
                return ref[(*index, cs, slice(None))].astype(jnp.float32)

            def point(j, n, inner, lo, hi):
                if j < 0:
                    return jnp.where(base == 0, lo(j + 3), inner(jnp.maximum(base + j, 0)))
                if j >= 16:
                    return jnp.where(base == 0, inner(jnp.minimum(base + j, n - 1)), hi(j - 16))
                return inner(base + j)

            def column(lead, y):
                return pl.ds((lead * nx + c0) * ny + y, TILE, stride=ny)

            def yv(j):
                return point(j, ny, lambda y: s2[column(k, y), :], lambda i: wide(ylo, k, i), lambda i: wide(yhi, k, i))

            def yu(j):
                return 0.5 * point(j, ny, lambda y: v2[column(1, y), :], lambda i: wide(uylo, i), lambda i: wide(uyhi, i))

            def yemit(j, value):
                dy2[column(k, base + j), :] = value

            def xv(j):
                return point(j, nx, lambda x: s_ref[k, x, cs, :], lambda i: wide(xlo, k, i), lambda i: wide(xhi, k, i))

            def xu(j):
                return 0.5 * point(j, nx, lambda x: v_ref[0, x, cs, :], lambda i: wide(uxlo, i), lambda i: wide(uxhi, i))

            def xemit(j, value):
                dx[k, base + j, cs, :] = value

            closure = closure_part(step, (EARLY, nx), CROSS_SIZE, stb_ref, vtb_ref, weights, tot, hidden, keys, accs)
            together(
                closure,
                (nx - EARLY) // CROSS_SIZE * 4 + 1,
                (Sweep(16, yv, yu, yemit), Sweep(16, xv, xu, xemit)),
            )

    with_sums(CROSS_SIZE, main)

    def finish(x, rate_t):
        back = rate_t.T
        for k in range(NV):
            rate = back[k * ny : (k + 1) * ny] - (dx[k, x] + dy[k, x])
            stepped = s_ref[k, x] + STEP * rate
            if last:
                stepped = 0.75 * old_ref[k, x] + 0.25 * stepped
            out_ref[k, x] = stepped

    for copy in coming:
        copy.wait()
    going = []
    for part in range(4):
        lo, hi = part * nx // 4, (part + 1) * nx // 4

        @pl.loop(lo, hi, unroll=4)
        def _(x):
            rate_t = rt_ref[x]
            if lo >= EARLY:
                rate_t = rate_t + jnp.where(band_ref[x // BS] > 0, tot[x], 0.0)
            finish(x, rate_t)

        for k in range(NV):
            span = pl.ds(lo, hi - lo)
            going.append(pltpu.make_async_copy(out_ref.at[k, span], out_hbm.at[k, span], sems.at[2 + part * NV + k]))
            going[-1].start()

    if not last:
        cut_slabs(out_ref, [(k, k) for k in range(NV)], *slabs)
    for copy in going:
        copy.wait()


def cut_slabs(ref, which, to_lo_x, to_hi_x, to_lo_y, to_hi_y):
    lead, nx, ny = ref.shape[:3]
    flat = ref.reshape(lead * nx * ny, 128)
    for src, dst in which:
        for j in range(3):
            to_lo_x[dst, j] = ref[src, j].astype(jnp.bfloat16)
            to_hi_x[dst, j] = ref[src, nx - 3 + j].astype(jnp.bfloat16)
            for target, y in ((to_lo_y, j), (to_hi_y, ny - 3 + j)):
                target[dst, j] = flat[pl.ds(src * nx * ny + y, nx, stride=ny), :].astype(jnp.bfloat16)


def slab_kernel(s_ref, v_ref, *slabs):
    cut_slabs(s_ref, [(k, k) for k in range(NV)], *slabs)
    nx, ny = v_ref.shape[1], v_ref.shape[2]
    flat = v_ref.reshape(3 * nx * ny, 128)
    for j in range(3):
        slabs[0][NV, j] = v_ref[0, j].astype(jnp.bfloat16)
        slabs[1][NV, j] = v_ref[0, nx - 3 + j].astype(jnp.bfloat16)
        slabs[2][NV, j] = flat[pl.ds(nx * ny + j, nx, stride=ny), :].astype(jnp.bfloat16)
        slabs[3][NV, j] = flat[pl.ds(nx * ny + ny - 3 + j, nx, stride=ny), :].astype(jnp.bfloat16)


VM = pl.BlockSpec(memory_space=pltpu.VMEM)
ANY = pl.BlockSpec(memory_space=pl.ANY)
PARAMS = pltpu.CompilerParams(vmem_limit_bytes=VMEM_LIMIT)


def set_keys(keys):
    row = lax.broadcasted_iota(jnp.int32, (2 * HID, 2 * HID), 0)
    lane = lax.broadcasted_iota(jnp.int32, (2 * HID, 2 * HID), 1)
    keys[0] = row % 32 - lane // HID
    keys[1] = lane % 32 - row // HID


def with_sums(size, body):
    pl.run_scoped(body, *[pltpu.ACC(m)((size * 64, 2 * HID), jnp.float32) for m in (0, 0, 1, 1)])


def closure_scratch(planes, size):
    return [
        pltpu.VMEM((planes // size, size * 128, 2 * HID), jnp.bfloat16),
        pltpu.VMEM((2, 2 * HID, 2 * HID), jnp.int32),
    ]


def slab_shapes(count, n):
    return [jax.ShapeDtypeStruct((count, 3, n, 128), jnp.bfloat16)] * 4


def slab_call(state, velocity):
    n = state.shape[1]
    return pl.pallas_call(
        slab_kernel,
        out_shape=slab_shapes(NV + 1, n),
        in_specs=[VM] * 2,
        out_specs=[VM] * 4,
        compiler_params=PARAMS,
        name="slabs",
    )(state, velocity)


def depth_call(opening, state, extra, band, weights):
    n = state.shape[1]
    plane = lambda dtype: jax.ShapeDtypeStruct((n, 128, 128), dtype)
    shapes = [plane(jnp.float32), plane(jnp.bfloat16)]
    if opening:
        shapes += [plane(jnp.bfloat16), plane(jnp.float32)]
    args = (state, *extra, band, *weights)
    return pl.pallas_call(
        functools.partial(depth_kernel, opening),
        out_shape=shapes,
        in_specs=[VM] * len(args),
        out_specs=[VM] * len(shapes),
        scratch_shapes=[pltpu.VMEM((n, 128, 128), jnp.float32), pltpu.VMEM((EARLY, 128, 128), jnp.float32)] + closure_scratch(EARLY, DEPTH_SIZE),
        compiler_params=PARAMS,
        cost_estimate=pl.CostEstimate(flops=1 << 34, bytes_accessed=8 << 20, transcendentals=0),
        name="depth",
    )(*args)


def cross_call(state, velocity, parts, band, weights, halos, old):
    n = state.shape[1]
    last = old is not None
    args = (state, velocity, *parts, band, *weights, *halos) + ((old,) if last else ())
    shapes = [jax.ShapeDtypeStruct(state.shape, jnp.float32)]
    if not last:
        shapes += slab_shapes(NV, n)
    return pl.pallas_call(
        functools.partial(cross_kernel, last),
        out_shape=shapes,
        in_specs=[VM] * 2 + [ANY] + [VM] * (len(args) - 4) + [ANY if last else VM],
        out_specs=[ANY] + [VM] * (len(shapes) - 1),
        scratch_shapes=[pltpu.VMEM(state.shape, jnp.float32)] * 2
        + [pltpu.VMEM((n, 128, 128), jnp.float32)]
        + closure_scratch(n - EARLY, CROSS_SIZE)
        + [pltpu.VMEM((n, 128, 128), jnp.float32), pltpu.VMEM(state.shape, jnp.float32)]
        + [pltpu.SemaphoreType.DMA((2 + 4 * NV,))]
        + ([pltpu.VMEM(state.shape, jnp.float32)] if last else []),
        compiler_params=PARAMS,
        cost_estimate=pl.CostEstimate(flops=1 << 35, bytes_accessed=12 << 20, transcendentals=0),
        name="cross",
    )(*args)


def send(value, axis, up):
    n = lax.axis_size(axis)
    if up:
        return lax.ppermute(value, axis, [(i, (i + 1) % n) for i in range(n)])
    return lax.ppermute(value, axis, [((i + 1) % n, i) for i in range(n)])


def exchange(to_lo_x, to_hi_x, to_lo_y, to_hi_y):
    return [
        send(to_hi_x, "gx", True),
        send(to_lo_x, "gx", False),
        send(to_hi_y, "gy", True),
        send(to_lo_y, "gy", False),
    ]


def prepare(w_in, w_mid, w_deep, w_out, ny):
    half = jnp.asarray(0.5, jnp.bfloat16)
    two = jnp.eye(2, dtype=jnp.bfloat16)
    padded = jnp.pad((w_in.T * half).astype(jnp.float32), ((0, 1), (0, 0)))
    wsel = jnp.tile(jnp.repeat(padded, ny, axis=0), (1, 2))
    wmid = jnp.kron(two, w_mid.T * half)
    wdeep = jnp.kron(two, w_deep.T * half)
    wout = jnp.tile(jnp.repeat(w_out.T.astype(jnp.float32), ny, axis=1), (2, 1))
    return wsel, wmid, wdeep, wout


def shards(state, velocity, routes, w_in, w_mid, w_deep, w_out):
    ny = state.shape[2]
    cut = slab_call(state, velocity)
    halos = exchange(*cut)
    opening = halos
    weights = prepare(w_in, w_mid, w_deep, w_out, ny)
    member = (routes >= 0).astype(jnp.float32)
    band = jnp.repeat(member.transpose(0, 2, 1), BS, axis=1)
    band = jnp.tile(jnp.repeat(band, BS, axis=2), (1, 1, NV))

    rt, stb, vtb, ut = depth_call(True, state, (velocity,), band, weights)
    first, *cut = cross_call(state, velocity, (rt, stb, vtb), band, weights, halos, None)
    halos = exchange(*cut)
    rt, stb = depth_call(False, first, (vtb, ut), band, weights)
    return cross_call(first, velocity, (rt, stb, vtb), band, weights, halos + opening, state)[0]


def solution(mesh):
    placed = (
        P(None, "gx", "gy", None),
        P(None, "gx", "gy", None),
        P("gx", "gy", None),
        P(),
        P(),
        P(),
        P(),
    )
    return jax.shard_map(
        shards, mesh=mesh, in_specs=placed, out_specs=P(None, "gx", "gy", None), check_vma=False
    )
```

time: 199 us -> 178 us (0.89)
  Pallas kernels: 169 us -> 152 us
  other arithmetic: 3.9 us -> 0.3 us
    pallas_call x2, Pallas kernels: 110 us -> 96.4 us  [cross_call(): pl.pallas_call(functools.partial(cross_kernel, last), out_shape=shapes, i...]
    select_n x2 -> x0, other arithmetic: 3.59 us -> none  [the longest x1 1.93 us: prepare(): jnp.where(hit, wide[None, :, None, :], zero).reshape(PAIRS, 8 * ny, 2 * HID)]
    pallas_call x2, Pallas kernels: 56.2 us -> 52.8 us  [depth_call(): pl.pallas_call(functools.partial(depth_kernel, opening), out_shape=shapes...]
    squeeze x4 -> x0, local copies, waits for them, and re-layouts: 2.64 us -> none  [shards(): speeds = [h[NV] for h in halos]]
  transfers between devices with their start and end apart: 8 -> 8, of which waited for: 0 -> 0; matrix products, arithmetic and copies ran while one was open for 4% -> 2% of each run, Pallas kernels for 28% -> 30%
where the time goes in v3:
time: 178 us
  Pallas kernels  152 us (85%)
  starting transfers between devices  20.1 us (11%)
  local copies, waits for them, and re-layouts  4.95 us (3%)
    pallas_call x2, Pallas kernels, cross_call(): pl.pallas_call(functools.partial(cross_kernel, last), out_shape=shapes, i...  96.4 us
    pallas_call x2, Pallas kernels, depth_call(): pl.pallas_call(functools.partial(depth_kernel, opening), out_shape=shapes...  52.8 us
    ppermute x4, starting transfers between devices, send(): return lax.ppermute(value, axis, [((i + 1) % n, i) for i in range(n)])  18 us
  transfers between devices with their start and end apart: 8, of which 0 were waited for; matrix products, arithmetic and copies ran while one was open for 2% of the time, Pallas kernels for 30%

profile of v3, /device:TPU:0, one launch (start us, length us, event | category | flops | bytes accessed | tf_op | source)
XLA Modules:
  0.0 178.0 jit_solution(6086567109863726538)
XLA Ops:
  0.0 0.0 copy-start.2
  0.0 0.0 copy-start.3
  0.0 0.0 copy-start.4
  0.0 0.0 copy-start
  0.0 0.0 copy-start.1
  0.0 3.1 %slabs.1 = (bf16[5,3,32,128]{3,2,1,0:T(8,128)(2,1)}, bf16[5,3,32,128]{3,2,1,0:T(8,128)(2,1)}, bf16[5,3,32,128]{3,2,1,0:T(8,128)(2,1)}, bf16[5,3,32,128]{3,2,1,0:T(8,128)(2,1)}) custom-call(f32[4,32,32,128]{3,2,1,0:T(8,128)} %refs_18_.1, f32[3,32,32,128]{3,2,1,0:T(8,128)} %refs_1_.5), custom_call_target="tpu_custom_call" | custom-call | tf_op jit(solution)/shard_map/slabs/pallas_call | solution.py:369
  3.1 2.0 %collective-permute-start = (bf16[5,3,32,128]{3,2,1,0:T(8,128)(2,1)}, bf16[5,3,32,128]{3,2,1,0:T(8,128)(2,1)S(1)}, u32[]{:S(2)}, u32[]{:S(2)}) collective-permute-start(bf16[5,3,32,128]{3,2,1,0:T(8,128)(2,1)} %get-tuple-element.23), channel_id=1, source_target_pairs={{0,16},{16,32},{32,48},{48,64},{64,80},{80,96},{96,112},{112,0},{1... | collective-permute-start | bytes 368648 | tf_op jit(solution)/shard_map/ppermute | solution.py:425
  5.1 3.1 %collective-permute-start.1 = (bf16[5,3,32,128]{3,2,1,0:T(8,128)(2,1)}, bf16[5,3,32,128]{3,2,1,0:T(8,128)(2,1)S(1)}, u32[]{:S(2)}, u32[]{:S(2)}) collective-permute-start(bf16[5,3,32,128]{3,2,1,0:T(8,128)(2,1)} %get-tuple-element.24), channel_id=1, source_target_pairs={{16,0},{32,16},{48,32},{64,48},{80,64},{96,80},{112,96},{0,112},{1... | collective-permute-start | bytes 368648 | tf_op jit(solution)/shard_map/ppermute | solution.py:426
  8.3 0.0 collective-permute-start.2
  8.3 5.4 %collective-permute-start.3 = (bf16[5,3,32,128]{3,2,1,0:T(8,128)(2,1)}, bf16[5,3,32,128]{3,2,1,0:T(8,128)(2,1)S(1)}, u32[]{:S(2)}, u32[]{:S(2)}) collective-permute-start(bf16[5,3,32,128]{3,2,1,0:T(8,128)(2,1)} %get-tuple-element.26), channel_id=1, source_target_pairs={{1,0},{2,1},{3,2},{4,3},{5,4},{6,5},{7,6},{8,7},{9,8},{10,9},{11,1... | collective-permute-start | bytes 368648 | tf_op jit(solution)/shard_map/ppermute | solution.py:426
  13.6 0.0 copy-done.2
  13.6 0.0 copy-done.3
  13.7 0.0 copy-done.4
  13.7 0.1 broadcast_in_dim.18
  13.8 0.1 reshape.34
  13.8 0.0 copy-done
  13.9 0.1 copy.12
  14.0 0.0 copy-done.1
  14.0 0.1 copy.13
  14.1 0.1 copy.14
  14.3 0.8 copy.15.refs_2_.refs_5_.refs_3_
  15.0 0.1 tile.34
  15.1 0.7 copy.25
  15.9 0.3 broadcast_multiply_fusion
  16.1 0.8 copy_bitcast_fusion.1
  16.9 0.7 tile.37
  17.6 27.1 %depth.2 = (f32[32,128,128]{2,1,0:T(8,128)}, bf16[32,128,128]{2,1,0:T(8,128)(2,1)}, bf16[32,128,128]{2,1,0:T(8,128)(2,1)}, f32[32,128,128]{2,1,0:T(8,128)}) custom-call(f32[4,32,32,128]{3,2,1,0:T(8,128)} %refs_18_.1, f32[3,32,32,128]{3,2,1,0:T(8,128)} %refs_1_.5, f32[2,128,128]{2,1,0:T(8,128)} %copy.15.refs_2_.refs_5_.refs_3_, f32[256,256]{1,0:T(8,128)} %bitcast.36, ...), custom_call_target="tpu_custom_call" | custom-call | flops 17179869184 | bytes 8388608 | tf_op jit(solution)/shard_map/depth/pallas_call | solution.py:386
  44.7 0.0 collective-permute-done.refs_10_.refs_14_
  44.7 0.0 copy-start.5
  44.7 0.0 collective-permute-done.1.refs_11_.refs_15_
  44.7 0.0 copy-start.6
  44.7 0.0 collective-permute-done.2.refs_12_.refs_16_
  44.7 0.0 copy-start.7
  44.7 0.0 collective-permute-done.3.refs_13_.refs_17_
  44.7 0.0 copy-start.8
  44.7 0.6 copy-done.5
  45.3 0.0 copy-done.6
  45.4 0.0 copy-done.7
  45.4 0.1 copy-done.8
  45.5 48.5 %cross.2 = (f32[4,32,32,128]{3,2,1,0:T(8,128)}, bf16[4,3,32,128]{3,2,1,0:T(8,128)(2,1)}, bf16[4,3,32,128]{3,2,1,0:T(8,128)(2,1)}, bf16[4,3,32,128]{3,2,1,0:T(8,128)(2,1)}, bf16[4,3,32,128]{3,2,1,0:T(8,128)(2,1)}) custom-call(f32[4,32,32,128]{3,2,1,0:T(8,128)} %refs_18_.1, f32[3,32,32,128]{3,2,1,0:T(8,128)} %refs_1_.5, ...), custom_call_target="tpu_custom_call" | custom-call | flops 34359738368 | bytes 12582912 | tf_op jit(solution)/shard_map/cross/pallas_call | solution.py:405
  94.0 0.1 collective-permute-start.4
  94.0 4.1 %collective-permute-start.5 = (bf16[4,3,32,128]{3,2,1,0:T(8,128)(2,1)}, bf16[4,3,32,128]{3,2,1,0:T(8,128)(2,1)S(1)}, u32[]{:S(2)}, u32[]{:S(2)}) collective-permute-start(bf16[4,3,32,128]{3,2,1,0:T(8,128)(2,1)} %get-tuple-element.32), channel_id=1, source_target_pairs={{16,0},{32,16},{48,32},{64,48},{80,64},{96,80},{112,96},{0,112},{1... | collective-permute-start | bytes 294920 | tf_op jit(solution)/shard_map/ppermute | solution.py:426
  98.2 0.0 collective-permute-start.6
  98.2 5.4 %collective-permute-start.7 = (bf16[4,3,32,128]{3,2,1,0:T(8,128)(2,1)}, bf16[4,3,32,128]{3,2,1,0:T(8,128)(2,1)S(1)}, u32[]{:S(2)}, u32[]{:S(2)}) collective-permute-start(bf16[4,3,32,128]{3,2,1,0:T(8,128)(2,1)} %get-tuple-element.34), channel_id=1, source_target_pairs={{1,0},{2,1},{3,2},{4,3},{5,4},{6,5},{7,6},{8,7},{9,8},{10,9},{11,1... | collective-permute-start | bytes 294920 | tf_op jit(solution)/shard_map/ppermute | solution.py:426
  103.5 25.7 %depth.3 = (f32[32,128,128]{2,1,0:T(8,128)}, bf16[32,128,128]{2,1,0:T(8,128)(2,1)}) custom-call(f32[4,32,32,128]{3,2,1,0:T(8,128)} %get-tuple-element.27.refs_0_, bf16[32,128,128]{2,1,0:T(8,128)(2,1)} %get-tuple-element.22.refs_4_.refs_1_, f32[32,128,128]{2,1,0:T(8,128)} %get-tuple-element.28.refs_2_, f32[2,128,128]{2,1,0:T(8,128)} %copy.15.refs_2_.refs_5_.refs_3_, ...), custom_call_target="tpu_custom_call" | custom-call | flops 17179869184 | bytes 8388608 | tf_op jit(solution)/shard_map/depth/pallas_call | solution.py:386
  129.2 0.0 collective-permute-done.4.refs_10_
  129.2 0.0 copy-start.9
  129.2 0.0 collective-permute-done.5.refs_11_
  129.3 0.0 copy-start.10
  129.3 0.0 collective-permute-done.6.refs_12_
  129.3 0.0 copy-start.11
  129.3 0.0 collective-permute-done.7.refs_13_
  129.3 0.0 copy-start.12
  129.3 0.6 copy-done.9
  129.9 0.0 copy-done.10
  129.9 0.0 copy-done.11
  130.0 0.0 copy-done.12
  130.0 47.9 %cross.3 = f32[4,32,32,128]{3,2,1,0:T(8,128)} custom-call(f32[4,32,32,128]{3,2,1,0:T(8,128)} %get-tuple-element.27.refs_0_, f32[3,32,32,128]{3,2,1,0:T(8,128)} %refs_1_.5, f32[32,128,128]{2,1,0:T(8,128)} %get-tuple-element.29.refs_2_, bf16[32,128,128]{2,1,0:T(8,128)(2,1)} %get-tuple-element.30.refs_3_, ...), custom_call_target="tpu_custom_call" | custom-call | flops 34359738368 | bytes 12582912 | tf_op jit(solution)/shard_map/cross/pallas_call | solution.py:405
  (11 shorter events, 0.1 us)
Async XLA Ops:
  0.0 13.6 %copy-start.2 = (s32[2,2,8]{2,1,0:T(2,128)S(1)}, s32[2,2,8]{2,1,0:T(2,128)}, u32[]{:S(2)}) copy-start(s32[2,2,8]{2,1,0:T(2,128)} %param.9) | copy-start | bytes 388
  0.0 13.6 %copy-start.3 = (bf16[128,7]{0,1:T(8,128)(2,1)S(1)}, bf16[128,7]{0,1:T(8,128)(2,1)}, u32[]{:S(2)}) copy-start(bf16[128,7]{0,1:T(8,128)(2,1)} %param.10) | copy-start | bytes 5380
  0.0 13.7 %copy-start.4 = (bf16[4,128]{1,0:T(4,128)(2,1)S(1)}, bf16[4,128]{1,0:T(4,128)(2,1)}, u32[]{:S(2)}) copy-start(bf16[4,128]{1,0:T(4,128)(2,1)} %param.13) | copy-start | bytes 3076
  0.0 13.8 %copy-start = (bf16[128,128]{1,0:T(8,128)(2,1)S(1)}, bf16[128,128]{1,0:T(8,128)(2,1)}, u32[]{:S(2)}) copy-start(bf16[128,128]{1,0:T(8,128)(2,1)} %param.11) | copy-start | bytes 98308
  0.0 14.0 %copy-start.1 = (bf16[128,128]{1,0:T(8,128)(2,1)S(1)}, bf16[128,128]{1,0:T(8,128)(2,1)}, u32[]{:S(2)}) copy-start(bf16[128,128]{1,0:T(8,128)(2,1)} %param.12) | copy-start | bytes 98308
  3.1 41.5 %collective-permute-start = (bf16[5,3,32,128]{3,2,1,0:T(8,128)(2,1)}, bf16[5,3,32,128]{3,2,1,0:T(8,128)(2,1)S(1)}, u32[]{:S(2)}, u32[]{:S(2)}) collective-permute-start(bf16[5,3,32,128]{3,2,1,0:T(8,128)(2,1)} %get-tuple-element.23), channel_id=1, source_target_pairs={{0,16},{16,32},{32,48},{48,64},{64,80},{80,96},{96,112},{112,0},{1... | collective-permute-start | bytes 368648 | tf_op jit(solution)/shard_map/ppermute | solution.py:425
  5.1 39.5 %collective-permute-start.1 = (bf16[5,3,32,128]{3,2,1,0:T(8,128)(2,1)}, bf16[5,3,32,128]{3,2,1,0:T(8,128)(2,1)S(1)}, u32[]{:S(2)}, u32[]{:S(2)}) collective-permute-start(bf16[5,3,32,128]{3,2,1,0:T(8,128)(2,1)} %get-tuple-element.24), channel_id=1, source_target_pairs={{16,0},{32,16},{48,32},{64,48},{80,64},{96,80},{112,96},{0,112},{1... | collective-permute-start | bytes 368648 | tf_op jit(solution)/shard_map/ppermute | solution.py:426
  8.3 36.4 %collective-permute-start.2 = (bf16[5,3,32,128]{3,2,1,0:T(8,128)(2,1)}, bf16[5,3,32,128]{3,2,1,0:T(8,128)(2,1)S(1)}, u32[]{:S(2)}, u32[]{:S(2)}) collective-permute-start(bf16[5,3,32,128]{3,2,1,0:T(8,128)(2,1)} %get-tuple-element.25), channel_id=1, source_target_pairs={{0,1},{1,2},{2,3},{3,4},{4,5},{5,6},{6,7},{7,8},{8,9},{9,10},{10,1... | collective-permute-start | bytes 368648 | tf_op jit(solution)/shard_map/ppermute | solution.py:425
  8.3 36.5 %collective-permute-start.3 = (bf16[5,3,32,128]{3,2,1,0:T(8,128)(2,1)}, bf16[5,3,32,128]{3,2,1,0:T(8,128)(2,1)S(1)}, u32[]{:S(2)}, u32[]{:S(2)}) collective-permute-start(bf16[5,3,32,128]{3,2,1,0:T(8,128)(2,1)} %get-tuple-element.26), channel_id=1, source_target_pairs={{1,0},{2,1},{3,2},{4,3},{5,4},{6,5},{7,6},{8,7},{9,8},{10,9},{11,1... | collective-permute-start | bytes 368648 | tf_op jit(solution)/shard_map/ppermute | solution.py:426
  44.7 0.6 copy-start.5
  44.7 0.7 copy-start.6
  44.7 0.7 copy-start.7
  44.7 0.7 copy-start.8
  94.0 35.3 %collective-permute-start.4 = (bf16[4,3,32,128]{3,2,1,0:T(8,128)(2,1)}, bf16[4,3,32,128]{3,2,1,0:T(8,128)(2,1)S(1)}, u32[]{:S(2)}, u32[]{:S(2)}) collective-permute-start(bf16[4,3,32,128]{3,2,1,0:T(8,128)(2,1)} %get-tuple-element.31), channel_id=1, source_target_pairs={{0,16},{16,32},{32,48},{48,64},{64,80},{80,96},{96,112},{112,0},{1... | collective-permute-start | bytes 294920 | tf_op jit(solution)/shard_map/ppermute | solution.py:425
  94.0 35.2 %collective-permute-start.5 = (bf16[4,3,32,128]{3,2,1,0:T(8,128)(2,1)}, bf16[4,3,32,128]{3,2,1,0:T(8,128)(2,1)S(1)}, u32[]{:S(2)}, u32[]{:S(2)}) collective-permute-start(bf16[4,3,32,128]{3,2,1,0:T(8,128)(2,1)} %get-tuple-element.32), channel_id=1, source_target_pairs={{16,0},{32,16},{48,32},{64,48},{80,64},{96,80},{112,96},{0,112},{1... | collective-permute-start | bytes 294920 | tf_op jit(solution)/shard_map/ppermute | solution.py:426
  98.2 31.1 %collective-permute-start.6 = (bf16[4,3,32,128]{3,2,1,0:T(8,128)(2,1)}, bf16[4,3,32,128]{3,2,1,0:T(8,128)(2,1)S(1)}, u32[]{:S(2)}, u32[]{:S(2)}) collective-permute-start(bf16[4,3,32,128]{3,2,1,0:T(8,128)(2,1)} %get-tuple-element.33), channel_id=1, source_target_pairs={{0,1},{1,2},{2,3},{3,4},{4,5},{5,6},{6,7},{7,8},{8,9},{9,10},{10,1... | collective-permute-start | bytes 294920 | tf_op jit(solution)/shard_map/ppermute | solution.py:425
  98.2 31.1 %collective-permute-start.7 = (bf16[4,3,32,128]{3,2,1,0:T(8,128)(2,1)}, bf16[4,3,32,128]{3,2,1,0:T(8,128)(2,1)S(1)}, u32[]{:S(2)}, u32[]{:S(2)}) collective-permute-start(bf16[4,3,32,128]{3,2,1,0:T(8,128)(2,1)} %get-tuple-element.34), channel_id=1, source_target_pairs={{1,0},{2,1},{3,2},{4,3},{5,4},{6,5},{7,6},{8,7},{9,8},{10,9},{11,1... | collective-permute-start | bytes 294920 | tf_op jit(solution)/shard_map/ppermute | solution.py:426
  129.2 0.6 copy-start.9
  129.3 0.7 copy-start.10
  129.3 0.7 copy-start.11
  129.3 0.7 copy-start.12

commit v4 on v3

--- a/solution.py
+++ b/solution.py
@@ -14,8 +14,10 @@
 NF = 7
 HID = 128
 PAIRS = 16
-DEPTH_SIZE = 4
-CROSS_SIZE = 8
+DEPTH_SIZE = 2
+REGIONS = 4
+LAG = 2
+CROSS_SIZE = 2
 EARLY = 8
 WENO_TYPE = jnp.bfloat16
 SILU_TYPE = jnp.bfloat16
@@ -63,9 +65,11 @@
     def points(self):
         return range(-3, self.last)
 
-    def advance(self, state, j):
+    def advance(self, state, j, token):
         us, fs, vs, fds, vds, frough, vrough, vseconds, before = state
         u, v = self.load_u(j), self.load_v(j)
+        if token is not None:
+            u = u + token
         f = u * v
         if vs:
             fds = fds + [f - fs[-1]]
@@ -90,20 +94,20 @@
     return (h + h * jnp.tanh(h)).astype(jnp.bfloat16)
 
 
-def closure_part(pair, planes, size, st_ref, vt_ref, weights, tot_ref, hidden, keys, accs):
-    wsel_ref, wmid_ref, wdeep_ref, wout_ref = weights
+def closure_part(pair, planes, size, st_ref, vt_ref, weights, tot_ref, hidden, keys, square, accs):
+    wsel_ref, _, _, wout_ref = weights
     chunks = (planes[1] - planes[0]) // size
     half = size * 64
     zero = jnp.zeros((2 * HID, 2 * HID), jnp.float32)
     layers = (
         lambda: jnp.where(keys[0] == 2 * pair, wsel_ref[...], zero).astype(jnp.bfloat16),
-        lambda: wmid_ref[...],
-        lambda: wdeep_ref[...],
+        lambda: square[0],
+        lambda: square[1],
         lambda: jnp.concatenate(
             [jnp.where(keys[1][:, :128] == 2 * pair, wout_ref[...], zero[:, :128]), zero[:, 128:]], axis=1
         ).astype(jnp.bfloat16),
     )
-    waiting = None
+    waiting, token = [], None
 
     def push(layer):
         for m in range(2):
@@ -111,32 +115,33 @@
 
     def take(layer, c, r):
         for m in range(2):
-            sums = pltpu.matmul_pop(accs[2 * m + r])
+            sums = pltpu.matmul_pop(accs[REGIONS * m + r])
             if layer < 3:
                 hidden[c, pl.ds(m * half, half), :] = silu_half(sums)
             else:
                 span = pl.ds(planes[0] + c * size + m * size // 2, size // 2)
                 tot_ref[span] = tot_ref[span] + sums[:, :128].reshape(size // 2, 128, 128)
+        return jnp.where(sums[-TILE:, :128] > 0.0, 0.0, -0.0)
 
     push(0)
     for layer in range(4):
         for c in range(chunks):
-            r = (layer * chunks + c) % 2
+            r = (layer * chunks + c) % REGIONS
             for m in range(2):
                 if layer == 0:
                     span = pl.ds(planes[0] + c * size + m * size // 2, size // 2)
                     lhs = jnp.concatenate([st_ref[span].reshape(half, 128), vt_ref[span].reshape(half, 128)], axis=1)
                 else:
                     lhs = hidden[c, pl.ds(m * half, half), :]
-                pltpu.matmul_acc_lhs(accs[2 * m + r], lhs, layer % 2 if c == 0 else None)
+                pltpu.matmul_acc_lhs(accs[REGIONS * m + r], lhs, layer % 2 if c == 0 else None)
             if c == 0 and layer < 3:
                 push(layer + 1)
-            if waiting is not None:
-                take(*waiting)
-            waiting = (layer, c, r)
-            yield
-    take(*waiting)
-    yield
+            waiting.append((layer, c, r))
+            if len(waiting) > LAG or (layer < 3 and c == chunks - 1 and chunks <= LAG):
+                token = take(*waiting.pop(0))
+            yield token
+    while waiting:
+        yield take(*waiting.pop(0))
 
 
 def together(closure, steps, sweeps):
@@ -145,12 +150,12 @@
     total, spent, at = sum(costs), 0.0, 0
     state, owner = None, None
     for i in range(steps):
-        next(closure, None)
+        token = next(closure, None)
         while at < len(work) and (i == steps - 1 or spent + costs[at] / 2 < total * (i + 1) / steps):
             sweep, j = work[at]
             if sweep is not owner:
                 state, owner = ([],) * 9, sweep
-            state = sweep.advance(state, j)
+            state = sweep.advance(state, j, token)
             spent += costs[at]
             at += 1
 
@@ -158,10 +163,10 @@
 def depth_kernel(opening, *refs):
     if opening:
         s_ref, v_ref, band_ref, *weights = refs[:7]
-        rt_ref, stb_ref, vtb_ref, ut_ref, st, tot, hidden, keys = refs[7:]
+        rt_ref, stb_ref, vtb_ref, ut_ref, st, tot, hidden, keys, square = refs[7:]
     else:
         s_ref, vtb_ref, ut_ref, band_ref, *weights = refs[:8]
-        rt_ref, stb_ref, st, tot, hidden, keys = refs[8:]
+        rt_ref, stb_ref, st, tot, hidden, keys, square = refs[8:]
     nx, ny = s_ref.shape[1], s_ref.shape[2]
 
     @pl.loop(0, nx, unroll=4)
@@ -184,6 +189,7 @@
     rt2 = rt_ref.reshape(nx * 128, 128)
 
     set_keys(keys)
+    set_square(square, weights)
 
     def main(*accs):
         @pl.loop(0, PAIRS)
@@ -198,8 +204,8 @@
                 rt2[at(j), :] = -value
 
             column = Sweep(16, lambda j: st2[at(j), :], lambda j: ut2[at(j), :], emit)
-            closure = closure_part(step, (0, EARLY), DEPTH_SIZE, stb_ref, vtb_ref, weights, tot, hidden, keys, accs)
-            together(closure, EARLY // DEPTH_SIZE * 4 + 1, (column,))
+            closure = closure_part(step, (0, EARLY), DEPTH_SIZE, stb_ref, vtb_ref, weights, tot, hidden, keys, square, accs)
+            together(closure, EARLY // DEPTH_SIZE * 4 + LAG, (column,))
 
     with_sums(DEPTH_SIZE, main)
 
@@ -214,10 +220,10 @@
     rest = refs[14:] if not last else refs[18:]
     uxlo, uxhi, uylo, uyhi = (r.at[NV] for r in (refs[10:14] if not last else refs[14:18]))
     if last:
-        old_hbm, out_hbm, dx, dy, tot, hidden, keys, rt_ref, out_ref, sems, old_ref = rest
+        old_hbm, out_hbm, dx, dy, tot, hidden, keys, square, rt_ref, out_ref, sems, old_ref = rest
     else:
         out_hbm, *slabs = rest[:5]
-        dx, dy, tot, hidden, keys, rt_ref, out_ref, sems = rest[5:]
+        dx, dy, tot, hidden, keys, square, rt_ref, out_ref, sems = rest[5:]
     nx, ny = s_ref.shape[1], s_ref.shape[2]
     s2 = s_ref.reshape(NV * nx * ny, 128)
     v2 = v_ref.reshape(3 * nx * ny, 128)
@@ -233,6 +239,7 @@
         tot[x] = jnp.zeros((128, 128), jnp.float32)
 
     set_keys(keys)
+    set_square(square, weights)
 
     def main(*accs):
         @pl.loop(0, PAIRS)
@@ -273,10 +280,10 @@
             def xemit(j, value):
                 dx[k, base + j, cs, :] = value
 
-            closure = closure_part(step, (EARLY, nx), CROSS_SIZE, stb_ref, vtb_ref, weights, tot, hidden, keys, accs)
+            closure = closure_part(step, (EARLY, nx), CROSS_SIZE, stb_ref, vtb_ref, weights, tot, hidden, keys, square, accs)
             together(
                 closure,
-                (nx - EARLY) // CROSS_SIZE * 4 + 1,
+                (nx - EARLY) // CROSS_SIZE * 4 + LAG,
                 (Sweep(16, yv, yu, yemit), Sweep(16, xv, xu, xemit)),
             )
 
@@ -349,14 +356,24 @@
     keys[1] = lane % 32 - row // HID
 
 
+def set_square(square, weights):
+    for i in range(2):
+        part = (0.5 * weights[1 + i][...].astype(jnp.float32)).T.astype(jnp.bfloat16)
+        none = jnp.zeros_like(part)
+        square[i] = jnp.concatenate(
+            [jnp.concatenate([part, none], axis=1), jnp.concatenate([none, part], axis=1)], axis=0
+        )
+
+
 def with_sums(size, body):
-    pl.run_scoped(body, *[pltpu.ACC(m)((size * 64, 2 * HID), jnp.float32) for m in (0, 0, 1, 1)])
+    pl.run_scoped(body, *[pltpu.ACC(m)((size * 64, 2 * HID), jnp.float32) for m in range(2) for _ in range(REGIONS)])
 
 
 def closure_scratch(planes, size):
     return [
         pltpu.VMEM((planes // size, size * 128, 2 * HID), jnp.bfloat16),
         pltpu.VMEM((2, 2 * HID, 2 * HID), jnp.int32),
+        pltpu.VMEM((2, 2 * HID, 2 * HID), jnp.bfloat16),
     ]
 
 
@@ -437,13 +454,10 @@
 
 def prepare(w_in, w_mid, w_deep, w_out, ny):
     half = jnp.asarray(0.5, jnp.bfloat16)
-    two = jnp.eye(2, dtype=jnp.bfloat16)
     padded = jnp.pad((w_in.T * half).astype(jnp.float32), ((0, 1), (0, 0)))
     wsel = jnp.tile(jnp.repeat(padded, ny, axis=0), (1, 2))
-    wmid = jnp.kron(two, w_mid.T * half)
-    wdeep = jnp.kron(two, w_deep.T * half)
     wout = jnp.tile(jnp.repeat(w_out.T.astype(jnp.float32), ny, axis=1), (2, 1))
-    return wsel, wmid, wdeep, wout
+    return wsel, w_mid, w_deep, wout
 
 
 def shards(state, velocity, routes, w_in, w_mid, w_deep, w_out):

time: 178 us -> 168 us (0.944)
  Pallas kernels: 152 us -> 143 us
    pallas_call x2, Pallas kernels: 52.8 us -> 47.7 us  [depth_call(): pl.pallas_call(functools.partial(depth_kernel, opening), out_shape=shapes...]
    pallas_call x2, Pallas kernels: 96.4 us -> 92.2 us  [cross_call(): pl.pallas_call(functools.partial(cross_kernel, last), out_shape=shapes, i...]
  transfers between devices with their start and end apart: 8 -> 8, of which waited for: 0 -> 0; matrix products, arithmetic and copies ran while one was open for 2% -> 2% of each run, Pallas kernels for 30% -> 29%
where the time goes in v4:
time: 168 us
  Pallas kernels  143 us (85%)
  starting transfers between devices  20.1 us (12%)
  local copies, waits for them, and re-layouts  3.98 us (2%)
    pallas_call x2, Pallas kernels, cross_call(): pl.pallas_call(functools.partial(cross_kernel, last), out_shape=shapes, i...  92.2 us
    pallas_call x2, Pallas kernels, depth_call(): pl.pallas_call(functools.partial(depth_kernel, opening), out_shape=shapes...  47.7 us
    ppermute x4, starting transfers between devices, send(): return lax.ppermute(value, axis, [((i + 1) % n, i) for i in range(n)])  18 us
  transfers between devices with their start and end apart: 8, of which 0 were waited for; matrix products, arithmetic and copies ran while one was open for 2% of the time, Pallas kernels for 29%

profile of v4, /device:TPU:0, one launch (start us, length us, event | category | flops | bytes accessed | tf_op | source)
XLA Modules:
  0.0 167.5 jit_solution(7620243075483904425)
XLA Ops:
  0.0 0.0 copy-start
  0.0 0.0 copy-start.1
  0.0 0.0 copy-start.2
  0.0 3.1 %slabs.1 = (bf16[5,3,32,128]{3,2,1,0:T(8,128)(2,1)}, bf16[5,3,32,128]{3,2,1,0:T(8,128)(2,1)}, bf16[5,3,32,128]{3,2,1,0:T(8,128)(2,1)}, bf16[5,3,32,128]{3,2,1,0:T(8,128)(2,1)}) custom-call(f32[4,32,32,128]{3,2,1,0:T(8,128)} %refs_18_.1, f32[3,32,32,128]{3,2,1,0:T(8,128)} %refs_1_.5), custom_call_target="tpu_custom_call" | custom-call | tf_op jit(solution)/shard_map/slabs/pallas_call | solution.py:386
  3.1 2.0 %collective-permute-start = (bf16[5,3,32,128]{3,2,1,0:T(8,128)(2,1)}, bf16[5,3,32,128]{3,2,1,0:T(8,128)(2,1)S(1)}, u32[]{:S(2)}, u32[]{:S(2)}) collective-permute-start(bf16[5,3,32,128]{3,2,1,0:T(8,128)(2,1)} %get-tuple-element.23), channel_id=1, source_target_pairs={{0,16},{16,32},{32,48},{48,64},{64,80},{80,96},{96,112},{112,0},{1... | collective-permute-start | bytes 368648 | tf_op jit(solution)/shard_map/ppermute | solution.py:442
  5.1 3.1 %collective-permute-start.1 = (bf16[5,3,32,128]{3,2,1,0:T(8,128)(2,1)}, bf16[5,3,32,128]{3,2,1,0:T(8,128)(2,1)S(1)}, u32[]{:S(2)}, u32[]{:S(2)}) collective-permute-start(bf16[5,3,32,128]{3,2,1,0:T(8,128)(2,1)} %get-tuple-element.24), channel_id=1, source_target_pairs={{16,0},{32,16},{48,32},{64,48},{80,64},{96,80},{112,96},{0,112},{1... | collective-permute-start | bytes 368648 | tf_op jit(solution)/shard_map/ppermute | solution.py:443
  8.3 0.0 collective-permute-start.2
  8.3 5.4 %collective-permute-start.3 = (bf16[5,3,32,128]{3,2,1,0:T(8,128)(2,1)}, bf16[5,3,32,128]{3,2,1,0:T(8,128)(2,1)S(1)}, u32[]{:S(2)}, u32[]{:S(2)}) collective-permute-start(bf16[5,3,32,128]{3,2,1,0:T(8,128)(2,1)} %get-tuple-element.26), channel_id=1, source_target_pairs={{1,0},{2,1},{3,2},{4,3},{5,4},{6,5},{7,6},{8,7},{9,8},{10,9},{11,1... | collective-permute-start | bytes 368648 | tf_op jit(solution)/shard_map/ppermute | solution.py:443
  13.6 0.0 copy-done
  13.6 0.0 copy-done.1
  13.7 0.0 copy-done.2
  13.7 0.1 broadcast_in_dim.12
  13.7 0.1 reshape.15
  13.8 0.1 copy.10
  14.0 0.8 copy.11.refs_2_.refs_5_.refs_3_
  14.7 0.1 tile.34
  14.8 0.7 copy.17
  15.6 0.7 tile.37
  16.2 24.6 %depth.2 = (f32[32,128,128]{2,1,0:T(8,128)}, bf16[32,128,128]{2,1,0:T(8,128)(2,1)}, bf16[32,128,128]{2,1,0:T(8,128)(2,1)}, f32[32,128,128]{2,1,0:T(8,128)}) custom-call(f32[4,32,32,128]{3,2,1,0:T(8,128)} %refs_18_.1, f32[3,32,32,128]{3,2,1,0:T(8,128)} %refs_1_.5, f32[2,128,128]{2,1,0:T(8,128)} %copy.11.refs_2_.refs_5_.refs_3_, f32[256,256]{1,0:T(8,128)} %bitcast.22, ...), custom_call_target="tpu_custom_call" | custom-call | flops 17179869184 | bytes 8388608 | tf_op jit(solution)/shard_map/depth/pallas_call | solution.py:403
  40.8 0.0 collective-permute-done.refs_10_.refs_14_
  40.8 0.0 copy-start.3
  40.8 0.0 collective-permute-done.1.refs_11_.refs_15_
  40.8 0.0 copy-start.4
  40.8 0.0 collective-permute-done.2.refs_12_.refs_16_
  40.8 0.0 copy-start.5
  40.8 0.0 collective-permute-done.3.refs_13_.refs_17_
  40.9 0.0 copy-start.6
  40.9 0.6 copy-done.3
  41.5 0.1 copy-done.4
  41.5 0.0 copy-done.5
  41.6 0.0 copy-done.6
  41.6 46.4 %cross.2 = (f32[4,32,32,128]{3,2,1,0:T(8,128)}, bf16[4,3,32,128]{3,2,1,0:T(8,128)(2,1)}, bf16[4,3,32,128]{3,2,1,0:T(8,128)(2,1)}, bf16[4,3,32,128]{3,2,1,0:T(8,128)(2,1)}, bf16[4,3,32,128]{3,2,1,0:T(8,128)(2,1)}) custom-call(f32[4,32,32,128]{3,2,1,0:T(8,128)} %refs_18_.1, f32[3,32,32,128]{3,2,1,0:T(8,128)} %refs_1_.5, ...), custom_call_target="tpu_custom_call" | custom-call | flops 34359738368 | bytes 12582912 | tf_op jit(solution)/shard_map/cross/pallas_call | solution.py:422
  88.0 0.1 collective-permute-start.4
  88.1 4.1 %collective-permute-start.5 = (bf16[4,3,32,128]{3,2,1,0:T(8,128)(2,1)}, bf16[4,3,32,128]{3,2,1,0:T(8,128)(2,1)S(1)}, u32[]{:S(2)}, u32[]{:S(2)}) collective-permute-start(bf16[4,3,32,128]{3,2,1,0:T(8,128)(2,1)} %get-tuple-element.32), channel_id=1, source_target_pairs={{16,0},{32,16},{48,32},{64,48},{80,64},{96,80},{112,96},{0,112},{1... | collective-permute-start | bytes 294920 | tf_op jit(solution)/shard_map/ppermute | solution.py:443
  92.3 0.0 collective-permute-start.6
  92.3 5.4 %collective-permute-start.7 = (bf16[4,3,32,128]{3,2,1,0:T(8,128)(2,1)}, bf16[4,3,32,128]{3,2,1,0:T(8,128)(2,1)S(1)}, u32[]{:S(2)}, u32[]{:S(2)}) collective-permute-start(bf16[4,3,32,128]{3,2,1,0:T(8,128)(2,1)} %get-tuple-element.34), channel_id=1, source_target_pairs={{1,0},{2,1},{3,2},{4,3},{5,4},{6,5},{7,6},{8,7},{9,8},{10,9},{11,1... | collective-permute-start | bytes 294920 | tf_op jit(solution)/shard_map/ppermute | solution.py:443
  97.6 23.2 %depth.3 = (f32[32,128,128]{2,1,0:T(8,128)}, bf16[32,128,128]{2,1,0:T(8,128)(2,1)}) custom-call(f32[4,32,32,128]{3,2,1,0:T(8,128)} %get-tuple-element.27.refs_0_, bf16[32,128,128]{2,1,0:T(8,128)(2,1)} %get-tuple-element.22.refs_4_.refs_1_, f32[32,128,128]{2,1,0:T(8,128)} %get-tuple-element.28.refs_2_, f32[2,128,128]{2,1,0:T(8,128)} %copy.11.refs_2_.refs_5_.refs_3_, ...), custom_call_target="tpu_custom_call" | custom-call | flops 17179869184 | bytes 8388608 | tf_op jit(solution)/shard_map/depth/pallas_call | solution.py:403
  120.8 0.0 collective-permute-done.4.refs_10_
  120.8 0.0 copy-start.7
  120.8 0.0 collective-permute-done.5.refs_11_
  120.8 0.0 copy-start.8
  120.8 0.0 collective-permute-done.6.refs_12_
  120.8 0.0 copy-start.9
  120.8 0.0 collective-permute-done.7.refs_13_
  120.9 0.0 copy-start.10
  120.9 0.6 copy-done.7
  121.5 0.0 copy-done.8
  121.5 0.0 copy-done.9
  121.5 0.0 copy-done.10
  121.6 45.8 %cross.3 = f32[4,32,32,128]{3,2,1,0:T(8,128)} custom-call(f32[4,32,32,128]{3,2,1,0:T(8,128)} %get-tuple-element.27.refs_0_, f32[3,32,32,128]{3,2,1,0:T(8,128)} %refs_1_.5, f32[32,128,128]{2,1,0:T(8,128)} %get-tuple-element.29.refs_2_, bf16[32,128,128]{2,1,0:T(8,128)(2,1)} %get-tuple-element.30.refs_3_, ...), custom_call_target="tpu_custom_call" | custom-call | flops 34359738368 | bytes 12582912 | tf_op jit(solution)/shard_map/cross/pallas_call | solution.py:422
  (8 shorter events, 0.0 us)
Async XLA Ops:
  0.0 13.6 %copy-start = (s32[2,2,8]{2,1,0:T(2,128)S(1)}, s32[2,2,8]{2,1,0:T(2,128)}, u32[]{:S(2)}) copy-start(s32[2,2,8]{2,1,0:T(2,128)} %param.9) | copy-start | bytes 388
  0.0 13.6 %copy-start.1 = (bf16[128,7]{0,1:T(8,128)(2,1)S(1)}, bf16[128,7]{0,1:T(8,128)(2,1)}, u32[]{:S(2)}) copy-start(bf16[128,7]{0,1:T(8,128)(2,1)} %param.10) | copy-start | bytes 5380
  0.0 13.6 %copy-start.2 = (bf16[4,128]{1,0:T(4,128)(2,1)S(1)}, bf16[4,128]{1,0:T(4,128)(2,1)}, u32[]{:S(2)}) copy-start(bf16[4,128]{1,0:T(4,128)(2,1)} %param.13) | copy-start | bytes 3076
  3.1 37.7 %collective-permute-start = (bf16[5,3,32,128]{3,2,1,0:T(8,128)(2,1)}, bf16[5,3,32,128]{3,2,1,0:T(8,128)(2,1)S(1)}, u32[]{:S(2)}, u32[]{:S(2)}) collective-permute-start(bf16[5,3,32,128]{3,2,1,0:T(8,128)(2,1)} %get-tuple-element.23), channel_id=1, source_target_pairs={{0,16},{16,32},{32,48},{48,64},{64,80},{80,96},{96,112},{112,0},{1... | collective-permute-start | bytes 368648 | tf_op jit(solution)/shard_map/ppermute | solution.py:442
  5.1 35.7 %collective-permute-start.1 = (bf16[5,3,32,128]{3,2,1,0:T(8,128)(2,1)}, bf16[5,3,32,128]{3,2,1,0:T(8,128)(2,1)S(1)}, u32[]{:S(2)}, u32[]{:S(2)}) collective-permute-start(bf16[5,3,32,128]{3,2,1,0:T(8,128)(2,1)} %get-tuple-element.24), channel_id=1, source_target_pairs={{16,0},{32,16},{48,32},{64,48},{80,64},{96,80},{112,96},{0,112},{1... | collective-permute-start | bytes 368648 | tf_op jit(solution)/shard_map/ppermute | solution.py:443
  8.3 32.6 %collective-permute-start.2 = (bf16[5,3,32,128]{3,2,1,0:T(8,128)(2,1)}, bf16[5,3,32,128]{3,2,1,0:T(8,128)(2,1)S(1)}, u32[]{:S(2)}, u32[]{:S(2)}) collective-permute-start(bf16[5,3,32,128]{3,2,1,0:T(8,128)(2,1)} %get-tuple-element.25), channel_id=1, source_target_pairs={{0,1},{1,2},{2,3},{3,4},{4,5},{5,6},{6,7},{7,8},{8,9},{9,10},{10,1... | collective-permute-start | bytes 368648 | tf_op jit(solution)/shard_map/ppermute | solution.py:442
  8.3 32.6 %collective-permute-start.3 = (bf16[5,3,32,128]{3,2,1,0:T(8,128)(2,1)}, bf16[5,3,32,128]{3,2,1,0:T(8,128)(2,1)S(1)}, u32[]{:S(2)}, u32[]{:S(2)}) collective-permute-start(bf16[5,3,32,128]{3,2,1,0:T(8,128)(2,1)} %get-tuple-element.26), channel_id=1, source_target_pairs={{1,0},{2,1},{3,2},{4,3},{5,4},{6,5},{7,6},{8,7},{9,8},{10,9},{11,1... | collective-permute-start | bytes 368648 | tf_op jit(solution)/shard_map/ppermute | solution.py:443
  40.8 0.7 copy-start.3
  40.8 0.7 copy-start.4
  40.8 0.7 copy-start.5
  40.9 0.7 copy-start.6
  88.0 32.8 %collective-permute-start.4 = (bf16[4,3,32,128]{3,2,1,0:T(8,128)(2,1)}, bf16[4,3,32,128]{3,2,1,0:T(8,128)(2,1)S(1)}, u32[]{:S(2)}, u32[]{:S(2)}) collective-permute-start(bf16[4,3,32,128]{3,2,1,0:T(8,128)(2,1)} %get-tuple-element.31), channel_id=1, source_target_pairs={{0,16},{16,32},{32,48},{48,64},{64,80},{80,96},{96,112},{112,0},{1... | collective-permute-start | bytes 294920 | tf_op jit(solution)/shard_map/ppermute | solution.py:442
  88.1 32.7 %collective-permute-start.5 = (bf16[4,3,32,128]{3,2,1,0:T(8,128)(2,1)}, bf16[4,3,32,128]{3,2,1,0:T(8,128)(2,1)S(1)}, u32[]{:S(2)}, u32[]{:S(2)}) collective-permute-start(bf16[4,3,32,128]{3,2,1,0:T(8,128)(2,1)} %get-tuple-element.32), channel_id=1, source_target_pairs={{16,0},{32,16},{48,32},{64,48},{80,64},{96,80},{112,96},{0,112},{1... | collective-permute-start | bytes 294920 | tf_op jit(solution)/shard_map/ppermute | solution.py:443
  92.3 28.6 %collective-permute-start.6 = (bf16[4,3,32,128]{3,2,1,0:T(8,128)(2,1)}, bf16[4,3,32,128]{3,2,1,0:T(8,128)(2,1)S(1)}, u32[]{:S(2)}, u32[]{:S(2)}) collective-permute-start(bf16[4,3,32,128]{3,2,1,0:T(8,128)(2,1)} %get-tuple-element.33), channel_id=1, source_target_pairs={{0,1},{1,2},{2,3},{3,4},{4,5},{5,6},{6,7},{7,8},{8,9},{9,10},{10,1... | collective-permute-start | bytes 294920 | tf_op jit(solution)/shard_map/ppermute | solution.py:442
  92.3 28.6 %collective-permute-start.7 = (bf16[4,3,32,128]{3,2,1,0:T(8,128)(2,1)}, bf16[4,3,32,128]{3,2,1,0:T(8,128)(2,1)S(1)}, u32[]{:S(2)}, u32[]{:S(2)}) collective-permute-start(bf16[4,3,32,128]{3,2,1,0:T(8,128)(2,1)} %get-tuple-element.34), channel_id=1, source_target_pairs={{1,0},{2,1},{3,2},{4,3},{5,4},{6,5},{7,6},{8,7},{9,8},{10,9},{11,1... | collective-permute-start | bytes 294920 | tf_op jit(solution)/shard_map/ppermute | solution.py:443
  120.8 0.6 copy-start.7
  120.8 0.7 copy-start.8
  120.8 0.7 copy-start.9
  120.9 0.7 copy-start.10

commit v5 on v4

--- a/solution.py
+++ b/solution.py
@@ -16,6 +16,8 @@
 PAIRS = 16
 DEPTH_SIZE = 2
 REGIONS = 4
+DEPTH_AHEAD = 3
+CROSS_AHEAD = 0
 LAG = 2
 CROSS_SIZE = 2
 EARLY = 8
@@ -144,14 +146,14 @@
         yield take(*waiting.pop(0))
 
 
-def together(closure, steps, sweeps):
+def together(closure, steps, ahead, sweeps):
     work = [(sweep, j) for sweep in sweeps for j in sweep.points()]
     costs = [1.0 if j > 1 else 0.15 for _, j in work]
     total, spent, at = sum(costs), 0.0, 0
     state, owner = None, None
     for i in range(steps):
         token = next(closure, None)
-        while at < len(work) and (i == steps - 1 or spent + costs[at] / 2 < total * (i + 1) / steps):
+        while at < len(work) and (i == steps - 1 or spent + costs[at] / 2 < total * (i + 1 + ahead) / (steps + ahead)):
             sweep, j = work[at]
             if sweep is not owner:
                 state, owner = ([],) * 9, sweep
@@ -163,10 +165,18 @@
 def depth_kernel(opening, *refs):
     if opening:
         s_ref, v_ref, band_ref, *weights = refs[:7]
-        rt_ref, stb_ref, vtb_ref, ut_ref, st, tot, hidden, keys, square = refs[7:]
+        rt_ref, stb_hbm, vtb_hbm, ut_hbm, st, tot, hidden, keys, square, stb_ref, vtb_ref, ut_ref, sems = refs[7:]
+        coming = []
+        going = [(vtb_ref, vtb_hbm, sems.at[0]), (ut_ref, ut_hbm, sems.at[1])]
     else:
-        s_ref, vtb_ref, ut_ref, band_ref, *weights = refs[:8]
-        rt_ref, stb_ref, st, tot, hidden, keys, square = refs[8:]
+        s_ref, vtb_hbm, ut_hbm, band_ref, *weights = refs[:8]
+        rt_ref, stb_hbm, st, tot, hidden, keys, square, stb_ref, vtb_ref, ut_ref, sems = refs[8:]
+        coming = [(vtb_hbm, vtb_ref, sems.at[0]), (ut_hbm, ut_ref, sems.at[1])]
+        going = []
+    coming = [pltpu.make_async_copy(*each) for each in coming]
+    going = [pltpu.make_async_copy(*each) for each in going + [(stb_ref, stb_hbm, sems.at[2])]]
+    for copy in coming:
+        copy.start()
     nx, ny = s_ref.shape[1], s_ref.shape[2]
 
     @pl.loop(0, nx, unroll=4)
@@ -180,6 +190,9 @@
             vtb_ref[x] = vt.astype(jnp.bfloat16)
             ut_ref[x] = jnp.concatenate([0.5 * w] * NV, axis=0).T
 
+    for copy in going:
+        copy.start()
+
     @pl.loop(0, EARLY, unroll=4)
     def _(x):
         tot[x] = jnp.zeros((128, 128), jnp.float32)
@@ -190,6 +203,8 @@
 
     set_keys(keys)
     set_square(square, weights)
+    for copy in coming:
+        copy.wait()
 
     def main(*accs):
         @pl.loop(0, PAIRS)
@@ -205,13 +220,16 @@
 
             column = Sweep(16, lambda j: st2[at(j), :], lambda j: ut2[at(j), :], emit)
             closure = closure_part(step, (0, EARLY), DEPTH_SIZE, stb_ref, vtb_ref, weights, tot, hidden, keys, square, accs)
-            together(closure, EARLY // DEPTH_SIZE * 4 + LAG, (column,))
+            together(closure, EARLY // DEPTH_SIZE * 4 + LAG, DEPTH_AHEAD, (column,))
 
     with_sums(DEPTH_SIZE, main)
 
     @pl.loop(0, EARLY, unroll=4)
     def _(x):
         rt_ref[x] = rt_ref[x] + jnp.where(band_ref[x // BS] > 0, tot[x], 0.0)
+
+    for copy in going:
+        copy.wait()
 
 
 def cross_kernel(last, *refs):
@@ -284,6 +302,7 @@
             together(
                 closure,
                 (nx - EARLY) // CROSS_SIZE * 4 + LAG,
+                CROSS_AHEAD,
                 (Sweep(16, yv, yu, yemit), Sweep(16, xv, xu, xemit)),
             )
 
@@ -403,9 +422,11 @@
     return pl.pallas_call(
         functools.partial(depth_kernel, opening),
         out_shape=shapes,
-        in_specs=[VM] * len(args),
-        out_specs=[VM] * len(shapes),
-        scratch_shapes=[pltpu.VMEM((n, 128, 128), jnp.float32), pltpu.VMEM((EARLY, 128, 128), jnp.float32)] + closure_scratch(EARLY, DEPTH_SIZE),
+        in_specs=[VM, VM if opening else ANY] + [VM if opening else ANY] * (not opening) + [VM] * (len(args) - 2 - (not opening)),
+        out_specs=[VM] + [ANY] * (len(shapes) - 1),
+        scratch_shapes=[pltpu.VMEM((n, 128, 128), jnp.float32), pltpu.VMEM((EARLY, 128, 128), jnp.float32)] + closure_scratch(EARLY, DEPTH_SIZE)
+        + [pltpu.VMEM((n, 128, 128), t) for t in (jnp.bfloat16, jnp.bfloat16, jnp.float32)]
+        + [pltpu.SemaphoreType.DMA((3,))],
         compiler_params=PARAMS,
         cost_estimate=pl.CostEstimate(flops=1 << 34, bytes_accessed=8 << 20, transcendentals=0),
         name="depth",

time: 168 us -> 165 us (0.982)
  Pallas kernels: 143 us -> 140 us
    pallas_call x2, Pallas kernels: 47.7 us -> 44.7 us  [depth_call(): pl.pallas_call(functools.partial(depth_kernel, opening), out_shape=shapes...]
  transfers between devices with their start and end apart: 8 -> 8, of which waited for: 0 -> 0; matrix products, arithmetic and copies ran while one was open for 2% -> 2% of each run, Pallas kernels for 29% -> 27%
where the time goes in v5:
time: 165 us
  Pallas kernels  140 us (85%)
  starting transfers between devices  20.1 us (12%)
  local copies, waits for them, and re-layouts  3.97 us (2%)
    pallas_call x2, Pallas kernels, cross_call(): pl.pallas_call(functools.partial(cross_kernel, last), out_shape=shapes, i...  92.2 us
    pallas_call x2, Pallas kernels, depth_call(): pl.pallas_call(functools.partial(depth_kernel, opening), out_shape=shapes...  44.7 us
    ppermute x4, starting transfers between devices, send(): return lax.ppermute(value, axis, [((i + 1) % n, i) for i in range(n)])  18 us
  transfers between devices with their start and end apart: 8, of which 0 were waited for; matrix products, arithmetic and copies ran while one was open for 2% of the time, Pallas kernels for 27%

profile of v5, /device:TPU:0, one launch (start us, length us, event | category | flops | bytes accessed | tf_op | source)
XLA Modules:
  0.0 164.5 jit_solution(12859097351495851137)
XLA Ops:
  0.0 0.0 copy-start
  0.0 0.0 copy-start.1
  0.0 0.0 copy-start.2
  0.0 3.1 %slabs.1 = (bf16[5,3,32,128]{3,2,1,0:T(8,128)(2,1)}, bf16[5,3,32,128]{3,2,1,0:T(8,128)(2,1)}, bf16[5,3,32,128]{3,2,1,0:T(8,128)(2,1)}, bf16[5,3,32,128]{3,2,1,0:T(8,128)(2,1)}) custom-call(f32[4,32,32,128]{3,2,1,0:T(8,128)} %refs_18_.1, f32[3,32,32,128]{3,2,1,0:T(8,128)} %refs_1_.5), custom_call_target="tpu_custom_call" | custom-call | tf_op jit(solution)/shard_map/slabs/pallas_call | solution.py:405
  3.1 2.0 %collective-permute-start = (bf16[5,3,32,128]{3,2,1,0:T(8,128)(2,1)}, bf16[5,3,32,128]{3,2,1,0:T(8,128)(2,1)S(1)}, u32[]{:S(2)}, u32[]{:S(2)}) collective-permute-start(bf16[5,3,32,128]{3,2,1,0:T(8,128)(2,1)} %get-tuple-element.23), channel_id=1, source_target_pairs={{0,16},{16,32},{32,48},{48,64},{64,80},{80,96},{96,112},{112,0},{1... | collective-permute-start | bytes 368648 | tf_op jit(solution)/shard_map/ppermute | solution.py:463
  5.1 3.1 %collective-permute-start.1 = (bf16[5,3,32,128]{3,2,1,0:T(8,128)(2,1)}, bf16[5,3,32,128]{3,2,1,0:T(8,128)(2,1)S(1)}, u32[]{:S(2)}, u32[]{:S(2)}) collective-permute-start(bf16[5,3,32,128]{3,2,1,0:T(8,128)(2,1)} %get-tuple-element.24), channel_id=1, source_target_pairs={{16,0},{32,16},{48,32},{64,48},{80,64},{96,80},{112,96},{0,112},{1... | collective-permute-start | bytes 368648 | tf_op jit(solution)/shard_map/ppermute | solution.py:464
  8.3 0.0 collective-permute-start.2
  8.3 5.4 %collective-permute-start.3 = (bf16[5,3,32,128]{3,2,1,0:T(8,128)(2,1)}, bf16[5,3,32,128]{3,2,1,0:T(8,128)(2,1)S(1)}, u32[]{:S(2)}, u32[]{:S(2)}) collective-permute-start(bf16[5,3,32,128]{3,2,1,0:T(8,128)(2,1)} %get-tuple-element.26), channel_id=1, source_target_pairs={{1,0},{2,1},{3,2},{4,3},{5,4},{6,5},{7,6},{8,7},{9,8},{10,9},{11,1... | collective-permute-start | bytes 368648 | tf_op jit(solution)/shard_map/ppermute | solution.py:464
  13.6 0.0 copy-done
  13.6 0.0 copy-done.1
  13.7 0.0 copy-done.2
  13.7 0.1 broadcast_in_dim.12
  13.7 0.1 reshape.15
  13.8 0.1 copy.10
  14.0 0.8 copy.11.refs_2_.refs_5_.refs_3_
  14.7 0.1 tile.34
  14.8 0.7 copy.17
  15.6 0.7 tile.37
  16.2 22.7 %depth.2 = (f32[32,128,128]{2,1,0:T(8,128)}, bf16[32,128,128]{2,1,0:T(8,128)(2,1)}, bf16[32,128,128]{2,1,0:T(8,128)(2,1)}, f32[32,128,128]{2,1,0:T(8,128)}) custom-call(f32[4,32,32,128]{3,2,1,0:T(8,128)} %refs_18_.1, f32[3,32,32,128]{3,2,1,0:T(8,128)} %refs_1_.5, f32[2,128,128]{2,1,0:T(8,128)} %copy.11.refs_2_.refs_5_.refs_3_, f32[256,256]{1,0:T(8,128)} %bitcast.22, ...), custom_call_target="tpu_custom_call" | custom-call | flops 17179869184 | bytes 8388608 | tf_op jit(solution)/shard_map/depth/pallas_call | solution.py:422
  39.0 0.0 collective-permute-done.refs_10_.refs_14_
  39.0 0.0 copy-start.3
  39.0 0.0 collective-permute-done.1.refs_11_.refs_15_
  39.0 0.0 copy-start.4
  39.0 0.0 collective-permute-done.2.refs_12_.refs_16_
  39.0 0.0 copy-start.5
  39.1 0.0 collective-permute-done.3.refs_13_.refs_17_
  39.1 0.0 copy-start.6
  39.1 0.6 copy-done.3
  39.7 0.1 copy-done.4
  39.7 0.0 copy-done.5
  39.8 0.0 copy-done.6
  39.8 46.5 %cross.2 = (f32[4,32,32,128]{3,2,1,0:T(8,128)}, bf16[4,3,32,128]{3,2,1,0:T(8,128)(2,1)}, bf16[4,3,32,128]{3,2,1,0:T(8,128)(2,1)}, bf16[4,3,32,128]{3,2,1,0:T(8,128)(2,1)}, bf16[4,3,32,128]{3,2,1,0:T(8,128)(2,1)}) custom-call(f32[4,32,32,128]{3,2,1,0:T(8,128)} %refs_18_.1, f32[3,32,32,128]{3,2,1,0:T(8,128)} %refs_1_.5, ...), custom_call_target="tpu_custom_call" | custom-call | flops 34359738368 | bytes 12582912 | tf_op jit(solution)/shard_map/cross/pallas_call | solution.py:443
  86.3 0.1 collective-permute-start.4
  86.3 4.1 %collective-permute-start.5 = (bf16[4,3,32,128]{3,2,1,0:T(8,128)(2,1)}, bf16[4,3,32,128]{3,2,1,0:T(8,128)(2,1)S(1)}, u32[]{:S(2)}, u32[]{:S(2)}) collective-permute-start(bf16[4,3,32,128]{3,2,1,0:T(8,128)(2,1)} %get-tuple-element.32), channel_id=1, source_target_pairs={{16,0},{32,16},{48,32},{64,48},{80,64},{96,80},{112,96},{0,112},{1... | collective-permute-start | bytes 294920 | tf_op jit(solution)/shard_map/ppermute | solution.py:464
  90.5 0.0 collective-permute-start.6
  90.5 5.4 %collective-permute-start.7 = (bf16[4,3,32,128]{3,2,1,0:T(8,128)(2,1)}, bf16[4,3,32,128]{3,2,1,0:T(8,128)(2,1)S(1)}, u32[]{:S(2)}, u32[]{:S(2)}) collective-permute-start(bf16[4,3,32,128]{3,2,1,0:T(8,128)(2,1)} %get-tuple-element.34), channel_id=1, source_target_pairs={{1,0},{2,1},{3,2},{4,3},{5,4},{6,5},{7,6},{8,7},{9,8},{10,9},{11,1... | collective-permute-start | bytes 294920 | tf_op jit(solution)/shard_map/ppermute | solution.py:464
  95.8 22.0 %depth.3 = (f32[32,128,128]{2,1,0:T(8,128)}, bf16[32,128,128]{2,1,0:T(8,128)(2,1)}) custom-call(f32[4,32,32,128]{3,2,1,0:T(8,128)} %get-tuple-element.27.refs_0_, bf16[32,128,128]{2,1,0:T(8,128)(2,1)} %get-tuple-element.22.refs_4_.refs_1_, f32[32,128,128]{2,1,0:T(8,128)} %get-tuple-element.28.refs_2_, f32[2,128,128]{2,1,0:T(8,128)} %copy.11.refs_2_.refs_5_.refs_3_, ...), custom_call_target="tpu_custom_call" | custom-call | flops 17179869184 | bytes 8388608 | tf_op jit(solution)/shard_map/depth/pallas_call | solution.py:422
  117.8 0.0 collective-permute-done.4.refs_10_
  117.8 0.0 copy-start.7
  117.8 0.0 collective-permute-done.5.refs_11_
  117.8 0.0 copy-start.8
  117.8 0.0 collective-permute-done.6.refs_12_
  117.8 0.0 copy-start.9
  117.9 0.0 collective-permute-done.7.refs_13_
  117.9 0.0 copy-start.10
  117.9 0.6 copy-done.7
  118.5 0.0 copy-done.8
  118.5 0.0 copy-done.9
  118.5 0.0 copy-done.10
  118.6 45.8 %cross.3 = f32[4,32,32,128]{3,2,1,0:T(8,128)} custom-call(f32[4,32,32,128]{3,2,1,0:T(8,128)} %get-tuple-element.27.refs_0_, f32[3,32,32,128]{3,2,1,0:T(8,128)} %refs_1_.5, f32[32,128,128]{2,1,0:T(8,128)} %get-tuple-element.29.refs_2_, bf16[32,128,128]{2,1,0:T(8,128)(2,1)} %get-tuple-element.30.refs_3_, ...), custom_call_target="tpu_custom_call" | custom-call | flops 34359738368 | bytes 12582912 | tf_op jit(solution)/shard_map/cross/pallas_call | solution.py:443
  (8 shorter events, 0.0 us)
Async XLA Ops:
  0.0 13.6 %copy-start = (s32[2,2,8]{2,1,0:T(2,128)S(1)}, s32[2,2,8]{2,1,0:T(2,128)}, u32[]{:S(2)}) copy-start(s32[2,2,8]{2,1,0:T(2,128)} %param.9) | copy-start | bytes 388
  0.0 13.6 %copy-start.1 = (bf16[128,7]{0,1:T(8,128)(2,1)S(1)}, bf16[128,7]{0,1:T(8,128)(2,1)}, u32[]{:S(2)}) copy-start(bf16[128,7]{0,1:T(8,128)(2,1)} %param.10) | copy-start | bytes 5380
  0.0 13.6 %copy-start.2 = (bf16[4,128]{1,0:T(4,128)(2,1)S(1)}, bf16[4,128]{1,0:T(4,128)(2,1)}, u32[]{:S(2)}) copy-start(bf16[4,128]{1,0:T(4,128)(2,1)} %param.13) | copy-start | bytes 3076
  3.1 35.9 %collective-permute-start = (bf16[5,3,32,128]{3,2,1,0:T(8,128)(2,1)}, bf16[5,3,32,128]{3,2,1,0:T(8,128)(2,1)S(1)}, u32[]{:S(2)}, u32[]{:S(2)}) collective-permute-start(bf16[5,3,32,128]{3,2,1,0:T(8,128)(2,1)} %get-tuple-element.23), channel_id=1, source_target_pairs={{0,16},{16,32},{32,48},{48,64},{64,80},{80,96},{96,112},{112,0},{1... | collective-permute-start | bytes 368648 | tf_op jit(solution)/shard_map/ppermute | solution.py:463
  5.1 33.9 %collective-permute-start.1 = (bf16[5,3,32,128]{3,2,1,0:T(8,128)(2,1)}, bf16[5,3,32,128]{3,2,1,0:T(8,128)(2,1)S(1)}, u32[]{:S(2)}, u32[]{:S(2)}) collective-permute-start(bf16[5,3,32,128]{3,2,1,0:T(8,128)(2,1)} %get-tuple-element.24), channel_id=1, source_target_pairs={{16,0},{32,16},{48,32},{64,48},{80,64},{96,80},{112,96},{0,112},{1... | collective-permute-start | bytes 368648 | tf_op jit(solution)/shard_map/ppermute | solution.py:464
  8.3 30.8 %collective-permute-start.2 = (bf16[5,3,32,128]{3,2,1,0:T(8,128)(2,1)}, bf16[5,3,32,128]{3,2,1,0:T(8,128)(2,1)S(1)}, u32[]{:S(2)}, u32[]{:S(2)}) collective-permute-start(bf16[5,3,32,128]{3,2,1,0:T(8,128)(2,1)} %get-tuple-element.25), channel_id=1, source_target_pairs={{0,1},{1,2},{2,3},{3,4},{4,5},{5,6},{6,7},{7,8},{8,9},{9,10},{10,1... | collective-permute-start | bytes 368648 | tf_op jit(solution)/shard_map/ppermute | solution.py:463
  8.3 30.8 %collective-permute-start.3 = (bf16[5,3,32,128]{3,2,1,0:T(8,128)(2,1)}, bf16[5,3,32,128]{3,2,1,0:T(8,128)(2,1)S(1)}, u32[]{:S(2)}, u32[]{:S(2)}) collective-permute-start(bf16[5,3,32,128]{3,2,1,0:T(8,128)(2,1)} %get-tuple-element.26), channel_id=1, source_target_pairs={{1,0},{2,1},{3,2},{4,3},{5,4},{6,5},{7,6},{8,7},{9,8},{10,9},{11,1... | collective-permute-start | bytes 368648 | tf_op jit(solution)/shard_map/ppermute | solution.py:464
  39.0 0.7 copy-start.3
  39.0 0.7 copy-start.4
  39.0 0.7 copy-start.5
  39.1 0.7 copy-start.6
  86.3 31.5 %collective-permute-start.4 = (bf16[4,3,32,128]{3,2,1,0:T(8,128)(2,1)}, bf16[4,3,32,128]{3,2,1,0:T(8,128)(2,1)S(1)}, u32[]{:S(2)}, u32[]{:S(2)}) collective-permute-start(bf16[4,3,32,128]{3,2,1,0:T(8,128)(2,1)} %get-tuple-element.31), channel_id=1, source_target_pairs={{0,16},{16,32},{32,48},{48,64},{64,80},{80,96},{96,112},{112,0},{1... | collective-permute-start | bytes 294920 | tf_op jit(solution)/shard_map/ppermute | solution.py:463
  86.3 31.5 %collective-permute-start.5 = (bf16[4,3,32,128]{3,2,1,0:T(8,128)(2,1)}, bf16[4,3,32,128]{3,2,1,0:T(8,128)(2,1)S(1)}, u32[]{:S(2)}, u32[]{:S(2)}) collective-permute-start(bf16[4,3,32,128]{3,2,1,0:T(8,128)(2,1)} %get-tuple-element.32), channel_id=1, source_target_pairs={{16,0},{32,16},{48,32},{64,48},{80,64},{96,80},{112,96},{0,112},{1... | collective-permute-start | bytes 294920 | tf_op jit(solution)/shard_map/ppermute | solution.py:464
  90.5 27.4 %collective-permute-start.6 = (bf16[4,3,32,128]{3,2,1,0:T(8,128)(2,1)}, bf16[4,3,32,128]{3,2,1,0:T(8,128)(2,1)S(1)}, u32[]{:S(2)}, u32[]{:S(2)}) collective-permute-start(bf16[4,3,32,128]{3,2,1,0:T(8,128)(2,1)} %get-tuple-element.33), channel_id=1, source_target_pairs={{0,1},{1,2},{2,3},{3,4},{4,5},{5,6},{6,7},{7,8},{8,9},{9,10},{10,1... | collective-permute-start | bytes 294920 | tf_op jit(solution)/shard_map/ppermute | solution.py:463
  90.5 27.4 %collective-permute-start.7 = (bf16[4,3,32,128]{3,2,1,0:T(8,128)(2,1)}, bf16[4,3,32,128]{3,2,1,0:T(8,128)(2,1)S(1)}, u32[]{:S(2)}, u32[]{:S(2)}) collective-permute-start(bf16[4,3,32,128]{3,2,1,0:T(8,128)(2,1)} %get-tuple-element.34), channel_id=1, source_target_pairs={{1,0},{2,1},{3,2},{4,3},{5,4},{6,5},{7,6},{8,7},{9,8},{10,9},{11,1... | collective-permute-start | bytes 294920 | tf_op jit(solution)/shard_map/ppermute | solution.py:464
  117.8 0.6 copy-start.7
  117.8 0.7 copy-start.8
  117.8 0.7 copy-start.9
  117.9 0.7 copy-start.10
